TPU v7x, 32 devices: a whole 2x2x4 slice. The times are simulated.
32 devices in a mesh: fsdp: 8 (over z, x), ctx: 4 (over y, core).
Axes of the slice: x: 2, y: 2, z: 4, core: 2. Of those that a mesh axis runs over, the one named last changes fastest.
Arguments:
- hidden_in: bfloat16 [2, 8, 256, 1024], P(None, 'fsdp', 'ctx'), may hold values from -6 to 6
- segment_ids: int32 [2, 8, 256], P(None, 'fsdp'), may hold values from 0 to 16, as said below
- out_grad: bfloat16 [2, 8, 256, 1024], P(None, 'fsdp', 'ctx'), may hold values from -6 to 6
- norm_gain: bfloat16 [1024], P('fsdp'), may hold values from 0.099609375 to 1.8984375
- w_qkv: bfloat16 [1024, 768], P('fsdp'), may hold values from -0.1875 to 0.1875
- w_o: bfloat16 [512, 1024], P('fsdp'), may hold values from -1 to 1
- w_zx: bfloat16 [1024, 3072], P('fsdp'), may hold values from -0.1875 to 0.1875
- w_bc: bfloat16 [1024, 256], P('fsdp'), may hold values from -0.1875 to 0.1875
- w_dt: bfloat16 [1024, 24], P('fsdp'), may hold values from -0.1875 to 0.1875
- conv_w: bfloat16 [4, 1792], P(None, 'fsdp'), may hold values from -3 to 3
- conv_b: bfloat16 [1792], P('fsdp'), may hold values from -3 to 3
- dt_bias: float32 [24], replicated, may hold values from -6.5 to -4.5
- a_log: float32 [24], replicated, may hold values from -2.5 to 2
- d_skip: float32 [24], replicated, may hold values from 0.5 to 1.5
- w_out: bfloat16 [1536, 1024], P('fsdp'), may hold values from -0.15625 to 0.15625
- second_gain: bfloat16 [1024], P('fsdp'), may hold values from 0.099609375 to 1.8984375
- w_gate_up: bfloat16 [1024, 4096], P('fsdp'), may hold values from -0.1875 to 0.1875
- w_down: bfloat16 [2048, 1024], P('fsdp'), may hold values from -0.1875 to 0.1875
Outputs:
- block_out: bfloat16 [2, 8, 256, 1024], P(None, 'fsdp', 'ctx')
- grad_in: bfloat16 [2, 8, 256, 1024], P(None, 'fsdp', 'ctx')
- grad_gain: float32 [1024], P('fsdp')
- grad_qkv: float32 [1024, 768], P('fsdp')
- grad_o: float32 [512, 1024], P('fsdp')
- grad_zx: float32 [1024, 3072], P('fsdp')
- grad_bc: float32 [1024, 256], P('fsdp')
- grad_dt: float32 [1024, 24], P('fsdp')
- grad_conv_w: float32 [4, 1792], P(None, 'fsdp')
- grad_conv_b: float32 [1792], P('fsdp')
- grad_dt_bias: float32 [24], replicated
- grad_a_log: float32 [24], replicated
- grad_d_skip: float32 [24], replicated
- grad_out: float32 [1536, 1024], P('fsdp')
- grad_second_gain: float32 [1024], P('fsdp')
- grad_gate_up: float32 [1024, 4096], P('fsdp')
- grad_down: float32 [2048, 1024], P('fsdp')
Inputs may be any that keep to these rules, and one draw needn't show every extreme that they name: `segment_ids`: in each pack the ids start at 0 at position 0, never fall, and rise by at most one from a token to the next; each pack holds exactly 17 segments; one segment covers every position from 32 to 223.
All inputs are finite; a program needn't handle non-finite values.
Results may differ from a plain program's by a relative error of at most 0.023.
Values may be sent and summed in bfloat16 or wider, within the bound.
No kernel may reach another device: no remote copies, remote signals or barrier semaphores. Data moves between devices by JAX's collectives and lax.ppermute only.
A program may use at most 192 MiB of HBM per device.

v0:
```python
import math

import jax
import jax.numpy as jnp
from jax import lax
from jax.sharding import PartitionSpec as P

HEADS = 8
KV = 2
HD = 64
MH = 24
MP = 64
NS = 128
CONV = 4
FF = 2048
QW = 512
KW = 128
DI = 1536
XC = 1792


epsilon = 1e-05
rope_base = 100000000000.0
highest = lax.Precision.HIGHEST


def from_behind(block, axis, distance):
    devices = range(lax.axis_size(axis))
    route = [(i - distance, i) for i in devices if i - distance in devices]
    return lax.ppermute(block, axis, route)


def prefix_2(part, axis, combine, identity):
    place = lax.axis_index(axis)
    gathered = jax.tree.map(lambda a: lax.all_gather(a, axis), part)
    state = jax.tree.map(lambda a, e: jnp.zeros_like(a) + jnp.asarray(e, a.dtype), part, identity)

    def one(hop, state):
        return combine(
            state, jax.tree.map(lambda a: lax.dynamic_index_in_dim(a, hop, 0, False), gathered)
        )

    return lax.fori_loop(0, place, one, state)


def entering(value, axis, combine, identity):
    peers, position = (lax.axis_size(axis), lax.axis_index(axis))
    everything = jax.tree.map(
        lambda part, kind: lax.all_gather(part.astype(kind), axis),
        value,
        jax.tree.map(lambda a: jnp.bfloat16 if a.dtype == jnp.float32 else a.dtype, value),
    )
    start = jax.tree.map(
        lambda part, zero: jnp.broadcast_to(jnp.asarray(zero, part.dtype), part.shape),
        value,
        identity,
    )

    def hop(k, before):
        at = peers - 1 - k
        reached = at > position
        new = combine(
            before, jax.tree.map(lambda part, own: part[at].astype(own.dtype), everything, value)
        )
        return jax.tree.map(lambda a, b: jnp.where(reached, a, b), new, before)

    return lax.fori_loop(0, peers, hop, start)


def dot_first(left, right):
    return lax.dot_general(
        left, right, (((0,), (0,)), ((), ())), preferred_element_type=jnp.float32
    )


def dot_last(left, right):
    return lax.dot_general(
        left, right, (((1,), (1,)), ((), ())), preferred_element_type=jnp.float32
    )


def rotary_tables(positions):
    half_width = HD // 2
    exponents = jnp.arange(half_width, dtype=jnp.float32) * (2.0 / HD)
    inverse = jnp.exp(-exponents * math.log(rope_base))
    angles = positions[:, None] * inverse[None, :]
    cosine = jnp.concatenate([jnp.cos(angles), jnp.cos(angles)], axis=1)
    sine_table = jnp.concatenate([jnp.sin(angles), jnp.sin(angles)], axis=1)
    return (cosine, sine_table)


def rotate(values, cosine, sine_table):
    half_width = values.shape[-1] // 2
    turned = jnp.concatenate([-values[..., half_width:], values[..., :half_width]], axis=-1)
    return values * cosine[:, None, :] + turned * sine_table[:, None, :]


def unrotate(grads, cosine, sine_table):
    half_width = grads.shape[-1] // 2
    scaled = grads * sine_table[:, None, :]
    turned_back = jnp.concatenate([scaled[..., half_width:], -scaled[..., :half_width]], axis=-1)
    return grads * cosine[:, None, :] + turned_back


def conv_mix(conv_ext, seg_ext, segments, conv_w, conv_b):
    length = segments.shape[0]
    summed = conv_b[None, :]
    for tap in range(CONV):
        same = (seg_ext[tap : tap + length] == segments)[:, None]
        summed = summed + jnp.where(same, conv_ext[tap : tap + length] * conv_w[tap][None, :], 0.0)
    return jax.nn.silu(summed)


def ssd_local(x_heads, step_size, decay_log, input_map, output_map, segments, prev_seg):
    length = segments.shape[0]
    cumulative = jnp.cumsum(decay_log, axis=0)
    order = jnp.arange(length)
    valid = ((order[:, None] >= order[None, :]) & (segments[:, None] == segments[None, :]))[
        :, :, None
    ]
    spread = cumulative[:, None, :] - cumulative[None, :, :]
    kernel = jnp.where(valid, jnp.exp(jnp.where(valid, spread, 0.0)), 0.0)
    intersection = jnp.dot(
        output_map, input_map.T, precision=highest, preferred_element_type=jnp.float32
    )
    weighted = kernel * intersection[:, :, None]
    driven = x_heads * step_size[:, :, None]
    local_term = jnp.einsum("tsh,shp->thp", weighted, driven, precision=highest)
    carry_in = jnp.where((segments == prev_seg)[:, None], jnp.exp(cumulative), 0.0)
    tail_weight = jnp.where(
        (segments == segments[-1])[:, None], jnp.exp(cumulative[-1][None, :] - cumulative), 0.0
    )
    decay_total = jnp.where(segments[-1] == prev_seg, jnp.exp(cumulative[-1]), 0.0)
    state_local = jnp.einsum(
        "shp,sn->hpn", driven * tail_weight[:, :, None], input_map, precision=highest
    )
    return (local_term, carry_in, decay_total, state_local)


def from_carry(output_map, carry_in, state_in):
    return jnp.einsum("tn,hpn->thp", output_map, state_in, precision=highest) * carry_in[:, :, None]


def mamba_parts(conv_ext, step_raw, conv_w, conv_b, dt_bias, a_log, seg_ext, segments):
    length = segments.shape[0]
    activated = conv_mix(conv_ext, seg_ext, segments, conv_w, conv_b)
    x_heads = activated[:, :DI].reshape(length, MH, MP)
    input_map = activated[:, DI : DI + NS]
    output_map = activated[:, DI + NS :]
    step_size = jax.nn.softplus(step_raw + dt_bias[None, :])
    decay_log = -step_size * jnp.exp(a_log)[None, :]
    return (x_heads, step_size, decay_log, input_map, output_map)


def mamba_whole(
    conv_ext,
    step_raw,
    gate_z,
    conv_w,
    conv_b,
    dt_bias,
    a_log,
    d_skip,
    state_in,
    seg_ext,
    segments,
    prev_seg,
):
    x_heads, step_size, decay_log, input_map, output_map = mamba_parts(
        conv_ext, step_raw, conv_w, conv_b, dt_bias, a_log, seg_ext, segments
    )
    local_term, carry_in, decay_total, state_local = ssd_local(
        x_heads, step_size, decay_log, input_map, output_map, segments, prev_seg
    )
    outputs = (
        local_term + from_carry(output_map, carry_in, state_in) + d_skip[None, :, None] * x_heads
    )
    gated = outputs.reshape(segments.shape[0], DI) * jax.nn.silu(gate_z)
    state_out = decay_total[:, None, None] * state_in + state_local
    return ((gated, state_out), (carry_in, output_map, decay_total))


def chain_combine(earlier, later):
    return (earlier[0] * later[0], later[0][:, None, None] * earlier[1] + later[1])


def masked_scores(queries, all_keys, allowed, scale_attn):
    scores = (
        jnp.einsum("qvgd,kvd->vgqk", queries, all_keys, preferred_element_type=jnp.float32)
        * scale_attn
    )
    return jnp.where(allowed[None, None], scores, -1e30)


def weight_products(saved_list):

    def fetch_rows(index):
        return jnp.concatenate([saved[index] for saved in saved_list], axis=0)

    normed = fetch_rows(0)
    return (
        dot_first(normed, fetch_rows(1)),
        dot_first(fetch_rows(5), fetch_rows(7)),
        dot_first(normed, fetch_rows(2)),
        dot_first(normed, fetch_rows(3)),
        dot_first(normed, fetch_rows(4)),
        dot_first(fetch_rows(6), fetch_rows(7)),
        dot_first(fetch_rows(8), fetch_rows(9)),
        dot_first(fetch_rows(10), fetch_rows(11)),
    )


def assemble(products, smalls):
    return (
        smalls[0],
        products[0],
        products[1],
        products[2],
        products[3],
        products[4],
        smalls[1],
        smalls[2],
        products[5],
        smalls[3],
        products[6],
        products[7],
    )


def reduce_shards(grads):
    return (
        lax.psum_scatter(grads[0], "fsdp", scatter_dimension=0, tiled=True),
        lax.psum_scatter(grads[1], "fsdp", scatter_dimension=0, tiled=True),
        lax.psum_scatter(grads[2], "fsdp", scatter_dimension=0, tiled=True),
        lax.psum_scatter(grads[3], "fsdp", scatter_dimension=0, tiled=True),
        lax.psum_scatter(grads[4], "fsdp", scatter_dimension=0, tiled=True),
        lax.psum_scatter(grads[5], "fsdp", scatter_dimension=0, tiled=True),
        lax.psum_scatter(grads[6], "fsdp", scatter_dimension=1, tiled=True),
        lax.psum_scatter(grads[7], "fsdp", scatter_dimension=0, tiled=True),
        lax.psum_scatter(grads[8], "fsdp", scatter_dimension=0, tiled=True),
        lax.psum_scatter(grads[9], "fsdp", scatter_dimension=0, tiled=True),
        lax.psum_scatter(grads[10], "fsdp", scatter_dimension=0, tiled=True),
        lax.psum_scatter(grads[11], "fsdp", scatter_dimension=0, tiled=True),
    )


def per_device(
    hidden_in,
    segment_ids,
    out_grad,
    norm_gain,
    w_qkv,
    w_o,
    w_zx,
    w_bc,
    w_dt,
    conv_w,
    conv_b,
    dt_bias,
    a_log,
    d_skip,
    w_out,
    second_gain,
    w_gate_up,
    w_down,
):
    micro_count = hidden_in.shape[0]
    tokens = hidden_in.shape[2]
    ctx_rank = lax.axis_index("ctx")
    group_size = HEADS // KV
    scale_attn = 1.0 / math.sqrt(HD)
    query_index = ctx_rank * tokens + jnp.arange(tokens)
    cosine, sine_table = rotary_tables(query_index.astype(jnp.float32))
    identity = (jnp.ones((MH,), jnp.float32), jnp.zeros((MH, MP, NS), jnp.float32))
    block_outs = []
    input_grads = []
    saved_list = []
    small_totals = None
    shard_totals = None
    head_totals = (
        jnp.zeros((MH,), jnp.float32),
        jnp.zeros((MH,), jnp.float32),
        jnp.zeros((MH,), jnp.float32),
    )
    for micro_index in range(micro_count):
        gathered = (
            lax.all_gather(norm_gain, "fsdp", axis=0, tiled=True),
            lax.all_gather(w_qkv, "fsdp", axis=0, tiled=True),
            lax.all_gather(w_o, "fsdp", axis=0, tiled=True),
            lax.all_gather(w_zx, "fsdp", axis=0, tiled=True),
            lax.all_gather(w_bc, "fsdp", axis=0, tiled=True),
            lax.all_gather(w_dt, "fsdp", axis=0, tiled=True),
            lax.all_gather(conv_w, "fsdp", axis=1, tiled=True),
            lax.all_gather(conv_b, "fsdp", axis=0, tiled=True),
            lax.all_gather(w_out, "fsdp", axis=0, tiled=True),
            lax.all_gather(second_gain, "fsdp", axis=0, tiled=True),
            lax.all_gather(w_gate_up, "fsdp", axis=0, tiled=True),
            lax.all_gather(w_down, "fsdp", axis=0, tiled=True),
        )
        (
            gain_full,
            qkv_full,
            o_full,
            zx_full,
            bc_full,
            dt_full,
            conv_w_full,
            conv_b_full,
            out_full,
            gain_two_full,
            gu_full,
            down_full,
        ) = gathered
        hidden = hidden_in[micro_index, 0].astype(jnp.float32)
        segments = segment_ids[micro_index, 0]
        seg_pad = jnp.concatenate([jnp.full((CONV - 1,), -1, jnp.int32), segments], axis=0)
        seg_ext = lax.dynamic_slice_in_dim(seg_pad, ctx_rank * tokens, tokens + CONV - 1)
        my_segs = seg_ext[CONV - 1 :]
        prev_seg = seg_ext[CONV - 2]
        inv_rms = lax.rsqrt(jnp.mean(hidden * hidden, axis=-1, keepdims=True) + epsilon)
        normed = (hidden * inv_rms * gain_full.astype(jnp.float32)[None, :]).astype(jnp.bfloat16)
        projected = jnp.dot(normed, qkv_full, preferred_element_type=jnp.float32)
        queries = rotate(projected[:, :QW].reshape(tokens, HEADS, HD), cosine, sine_table)
        queries = queries.astype(jnp.bfloat16).reshape(tokens, KV, group_size, HD)
        key_rows = rotate(projected[:, QW : QW + KW].reshape(tokens, KV, HD), cosine, sine_table)
        key_rows = key_rows.astype(jnp.bfloat16).reshape(tokens, KW)
        value_rows = projected[:, QW + KW :].astype(jnp.bfloat16)
        all_keys, all_values = (
            lax.all_gather(key_rows, "ctx", axis=0, tiled=True),
            lax.all_gather(value_rows, "ctx", axis=0, tiled=True),
        )
        seq_tokens = all_keys.shape[0]
        all_keys = all_keys.reshape(seq_tokens, KV, HD)
        all_values = all_values.reshape(seq_tokens, KV, HD)
        allowed = (jnp.arange(seq_tokens)[None, :] <= query_index[:, None]) & (
            segments[None, :] == my_segs[:, None]
        )
        scores = masked_scores(queries, all_keys, allowed, scale_attn)
        row_peak = jnp.max(scores, axis=-1, keepdims=True)
        expo = jnp.exp(scores - row_peak)
        row_total = jnp.sum(expo, axis=-1, keepdims=True)
        log_total = row_peak + jnp.log(row_total)
        probability = expo / row_total
        attended = (
            jnp.einsum(
                "vgqk,kvd->qvgd",
                probability.astype(jnp.bfloat16),
                all_values,
                preferred_element_type=jnp.float32,
            )
            .reshape(tokens, QW)
            .astype(jnp.bfloat16)
        )
        attn_out = jnp.dot(attended, o_full, preferred_element_type=jnp.float32)
        inner_proj = jnp.dot(normed, zx_full, preferred_element_type=jnp.float32)
        mixed_bc = jnp.dot(normed, bc_full, preferred_element_type=jnp.float32)
        step_raw = jnp.dot(normed, dt_full, preferred_element_type=jnp.float32)
        gate_z = inner_proj[:, :DI]
        conv_in = jnp.concatenate([inner_proj[:, DI:], mixed_bc], axis=1).astype(jnp.bfloat16)
        rim_rows = from_behind(conv_in[tokens - (CONV - 1) :], "ctx", 1)
        conv_ext = jnp.concatenate([rim_rows, conv_in], axis=0)
        conv_w_f = conv_w_full.astype(jnp.float32)
        conv_b_f = conv_b_full.astype(jnp.float32)
        x_heads, step_size, decay_log, input_map, output_map = mamba_parts(
            conv_ext.astype(jnp.float32),
            step_raw,
            conv_w_f,
            conv_b_f,
            dt_bias,
            a_log,
            seg_ext,
            my_segs,
        )
        local_term, carry_in, decay_total, state_local = ssd_local(
            x_heads, step_size, decay_log, input_map, output_map, my_segs, prev_seg
        )
        prefix = prefix_2((decay_total, state_local), "ctx", chain_combine, identity)
        state_in = prefix[1]
        outputs = (
            local_term
            + from_carry(output_map, carry_in, state_in)
            + d_skip[None, :, None] * x_heads
        )
        gated_out = (outputs.reshape(tokens, DI) * jax.nn.silu(gate_z)).astype(jnp.bfloat16)
        mamba_out = jnp.dot(gated_out, out_full, preferred_element_type=jnp.float32)
        middle = hidden + attn_out + mamba_out
        second_rms = lax.rsqrt(jnp.mean(middle * middle, axis=-1, keepdims=True) + epsilon)
        second_normed = (middle * second_rms * gain_two_full.astype(jnp.float32)[None, :]).astype(
            jnp.bfloat16
        )
        gate_up = jnp.dot(second_normed, gu_full, preferred_element_type=jnp.float32)
        gate_part = gate_up[:, :FF]
        up_part = gate_up[:, FF:]
        gate_sigmoid = jax.nn.sigmoid(gate_part)
        gate_silu = gate_part * gate_sigmoid
        hidden_units = (gate_silu * up_part).astype(jnp.bfloat16)
        block_outs.append(
            (middle + jnp.dot(hidden_units, down_full, preferred_element_type=jnp.float32)).astype(
                jnp.bfloat16
            )
        )
        (
            gain_back,
            qkv_back,
            o_back,
            zx_back,
            bc_back,
            dt_back,
            conv_w_back,
            conv_b_back,
            out_back,
            gain_two_back,
            gu_back,
            down_back,
        ) = gathered
        cotangent = out_grad[micro_index, 0]
        d_units = dot_last(cotangent, down_back).astype(jnp.bfloat16).astype(jnp.float32)
        d_gate_up = jnp.concatenate(
            [
                d_units * up_part * (gate_sigmoid * (1.0 + gate_part * (1.0 - gate_sigmoid))),
                d_units * gate_silu,
            ],
            axis=1,
        ).astype(jnp.bfloat16)
        d_second = dot_last(d_gate_up, gu_back)
        gain_two_f = gain_two_back.astype(jnp.float32)
        grad_gain_two_part = jnp.sum(d_second * middle * second_rms, axis=0)
        scaled_two = d_second * gain_two_f[None, :]
        d_middle = (
            cotangent.astype(jnp.float32)
            + second_rms * scaled_two
            - middle
            * second_rms
            * second_rms
            * second_rms
            * jnp.mean(middle * scaled_two, axis=-1, keepdims=True)
        )
        d_middle = d_middle.astype(jnp.bfloat16)
        d_gated = dot_last(d_middle, out_back).astype(jnp.bfloat16)
        d_attended = dot_last(d_middle, o_back).astype(jnp.bfloat16)
        scores = masked_scores(queries, all_keys, allowed, scale_attn)
        probability = jnp.exp(scores - log_total)
        d_att = d_attended.reshape(tokens, KV, group_size, HD)
        d_prob = jnp.einsum("qvgd,kvd->vgqk", d_att, all_values, preferred_element_type=jnp.float32)
        row_delta = jnp.sum(probability * d_prob, axis=-1, keepdims=True)
        d_scores = (probability * (d_prob - row_delta)).astype(jnp.bfloat16)
        d_queries = (
            jnp.einsum("vgqk,kvd->qvgd", d_scores, all_keys, preferred_element_type=jnp.float32)
            * scale_attn
        )
        d_keys = (
            jnp.einsum("vgqk,qvgd->kvd", d_scores, queries, preferred_element_type=jnp.float32)
            * scale_attn
        )
        d_values = jnp.einsum(
            "vgqk,qvgd->kvd",
            probability.astype(jnp.bfloat16),
            d_att,
            preferred_element_type=jnp.float32,
        )
        own_keys, own_values = (
            lax.psum_scatter(
                d_keys.reshape(seq_tokens, KW).astype(jnp.bfloat16),
                "ctx",
                scatter_dimension=0,
                tiled=True,
            ).astype(jnp.float32),
            lax.psum_scatter(
                d_values.reshape(seq_tokens, KW).astype(jnp.bfloat16),
                "ctx",
                scatter_dimension=0,
                tiled=True,
            ).astype(jnp.float32),
        )
        d_projected = jnp.concatenate(
            [
                unrotate(d_queries.reshape(tokens, HEADS, HD), cosine, sine_table).reshape(
                    tokens, QW
                ),
                unrotate(own_keys.reshape(tokens, KV, HD), cosine, sine_table).reshape(tokens, KW),
                own_values,
            ],
            axis=1,
        ).astype(jnp.bfloat16)
        d_normed = dot_last(d_projected, qkv_back)

        def mamba_local(
            conv_arg, step_arg, gate_arg, taps_arg, bias_arg, dtb_arg, alog_arg, skip_arg, state_arg
        ):
            return mamba_whole(
                conv_arg,
                step_arg,
                gate_arg,
                taps_arg,
                bias_arg,
                dtb_arg,
                alog_arg,
                skip_arg,
                state_arg,
                seg_ext,
                my_segs,
                prev_seg,
            )

        primal, pullback, aux_parts = jax.vjp(
            mamba_local,
            conv_ext.astype(jnp.float32),
            step_raw,
            gate_z,
            conv_w_back.astype(jnp.float32),
            conv_b_back.astype(jnp.float32),
            dt_bias,
            a_log,
            d_skip,
            state_in,
            has_aux=True,
        )
        carry_back, output_back, decay_back = aux_parts
        d_gated_f = d_gated.astype(jnp.float32)
        d_heads = (d_gated_f * jax.nn.silu(gate_z)).reshape(tokens, MH, MP)
        local_grad = jnp.einsum(
            "thp,tn->hpn", d_heads * carry_back[:, :, None], output_back, precision=highest
        )
        suffix = entering((decay_back, local_grad), "ctx", chain_combine, identity)
        (
            d_conv_ext,
            d_step_raw,
            d_gate_z,
            grad_taps,
            grad_bias,
            grad_dtb,
            grad_alog,
            grad_skip,
            _,
        ) = pullback((d_gated_f, suffix[1]))
        returned = from_behind(d_conv_ext[: CONV - 1], "ctx", -1)
        d_conv_in = d_conv_ext[CONV - 1 :] + jnp.concatenate(
            [jnp.zeros((tokens - (CONV - 1), XC), jnp.float32), returned], axis=0
        )
        d_inner = jnp.concatenate([d_gate_z, d_conv_in[:, :DI]], axis=1).astype(jnp.bfloat16)
        d_mixed = d_conv_in[:, DI:].astype(jnp.bfloat16)
        d_step = d_step_raw.astype(jnp.bfloat16)
        d_normed = (
            d_normed
            + dot_last(d_inner, zx_back)
            + dot_last(d_mixed, bc_back)
            + dot_last(d_step, dt_back)
        )
        gain_f = gain_back.astype(jnp.float32)
        grad_gain_part = jnp.sum(d_normed * hidden * inv_rms, axis=0)
        scaled_grad = d_normed * gain_f[None, :]
        grad_hidden = (
            d_middle.astype(jnp.float32)
            + inv_rms * scaled_grad
            - hidden
            * inv_rms
            * inv_rms
            * inv_rms
            * jnp.mean(hidden * scaled_grad, axis=-1, keepdims=True)
        )
        input_grads.append(grad_hidden.astype(jnp.bfloat16))
        saved = (
            normed,
            d_projected,
            d_inner,
            d_mixed,
            d_step,
            attended,
            gated_out,
            d_middle,
            second_normed,
            d_gate_up,
            hidden_units,
            cotangent,
        )
        smalls = (grad_gain_part, grad_taps, grad_bias, grad_gain_two_part)
        head_totals = (
            head_totals[0] + grad_dtb,
            head_totals[1] + grad_alog,
            head_totals[2] + grad_skip,
        )
        saved_list.append(saved)
        small_totals = (
            smalls
            if small_totals is None
            else tuple((total + part for total, part in zip(small_totals, smalls)))
        )
    shard_totals = reduce_shards(assemble(weight_products(saved_list), small_totals))
    summed = (
        lax.psum(shard_totals[0].astype(jnp.bfloat16), "ctx").astype(jnp.float32),
        lax.psum(shard_totals[1].astype(jnp.bfloat16), "ctx").astype(jnp.float32),
        lax.psum(shard_totals[2].astype(jnp.bfloat16), "ctx").astype(jnp.float32),
        lax.psum(shard_totals[3].astype(jnp.bfloat16), "ctx").astype(jnp.float32),
        lax.psum(shard_totals[4].astype(jnp.bfloat16), "ctx").astype(jnp.float32),
        lax.psum(shard_totals[5].astype(jnp.bfloat16), "ctx").astype(jnp.float32),
        lax.psum(shard_totals[6].astype(jnp.bfloat16), "ctx").astype(jnp.float32),
        lax.psum(shard_totals[7].astype(jnp.bfloat16), "ctx").astype(jnp.float32),
        lax.psum(shard_totals[8].astype(jnp.bfloat16), "ctx").astype(jnp.float32),
        lax.psum(shard_totals[9].astype(jnp.bfloat16), "ctx").astype(jnp.float32),
        lax.psum(shard_totals[10].astype(jnp.bfloat16), "ctx").astype(jnp.float32),
        lax.psum(shard_totals[11].astype(jnp.bfloat16), "ctx").astype(jnp.float32),
    )
    heads_summed = lax.psum((head_totals[0], head_totals[1], head_totals[2]), ("fsdp", "ctx"))
    block_out = jnp.stack(block_outs, axis=0)[:, None]
    grad_in = jnp.stack(input_grads, axis=0)[:, None]
    return (
        block_out,
        grad_in,
        summed[0],
        summed[1],
        summed[2],
        summed[3],
        summed[4],
        summed[5],
        summed[6],
        summed[7],
        heads_summed[0],
        heads_summed[1],
        heads_summed[2],
        summed[8],
        summed[9],
        summed[10],
        summed[11],
    )


def solution(mesh):
    return jax.shard_map(
        per_device,
        mesh=mesh,
        in_specs=(
            P(None, "fsdp", "ctx", None),
            P(None, "fsdp", None),
            P(None, "fsdp", "ctx", None),
            P("fsdp"),
            P("fsdp", None),
            P("fsdp", None),
            P("fsdp", None),
            P("fsdp", None),
            P("fsdp", None),
            P(None, "fsdp"),
            P("fsdp"),
            P(),
            P(),
            P(),
            P("fsdp", None),
            P("fsdp"),
            P("fsdp", None),
            P("fsdp", None),
        ),
        out_specs=(
            P(None, "fsdp", "ctx", None),
            P(None, "fsdp", "ctx", None),
            P("fsdp"),
            P("fsdp", None),
            P("fsdp", None),
            P("fsdp", None),
            P("fsdp", None),
            P("fsdp", None),
            P(None, "fsdp"),
            P("fsdp"),
            P(),
            P(),
            P(),
            P("fsdp", None),
            P("fsdp"),
            P("fsdp", None),
            P("fsdp", None),
        ),
        check_vma=False,
    )
```

profile of v0, /device:TPU:3, one launch (start us, length us, event | category | flops | bytes accessed | tf_op | source)
XLA Modules:
  0.0 1904.9 jit_solution(3225643427502019866)
XLA Ops:
  13.6 13.9 all-gather.4
  28.6 22.7 %all-gather.5 = bf16[8,224,4]{1,2,0:T(4,128)(2,1)S(1)} all-gather(bf16[1,224,4]{1,2,0:T(4,128)(2,1)} %bitcast.481), channel_id=1, replica_groups=mesh['fsdp'=8,'ctx'=4] {'fsdp'}, dimensions={0}, use_global_device_ids=true | all-gather | bytes 16128 | tf_op jit(solution)/shard_map/all_gather | solution.py:293
  51.6 27.5 %all_gather.107 = bf16[1024,256]{1,0:T(8,128)(2,1)S(1)} all-gather(bf16[128,256]{1,0:T(8,128)(2,1)} %param.34), channel_id=1, replica_groups=mesh['fsdp'=8,'ctx'=4] {'fsdp'}, dimensions={0}, use_global_device_ids=true | all-gather | bytes 589824 | tf_op jit(solution)/shard_map/all_gather | solution.py:291
  82.6 16.9 all-reduce.30
  101.2 21.0 %all_gather.109 = bf16[1024,24]{0,1:T(8,128)(2,1)S(1)} all-gather(bf16[128,24]{0,1:T(8,128)(2,1)S(1)} %copy-done.166), channel_id=1, replica_groups=mesh['fsdp'=8,'ctx'=4] {'fsdp'}, dimensions={0}, use_global_device_ids=true | all-gather | bytes 55296 | tf_op jit(solution)/shard_map/all_gather | solution.py:292
  131.0 24.0 %collective-permute-start = (bf16[3,1792]{1,0:T(4,128)(2,1)S(1)}, bf16[3,1792]{1,0:T(4,128)(2,1)S(1)}, u32[]{:S(2)}, u32[]{:S(2)}) collective-permute-start(bf16[3,1792]{1,0:T(4,128)(2,1)S(1)} %pad_maximum_fusion.11), channel_id=1, source_target_pairs={{0,1},{1,2},{2,3},{4,5},{5,6},{6,7},{8,9},{9,10},{10,11},{12,13},{... | collective-permute-start | bytes 32264 | tf_op jit(solution)/shard_map/ppermute | solution.py:30
  184.3 15.4 all-gather.7
  204.0 8.7 all_gather.117
  255.8 12.1 all-gather.34.cloned.1.call-done
  276.8 51.4 %all-gather.28.cloned.1.call-done = bf16[1536,1024]{1,0:T(8,128)(2,1)} async-done(((bf16[192,1024]{1,0:T(8,128)(2,1)}), bf16[1536,1024]{1,0:T(8,128)(2,1)}) %all-gather.28.cloned.1.call-update) | async-done | bytes 3145744 | tf_op jit(solution)/shard_map/all_gather | solution.py:295
  333.3 121.0 %all-gather.30.cloned.1.call-done = bf16[1024,4096]{1,0:T(8,128)(2,1)} async-done(((bf16[128,4096]{1,0:T(8,128)(2,1)}), bf16[1024,4096]{1,0:T(8,128)(2,1)}) %all-gather.30.cloned.1.call-update) | async-done | bytes 8388624 | tf_op jit(solution)/shard_map/all_gather | solution.py:297
  460.3 67.0 %all-gather.32.cloned.1.call-done = bf16[2048,1024]{1,0:T(8,128)(2,1)} async-done(((bf16[256,1024]{1,0:T(8,128)(2,1)}), bf16[2048,1024]{1,0:T(8,128)(2,1)}) %all-gather.32.cloned.1.call-update) | async-done | bytes 4194320 | tf_op jit(solution)/shard_map/all_gather | solution.py:298
  732.1 9.5 fusion.28
  774.2 38.8 %all-reduce.34 = (f32[24]{0:T(128)}, f32[24]{0:T(128)}, f32[24]{0:T(128)}) all-reduce(f32[24]{0:T(128)S(1)} %add.608, f32[24]{0:T(128)S(1)} %add_multiply_fusion, f32[24]{0:T(128)S(1)} %copy-done.177), channel_id=1, replica_groups=mesh['fsdp'=8,'ctx'=4] {'fsdp','ctx'}, use_global_device_ids=true, to_apply=%region_78.80 | all-reduce | flops 72 | bytes 576 | tf_op jit(solution)/shard_map/psum | solution.py:603
  819.5 20.5 %reduce-scatter.30.cloned.1.call-done = f32[128,256]{1,0:T(8,128)} async-done(((f32[1024,256]{1,0:T(8,128)}), f32[128,256]{1,0:T(8,128)}) %reduce-scatter.30.cloned.1.call-update) | async-done | bytes 131088 | tf_op jit(solution)/shard_map/reduce_scatter | solution.py:236
  841.6 77.3 %reduce-scatter.24.cloned.1.call-done = f32[128,768]{1,0:T(8,128)} async-done(((f32[1024,768]{1,0:T(8,128)}), f32[128,768]{1,0:T(8,128)}) %reduce-scatter.24.cloned.1.call-update) | async-done | bytes 393232 | tf_op jit(solution)/shard_map/reduce_scatter | solution.py:233
  920.6 119.1 %reduce-scatter.34.cloned.1.call-done = f32[192,1024]{1,0:T(8,128)} async-done(((f32[1536,1024]{1,0:T(8,128)}), f32[192,1024]{1,0:T(8,128)}) %reduce-scatter.34.cloned.1.call-update) | async-done | bytes 786448 | tf_op jit(solution)/shard_map/reduce_scatter | solution.py:240
  1041.6 151.2 %reduce-scatter.38.cloned.1.call-done = f32[256,1024]{1,0:T(8,128)} async-done(((f32[2048,1024]{1,0:T(8,128)}), f32[256,1024]{1,0:T(8,128)}) %reduce-scatter.38.cloned.1.call-update) | async-done | bytes 1048592 | tf_op jit(solution)/shard_map/reduce_scatter | solution.py:243
  1194.9 207.8 %reduce-scatter.28.cloned.1.call-done = f32[128,3072]{1,0:T(8,128)} async-done(((f32[1024,3072]{1,0:T(8,128)}), f32[128,3072]{1,0:T(8,128)}) %reduce-scatter.28.cloned.1.call-update) | async-done | bytes 1572880 | tf_op jit(solution)/shard_map/reduce_scatter | solution.py:235
  1405.1 283.3 %reduce-scatter.36.cloned.1.call-done = f32[128,4096]{1,0:T(8,128)} async-done(((f32[1024,4096]{1,0:T(8,128)}), f32[128,4096]{1,0:T(8,128)}) %reduce-scatter.36.cloned.1.call-update) | async-done | bytes 2097168 | tf_op jit(solution)/shard_map/reduce_scatter | solution.py:242
  1698.4 24.4 %all-reduce.35 = (bf16[1024]{0:T(1024)(128)(2,1)S(1)}, bf16[1792]{0:T(1024)(128)(2,1)S(1)}, bf16[1024]{0:T(1024)(128)(2,1)S(1)}) all-reduce(f32[1024]{0:T(1024)S(1)} %add.605, f32[1792]{0:T(1024)S(1)} %add.607, f32[1024]{0:T(1024)S(1)} %copy-done.134), channel_id=10, replica_groups=mesh['fsdp'=8,'ctx'=4] {'fsdp'}, use_global_device_ids=true, to_apply=%region_50.52.clone | all-reduce | flops 3840 | bytes 23040
  1724.0 28.3 %reduce-scatter.44.cloned.1.call-done = f32[224,4]{1,0:T(8,128)} async-done(((f32[1792,4]{1,0:T(8,128)}), f32[224,4]{1,0:T(8,128)}) %reduce-scatter.44.cloned.1.call-update) | async-done | bytes 3600
  1753.3 59.4 %reduce-scatter.32.cloned.1.call-done = f32[128,24]{0,1:T(8,128)} async-done(((f32[1024,24]{0,1:T(8,128)}), f32[128,24]{0,1:T(8,128)}) %reduce-scatter.32.cloned.1.call-update) | async-done | bytes 12304 | tf_op jit(solution)/shard_map/reduce_scatter | solution.py:237
  1824.2 63.5 %all-reduce.40.cloned.1.call-done = (bf16[128,768]{1,0:T(8,128)(2,1)}, bf16[64,1024]{1,0:T(8,128)(2,1)}, bf16[128,3072]{1,0:T(8,128)(2,1)}, bf16[128,256]{1,0:T(...) async-done(((bf16[128,768]{1,0:T(8,128)(2,1)}, bf16[64,1024]{1,0:T(8,128)(2,1)}, bf16[128,3072]{1,0:T(8,128)(2,1)}, ...) | async-done | bytes 3145744 | tf_op jit(solution)/shard_map/psum | solution.py:591
  (753 shorter events, 417.1 us)
Async XLA Ops:
  7.2 118.7 %all-gather.26.cloned.1.call-start = ((), (), s32[]{:S(2)}) async-start(), calls=%async_computation.15 | async-start | bytes 7077888 | tf_op jit(solution)/shard_map/all_gather | solution.py:290
  8.0 191.8 %all-gather.22.cloned.1.call-start = ((), (), s32[]{:S(2)}) async-start(), calls=%async_computation.13 | async-start | bytes 1769472 | tf_op jit(solution)/shard_map/all_gather | solution.py:288
  8.7 233.5 %all-gather.24.cloned.1.call-start = ((), (), s32[]{:S(2)}) async-start(), calls=%async_computation.14 | async-start | bytes 1179648 | tf_op jit(solution)/shard_map/all_gather | solution.py:289
  9.4 237.8 %all-gather.36.cloned.1.call-start = ((), (), s32[]{:S(2)}) async-start(), calls=%async_computation.30 | async-start | bytes 3932160 | tf_op jit(solution)/shard_map/all_gather | solution.py:35
  163.3 104.6 %all-gather.34.cloned.1.call-start = ((), (), s32[]{:S(2)}) async-start(), calls=%async_computation.29 | async-start | bytes 3932160 | tf_op jit(solution)/shard_map/all_gather | solution.py:35
  168.5 159.7 %all-gather.28.cloned.1.call-start = ((), (), s32[]{:S(2)}) async-start(), calls=%async_computation.16 | async-start | bytes 3538944 | tf_op jit(solution)/shard_map/all_gather | solution.py:295
  169.1 285.3 %all-gather.30.cloned.1.call-start = ((), (), s32[]{:S(2)}) async-start(), calls=%async_computation.17 | async-start | bytes 9437184 | tf_op jit(solution)/shard_map/all_gather | solution.py:297
  169.9 357.5 %all-gather.32.cloned.1.call-start = ((), (), s32[]{:S(2)}) async-start(), calls=%async_computation.18 | async-start | bytes 4718592 | tf_op jit(solution)/shard_map/all_gather | solution.py:298
  170.6 462.5 %all-gather.38.cloned.1.call-start = ((), (), s32[]{:S(2)}) async-start(), calls=%async_computation.31 | async-start | bytes 1966080 | tf_op jit(solution)/shard_map/all_gather | solution.py:49
  554.0 89.1 %all-gather.40.cloned.1.call-start = ((), (), s32[]{:S(2)}) async-start(), calls=%async_computation.32 | async-start | bytes 1966080 | tf_op jit(solution)/shard_map/all_gather | solution.py:49
  593.3 96.0 %reduce-scatter.20.cloned.1.call-start = ((), (), s32[]{:S(2)}) async-start(), calls=%async_computation.19 | async-start | bytes 81920 | tf_op jit(solution)/shard_map/reduce_scatter | solution.py:462
  620.1 70.6 %reduce-scatter.22.cloned.1.call-start = ((), (), s32[]{:S(2)}) async-start(), calls=%async_computation.20 | async-start | bytes 81920 | tf_op jit(solution)/shard_map/reduce_scatter | solution.py:462
  623.6 80.2 %reduce-scatter.42.cloned.1.call-start = ((), (), s32[]{:S(2)}) async-start(), calls=%async_computation.34 | async-start | bytes 81920
  626.9 78.4 %reduce-scatter.40.cloned.1.call-start = ((), (), s32[]{:S(2)}) async-start(), calls=%async_computation.33 | async-start | bytes 81920
  630.1 187.8 %reduce-scatter.26.cloned.1.call-start = ((), (), s32[]{:S(2)}) async-start(), calls=%async_computation.22 | async-start | bytes 2359296 | tf_op jit(solution)/shard_map/reduce_scatter | solution.py:234
  633.0 207.0 %reduce-scatter.30.cloned.1.call-start = ((), (), s32[]{:S(2)}) async-start(), calls=%async_computation.24 | async-start | bytes 1179648 | tf_op jit(solution)/shard_map/reduce_scatter | solution.py:236
  686.8 232.2 %reduce-scatter.24.cloned.1.call-start = ((), (), s32[]{:S(2)}) async-start(), calls=%async_computation.21 | async-start | bytes 3538944 | tf_op jit(solution)/shard_map/reduce_scatter | solution.py:233
  710.1 329.6 %reduce-scatter.34.cloned.1.call-start = ((), (), s32[]{:S(2)}) async-start(), calls=%async_computation.26 | async-start | bytes 7077888 | tf_op jit(solution)/shard_map/reduce_scatter | solution.py:240
  715.0 477.8 %reduce-scatter.38.cloned.1.call-start = ((), (), s32[]{:S(2)}) async-start(), calls=%async_computation.28 | async-start | bytes 9437184 | tf_op jit(solution)/shard_map/reduce_scatter | solution.py:243
  721.8 680.8 %reduce-scatter.28.cloned.1.call-start = ((), (), s32[]{:S(2)}) async-start(), calls=%async_computation.23 | async-start | bytes 14155776 | tf_op jit(solution)/shard_map/reduce_scatter | solution.py:235
  732.1 956.2 %reduce-scatter.36.cloned.1.call-start = ((), (), s32[]{:S(2)}) async-start(), calls=%async_computation.27 | async-start | bytes 18874368 | tf_op jit(solution)/shard_map/reduce_scatter | solution.py:242
  741.7 1010.7 %reduce-scatter.44.cloned.1.call-start = ((), (), s32[]{:S(2)}) async-start(), calls=%async_computation.35 | async-start | bytes 1032192
  773.2 1039.5 %reduce-scatter.32.cloned.1.call-start = ((), (), s32[]{:S(2)}) async-start(), calls=%async_computation.25 | async-start | bytes 110592 | tf_op jit(solution)/shard_map/reduce_scatter | solution.py:237
  774.2 1113.5 %all-reduce.40.cloned.1.call-start = ((), (), s32[]{:S(2)}) async-start(), calls=%async_computation.36 | async-start | bytes 6291456 | tf_op jit(solution)/shard_map/psum | solution.py:591
  (184 other events, 5502.8 us)
Sparse Core Ops, SparseCore 0:
  10.2 108.9 all-gather.25
  121.4 42.4 all-gather.21
  166.1 38.2 all-gather.23
  206.3 31.1 all-gather.35
  239.5 28.3 all-gather.33
  269.9 58.2 all-gather.27
  330.3 123.9 all-gather.29
  456.5 70.7 all-gather.31
  554.1 20.4 all-gather.37
  593.4 18.7 all-gather.39
  620.2 17.6 reduce-scatter.19
  640.3 19.4 reduce-scatter.21
  662.2 19.4 reduce-scatter.41
  684.1 19.4 reduce-scatter.39
  707.5 66.0 reduce-scatter.25
  777.5 62.4 reduce-scatter.29
  843.9 74.9 reduce-scatter.23
  922.8 116.8 reduce-scatter.33
  1043.8 149.0 reduce-scatter.37
  1196.2 206.3 reduce-scatter.27
  1406.4 281.8 reduce-scatter.35
  1692.6 59.7 reduce-scatter.43
  1755.6 57.0 reduce-scatter.31
  1817.1 70.4 all-reduce.39
where the time goes:
time: 1920 us; the launch traced here: 1900 us
  waiting for transfers between devices  1270 us (66%)
  blocking collectives  237 us (12%)
  matrix products  181 us (9%)
  other arithmetic  95.7 us (5%)
  local copies, waits for them, and re-layouts  66.7 us (3%)
  starting transfers between devices  31.8 us (2%)
  between operations  22 us (1%)
    reduce_scatter x1, waiting for transfers between devices, reduce_shards(): lax.psum_scatter(grads[10], 'fsdp', scatter_dimension=0, tiled=True)  283 us
    reduce_scatter x1, waiting for transfers between devices, reduce_shards(): lax.psum_scatter(grads[3], 'fsdp', scatter_dimension=0, tiled=True)  208 us
    reduce_scatter x1, waiting for transfers between devices, reduce_shards(): lax.psum_scatter(grads[11], 'fsdp', scatter_dimension=0, tiled=True)  151 us
    all_gather x1, waiting for transfers between devices, per_device(): lax.all_gather(w_gate_up, 'fsdp', axis=0, tiled=True)  121 us
    reduce_scatter x1, waiting for transfers between devices, reduce_shards(): lax.psum_scatter(grads[8], 'fsdp', scatter_dimension=0, tiled=True)  119 us
    reduce_scatter x1, waiting for transfers between devices, reduce_shards(): lax.psum_scatter(grads[1], 'fsdp', scatter_dimension=0, tiled=True)  77.3 us
    all_gather x1, waiting for transfers between devices, per_device(): lax.all_gather(w_down, 'fsdp', axis=0, tiled=True)  67 us
    psum x1, waiting for transfers between devices, per_device(): lax.psum(shard_totals[1].astype(jnp.bfloat16), 'ctx').astype(jnp.float32)  63.5 us
  transfers between devices with their start and end apart: 28, of which 16 were waited for; matrix products, arithmetic and copies ran while one was open for 16% of the time, Pallas kernels for 0%

commit v1 on v0

v1 whole, which is shorter than its diff:
```python
import math

import jax
import jax.numpy as jnp
from jax import lax
from jax.sharding import PartitionSpec as P

HEADS = 8
KV = 2
HD = 64
MH = 24
MP = 64
NS = 128
CONV = 4
FF = 2048
QW = 512
KW = 128
DI = 1536
XC = 1792

epsilon = 1e-05
rope_base = 100000000000.0
f32 = jnp.float32
bf16 = jnp.bfloat16


def dot_plain(left, right):
    return jnp.dot(left, right, preferred_element_type=f32)


def dot_first(left, right):
    return lax.dot_general(left, right, (((0,), (0,)), ((), ())), preferred_element_type=f32)


def dot_last(left, right):
    return lax.dot_general(left, right, (((1,), (1,)), ((), ())), preferred_element_type=f32)


def swap(block, axis, bit):
    devices = range(lax.axis_size(axis))
    return lax.ppermute(block, axis, [(i, i ^ bit) for i in devices])


def ctx_gather(block):
    size = lax.axis_size("ctx")
    place = lax.axis_index("ctx")
    out = block[None]
    bit = size // 2
    while bit:
        other = swap(out, "ctx", bit)
        low = (place // bit) % 2 == 0
        out = jnp.where(low, jnp.stack([out, other], 1), jnp.stack([other, out], 1))
        out = out.reshape((-1,) + block.shape)
        bit //= 2
    return out


def ctx_scatter(parts):
    size = lax.axis_size("ctx")
    place = lax.axis_index("ctx")
    bit = 1
    while bit < size:
        mine = (place // bit) % 2
        parts = parts.reshape((-1, 2) + parts.shape[1:])
        keep = lax.dynamic_index_in_dim(parts, mine, 1, False)
        send = lax.dynamic_index_in_dim(parts, 1 - mine, 1, False)
        got = swap(send.astype(bf16), "ctx", bit)
        parts = keep.astype(f32) + got.astype(f32)
        bit *= 2
    return parts[0]


def everywhere_sum(value):
    for axis in ("ctx", "fsdp"):
        bit = 1
        while bit < lax.axis_size(axis):
            value = value + swap(value, axis, bit)
            bit *= 2
    return value


def to_owner_columns(rows, back):
    F, C = lax.axis_size("fsdp"), lax.axis_size("ctx")
    route = []
    for f in range(F):
        for c in range(C):
            pair = (f * C + c, ((f % (F // C)) * C + c) * C + f // (F // C))
            route.append(pair[::-1] if back else pair)
    return lax.ppermute(rows, ("fsdp", "ctx"), route)


def rotary_tables(positions):
    half_width = HD // 2
    exponents = jnp.arange(half_width, dtype=f32) * (2.0 / HD)
    inverse = jnp.exp(-exponents * math.log(rope_base))
    angles = positions[:, None] * inverse[None, :]
    cosine = jnp.concatenate([jnp.cos(angles), jnp.cos(angles)], axis=1)
    sine = jnp.concatenate([jnp.sin(angles), jnp.sin(angles)], axis=1)
    return (cosine, sine)


def rotate(values, cosine, sine):
    half = HD // 2
    turned = jnp.concatenate([-values[..., half:], values[..., :half]], axis=-1)
    return values * cosine[:, None, :] + turned * sine[:, None, :]


def unrotate(grads, cosine, sine):
    half = HD // 2
    scaled = grads * sine[:, None, :]
    turned = jnp.concatenate([scaled[..., half:], -scaled[..., :half]], axis=-1)
    return grads * cosine[:, None, :] + turned


def shifted(rows, distance):
    if distance == 0:
        return rows
    if distance > 0:
        return jnp.pad(rows, ((0, 0), (distance, 0), (0, 0)))[:, : rows.shape[1]]
    return jnp.pad(rows, ((0, 0), (0, -distance), (0, 0)))[:, -distance:]


def conv_masks(segments):
    masks = []
    for distance in range(CONV):
        behind = jnp.pad(segments, ((0, 0), (distance, 0)), constant_values=-1)
        masks.append((behind[:, : segments.shape[1]] == segments)[:, :, None])
    return masks


def mamba_forward(conv_in, dt_raw, gate_z, taps, bias, dt_bias, a_rate, skip, segments):
    micro, length, _ = conv_in.shape
    heads = dt_bias.shape[0]
    width = heads * MP
    masks = conv_masks(segments)
    conv_f = conv_in.astype(f32)
    behind = [jnp.where(masks[k], shifted(conv_f, k), 0.0) for k in range(CONV)]
    pre = bias[None, None, :]
    for k in range(CONV):
        pre = pre + behind[k] * taps[CONV - 1 - k][None, None, :]
    act = jax.nn.silu(pre)
    x_heads = act[..., :width].reshape(micro, length, heads, MP)
    b_map = act[..., width : width + NS].astype(bf16)
    c_map = act[..., width + NS :].astype(bf16)
    step_pre = dt_raw + dt_bias
    step = jax.nn.softplus(step_pre)
    decay_log = -step * a_rate
    cum = jnp.cumsum(decay_log, axis=1)
    order = jnp.arange(length)
    valid = (order[:, None] >= order[None, :])[None] & (
        segments[:, :, None] == segments[:, None, :]
    )
    cum_h = cum.transpose(0, 2, 1)
    spread = cum_h[:, :, :, None] - cum_h[:, :, None, :]
    kernel = jnp.exp(jnp.where(valid[:, None], spread, -1e30))
    cross = jnp.einsum("mtn,msn->mts", c_map, b_map, preferred_element_type=f32)
    weighted = kernel * cross[:, None]
    driven = x_heads * step[..., None]
    y_state = jnp.einsum(
        "mhts,mshp->mthp", weighted.astype(bf16), driven.astype(bf16), preferred_element_type=f32
    )
    y = (y_state + skip[:, None] * x_heads).reshape(micro, length, width)
    gated = (y * jax.nn.silu(gate_z)).astype(bf16)
    saved = (behind, pre, x_heads, b_map, c_map, step_pre, step, decay_log, kernel, cross, driven, y, masks)
    return gated, saved


def silu_slope(v):
    s = jax.nn.sigmoid(v)
    return s * (1.0 + v * (1.0 - s))


def mamba_backward(saved, d_gated, gate_z, taps, a_rate, skip):
    behind, pre, x_heads, b_map, c_map, step_pre, step, decay_log, kernel, cross, driven, y, masks = saved
    micro, length, heads, _ = x_heads.shape
    d_y = (d_gated * jax.nn.silu(gate_z)).reshape(micro, length, heads, MP)
    d_gate = d_gated * y * silu_slope(gate_z)
    d_y16 = d_y.astype(bf16)
    weighted = kernel * cross[:, None]
    d_weighted = jnp.einsum("mthp,mshp->mhts", d_y16, driven.astype(bf16), preferred_element_type=f32)
    d_driven = jnp.einsum("mhts,mthp->mshp", weighted.astype(bf16), d_y16, preferred_element_type=f32)
    d_cross = jnp.sum(d_weighted * kernel, axis=1).astype(bf16)
    pairs = d_weighted * weighted
    d_cum = (jnp.sum(pairs, axis=3) - jnp.sum(pairs, axis=2)).transpose(0, 2, 1)
    d_decay_log = jnp.cumsum(d_cum[:, ::-1], axis=1)[:, ::-1]
    d_c = jnp.einsum("mts,msn->mtn", d_cross, b_map, preferred_element_type=f32)
    d_b = jnp.einsum("mts,mtn->msn", d_cross, c_map, preferred_element_type=f32)
    d_x = d_driven * step[..., None] + skip[:, None] * d_y
    d_step = jnp.sum(d_driven * x_heads, axis=-1) - d_decay_log * a_rate
    d_dt = d_step * jax.nn.sigmoid(step_pre)
    g_dt_bias = jnp.sum(d_dt, axis=(0, 1))
    g_a_log = jnp.sum(d_decay_log * decay_log, axis=(0, 1))
    g_skip = jnp.sum(d_y * x_heads, axis=(0, 1, 3))
    d_act = jnp.concatenate([d_x.reshape(micro, length, heads * MP), d_b, d_c], axis=2)
    d_pre = d_act * silu_slope(pre)
    g_bias = jnp.sum(d_pre, axis=(0, 1))
    g_taps = jnp.stack([jnp.sum(d_pre * behind[CONV - 1 - j], axis=(0, 1)) for j in range(CONV)])
    d_conv = 0.0
    for k in range(CONV):
        d_conv = d_conv + shifted(jnp.where(masks[k], d_pre, 0.0), -k) * taps[CONV - 1 - k]
    return d_gate, d_conv, d_dt, g_taps, g_bias, g_dt_bias, g_a_log, g_skip


def attend(queries, keys, values, allowed, scale):
    scores = jnp.einsum("mqhd,mkd->mhqk", queries, keys, preferred_element_type=f32) * scale
    scores = jnp.where(allowed[:, None], scores, -1e30)
    peak = jnp.max(scores, axis=-1, keepdims=True)
    expo = jnp.exp(scores - peak)
    probability = expo / jnp.sum(expo, axis=-1, keepdims=True)
    attended = jnp.einsum(
        "mhqk,mkd->mqhd", probability.astype(bf16), values, preferred_element_type=f32
    )
    return probability, attended


def attend_back(probability, d_att, queries, keys, values, scale):
    d_prob = jnp.einsum("mqhd,mkd->mhqk", d_att, values, preferred_element_type=f32)
    delta = jnp.sum(probability * d_prob, axis=-1, keepdims=True)
    d_scores = (probability * (d_prob - delta)).astype(bf16)
    d_q = jnp.einsum("mhqk,mkd->mqhd", d_scores, keys, preferred_element_type=f32) * scale
    d_k = jnp.einsum("mhqk,mqhd->mkd", d_scores, queries, preferred_element_type=f32) * scale
    d_v = jnp.einsum(
        "mhqk,mqhd->mkd", probability.astype(bf16), d_att, preferred_element_type=f32
    )
    return d_q, d_k, d_v


def per_device(
    hidden_in,
    segment_ids,
    out_grad,
    norm_gain,
    w_qkv,
    w_o,
    w_zx,
    w_bc,
    w_dt,
    conv_w,
    conv_b,
    dt_bias,
    a_log,
    d_skip,
    w_out,
    second_gain,
    w_gate_up,
    w_down,
):
    micro, _, tokens, D = hidden_in.shape
    F, C = lax.axis_size("fsdp"), lax.axis_size("ctx")
    c = lax.axis_index("ctx")
    f = lax.axis_index("fsdp")
    length = tokens * C
    rows = micro * length
    qh, mh = HEADS // C, MH // C
    qw, dw, fw = QW // C, DI // C, FF // C
    kv = c * KV // C
    scale = 1.0 / math.sqrt(HD)
    dt_pad = 128 - mh

    def cols(weight, start, size):
        return lax.dynamic_slice_in_dim(weight, start, size, 1)

    block = w_qkv.shape[0]
    first_shard = jnp.concatenate(
        [
            cols(w_qkv, c * qw, qw),
            cols(w_qkv, QW + kv * HD, HD),
            cols(w_qkv, QW + KW + kv * HD, HD),
            cols(w_zx, c * dw, dw),
            cols(w_zx, DI + c * dw, dw),
            w_bc,
            cols(w_dt, c * mh, mh),
            jnp.zeros((block, dt_pad), bf16),
        ],
        axis=1,
    )
    gu_shard = jnp.concatenate([cols(w_gate_up, c * fw, fw), cols(w_gate_up, FF + c * fw, fw)], 1)
    ro, rz, rd = w_o.shape[0] // C, w_out.shape[0] // C, w_down.shape[0] // C
    row_shard = jnp.concatenate(
        [
            lax.dynamic_slice_in_dim(w_o, c * ro, ro, 0),
            lax.dynamic_slice_in_dim(w_out, c * rz, rz, 0),
            lax.dynamic_slice_in_dim(w_down, c * rd, rd, 0),
        ],
        axis=0,
    )
    row_shard = to_owner_columns(row_shard, False)
    xb = conv_b.shape[0]
    small_shard = jnp.concatenate(
        [conv_w.reshape(-1), conv_b, norm_gain, second_gain], axis=0
    )
    small_all = lax.all_gather(small_shard, "fsdp", axis=0, tiled=False)
    w_first = lax.all_gather(first_shard, "fsdp", axis=0, tiled=True)
    row_all = lax.all_gather(row_shard, "fsdp", axis=0, tiled=False)
    w_gu = lax.all_gather(gu_shard, "fsdp", axis=0, tiled=True)

    conv_all = small_all[:, : (CONV + 1) * xb].reshape(F, CONV + 1, xb)
    conv_all = conv_all.transpose(1, 0, 2).reshape(CONV + 1, XC).astype(f32)
    conv_own = jnp.concatenate([cols(conv_all, c * dw, dw), conv_all[:, DI:]], axis=1)
    taps, conv_bias = conv_own[:CONV], conv_own[CONV]
    gains = small_all[:, (CONV + 1) * xb :].astype(f32)
    gain = gains[:, :block].reshape(1, D)
    gain_two = gains[:, block:].reshape(1, D)
    w_o_own = row_all[:, :ro].reshape(F * ro, D)
    w_out_own = row_all[:, ro : ro + rz].reshape(F * rz, D)
    w_down_own = row_all[:, ro + rz :].reshape(F * rd, D)
    dtb = lax.dynamic_slice_in_dim(dt_bias, c * mh, mh, 0)
    a_rate = jnp.exp(lax.dynamic_slice_in_dim(a_log, c * mh, mh, 0))
    skip = lax.dynamic_slice_in_dim(d_skip, c * mh, mh, 0)

    def gather_tokens(own):
        return ctx_gather(own).transpose(1, 0, 2, 3).reshape(rows, D)

    def scatter_tokens(partial):
        return ctx_scatter(partial.reshape(micro, C, tokens, D).transpose(1, 0, 2, 3))

    hidden_own = hidden_in[:, 0].astype(f32)
    hidden = gather_tokens(hidden_in[:, 0]).astype(f32)
    cot = gather_tokens(out_grad[:, 0])
    segments = segment_ids[:, 0]
    order = jnp.arange(length)
    cosine, sine = rotary_tables(order.astype(f32))
    allowed = (order[None, :] <= order[:, None])[None] & (
        segments[:, None, :] == segments[:, :, None]
    )

    inv_rms = lax.rsqrt(jnp.mean(hidden * hidden, axis=-1, keepdims=True) + epsilon)
    normed = (hidden * inv_rms * gain).astype(bf16)
    first = dot_plain(normed, w_first).reshape(micro, length, -1)
    at = qw
    queries = rotate(first[..., :qw].reshape(micro, length, qh, HD), cosine, sine).astype(bf16)
    keys = rotate(first[..., at : at + HD].reshape(micro, length, 1, HD), cosine, sine)[:, :, 0].astype(bf16)
    values = first[..., at + HD : at + 2 * HD].astype(bf16)
    at += 2 * HD
    gate_z = first[..., at : at + dw]
    at += dw
    conv_in = first[..., at : at + dw + 2 * NS].astype(bf16)
    at += dw + 2 * NS
    dt_raw = first[..., at : at + mh]

    probability, attended = attend(queries, keys, values, allowed, scale)
    attended = attended.reshape(rows, qw).astype(bf16)
    gated, saved = mamba_forward(conv_in, dt_raw, gate_z, taps, conv_bias, dtb, a_rate, skip, segments)
    gated = gated.reshape(rows, dw)
    mixed = dot_plain(attended, w_o_own) + dot_plain(gated, w_out_own)
    middle = hidden_own + scatter_tokens(mixed)
    second_rms = lax.rsqrt(jnp.mean(middle * middle, axis=-1, keepdims=True) + epsilon)
    second_normed = gather_tokens((middle * second_rms * gain_two).astype(bf16))

    gate_up = dot_plain(second_normed, w_gu)
    gate_part, up_part = gate_up[:, :fw], gate_up[:, fw:]
    sig = jax.nn.sigmoid(gate_part)
    gate_silu = gate_part * sig
    units = (gate_silu * up_part).astype(bf16)
    d_units = dot_last(cot, w_down_own).astype(bf16).astype(f32)
    d_gate_up = jnp.concatenate(
        [d_units * up_part * (sig * (1.0 + gate_part * (1.0 - sig))), d_units * gate_silu], axis=1
    ).astype(bf16)
    d_second = scatter_tokens(dot_last(d_gate_up, w_gu))
    block_out = (middle + scatter_tokens(dot_plain(units, w_down_own))).astype(bf16)
    g_gu = dot_first(second_normed, d_gate_up)
    g_down = dot_first(units, cot)

    g_gain_two = jnp.sum(d_second * middle * second_rms, axis=(0, 1))
    scaled_two = d_second * gain_two
    d_middle_own = (
        out_grad[:, 0].astype(f32)
        + second_rms * scaled_two
        - middle * second_rms**3 * jnp.mean(middle * scaled_two, axis=-1, keepdims=True)
    ).astype(bf16)
    d_middle = gather_tokens(d_middle_own)
    d_gated = dot_last(d_middle, w_out_own).astype(bf16).astype(f32).reshape(micro, length, dw)
    d_att = dot_last(d_middle, w_o_own).astype(bf16).reshape(micro, length, qh, HD)
    g_o = dot_first(attended, d_middle)
    g_out = dot_first(gated, d_middle)

    d_q, d_k, d_v = attend_back(probability, d_att, queries, keys, values, scale)
    d_q = unrotate(d_q, cosine, sine).reshape(micro, length, qw)
    d_k = unrotate(d_k[:, :, None], cosine, sine)[:, :, 0]
    d_gate, d_conv, d_dt, g_taps, g_bias, g_dtb, g_alog, g_skip = mamba_backward(
        saved, d_gated, gate_z, taps, a_rate, skip
    )
    d_first = jnp.concatenate(
        [d_q, d_k, d_v, d_gate, d_conv, d_dt, jnp.zeros((micro, length, dt_pad), f32)], axis=2
    )
    d_first = d_first.astype(bf16).reshape(rows, -1)
    d_normed_part = dot_last(d_first, w_first)
    g_first = dot_first(normed, d_first)
    g_gain = jnp.sum(d_normed_part * hidden * inv_rms, axis=0)
    d_normed = scatter_tokens(d_normed_part)
    inv_own = lax.rsqrt(jnp.mean(hidden_own * hidden_own, axis=-1, keepdims=True) + epsilon)
    scaled = d_normed * gain
    grad_in = (
        d_middle_own.astype(f32)
        + inv_own * scaled
        - hidden_own * inv_own**3 * jnp.mean(hidden_own * scaled, axis=-1, keepdims=True)
    ).astype(bf16)

    ffn = jnp.concatenate([g_gu.reshape(F, block, -1), g_down.reshape(F, rd, D)], axis=1)
    ffn = lax.psum_scatter(ffn.astype(bf16), "fsdp", scatter_dimension=0, tiled=False)
    mix = jnp.concatenate([g_o.reshape(F, ro, D), g_out.reshape(F, rz, D)], axis=1)
    mix = lax.psum_scatter(mix.astype(bf16), "fsdp", scatter_dimension=0, tiled=False)
    first_sum = lax.psum_scatter(g_first.astype(bf16), "fsdp", scatter_dimension=0, tiled=True)
    turned = to_owner_columns(jnp.concatenate([mix, ffn[block:]], axis=0), True)
    turned = ctx_gather(turned).astype(f32)
    grad_o = turned[:, :ro].reshape(C * ro, D)
    grad_out = turned[:, ro : ro + rz].reshape(C * rz, D)
    grad_down = turned[:, ro + rz :].reshape(C * rd, D)

    def side(parts):
        return jnp.concatenate([parts[i] for i in range(C)], axis=1)

    gu_all = ctx_gather(ffn[:block]).astype(f32)
    grad_gate_up = jnp.concatenate([side(gu_all[:, :, :fw]), side(gu_all[:, :, fw:])], axis=1)
    first_all = ctx_gather(first_sum).astype(f32)
    at = qw
    kv_pairs = first_all[:, :, at : at + 2 * HD].reshape(KV, C // KV, block, 2 * HD).sum(1)
    grad_qkv = jnp.concatenate(
        [side(first_all[:, :, :qw])]
        + [kv_pairs[j, :, :HD] for j in range(KV)]
        + [kv_pairs[j, :, HD:] for j in range(KV)],
        axis=1,
    )
    at += 2 * HD
    grad_zx = jnp.concatenate(
        [side(first_all[:, :, at : at + dw]), side(first_all[:, :, at + dw : at + 2 * dw])], axis=1
    )
    at += 2 * dw
    grad_bc = first_all[:, :, at : at + 2 * NS].sum(0)
    at += 2 * NS
    grad_dt = side(first_all[:, :, at : at + mh])

    g_conv = jnp.concatenate([g_taps, g_bias[None]], axis=0)
    conv_x = lax.dynamic_update_slice(
        jnp.zeros((CONV + 1, DI), f32), g_conv[:, :dw], (0, c * dw)
    )
    conv_full = jnp.concatenate([conv_x, g_conv[:, dw:]], axis=1)
    conv_full = conv_full.reshape(CONV + 1, F, xb).transpose(1, 0, 2).reshape(F, -1)
    small = jnp.concatenate([conv_full, g_gain.reshape(F, block), g_gain_two.reshape(F, block)], 1)
    heads = jnp.stack([g_dtb, g_alog, g_skip])
    heads = lax.dynamic_update_slice(jnp.zeros((3, MH), f32), heads, (0, c * mh))
    small = lax.psum_scatter(small, "fsdp", scatter_dimension=0, tiled=False)
    small = lax.psum(small, "ctx")
    heads = lax.psum(heads, ("fsdp", "ctx"))
    conv_sum = small[: (CONV + 1) * xb].reshape(CONV + 1, xb)
    at = (CONV + 1) * xb
    return (
        block_out[:, None],
        grad_in[:, None],
        small[at : at + block],
        grad_qkv,
        grad_o,
        grad_zx,
        grad_bc,
        grad_dt,
        conv_sum[:CONV],
        conv_sum[CONV],
        heads[0],
        heads[1],
        heads[2],
        grad_out,
        small[at + block :],
        grad_gate_up,
        grad_down,
    )


def solution(mesh):
    tokens = P(None, "fsdp", "ctx", None)
    rows = P("fsdp", None)
    return jax.shard_map(
        per_device,
        mesh=mesh,
        in_specs=(
            tokens,
            P(None, "fsdp", None),
            tokens,
            P("fsdp"),
            rows,
            rows,
            rows,
            rows,
            rows,
            P(None, "fsdp"),
            P("fsdp"),
            P(),
            P(),
            P(),
            rows,
            P("fsdp"),
            rows,
            rows,
        ),
        out_specs=(
            tokens,
            tokens,
            P("fsdp"),
            rows,
            rows,
            rows,
            rows,
            rows,
            P(None, "fsdp"),
            P("fsdp"),
            P(),
            P(),
            P(),
            rows,
            P("fsdp"),
            rows,
            rows,
        ),
        check_vma=False,
    )
```

time: 1920 us -> 507 us (0.26)
  waiting for transfers between devices: 1270 us -> 121 us
  blocking collectives: 237 us -> 103 us
  matrix products: 181 us -> 56.9 us
  other arithmetic: 95.7 us -> 65.8 us
  local copies, waits for them, and re-layouts: 66.7 us -> 91.1 us
    reduce_scatter x10 -> x3, waiting for transfers between devices: 919 us -> 12.7 us  [the longest x1 12.7 us: per_device(): lax.psum_scatter(g_first.astype(bf16), 'fsdp', scatter_dimension=0, tiled...]
    all_gather x10 -> x3, waiting for transfers between devices: 252 us -> 48.8 us  [the longest x1 48.8 us: per_device(): w_first = lax.all_gather(first_shard, 'fsdp', axis=0, tiled=True)]
    all_gather x13 -> x0, blocking collectives: 149 us -> none  [the longest x1 27.5 us: per_device(): lax.all_gather(w_bc, 'fsdp', axis=0, tiled=True)]
    dot_general x52 -> x16, matrix products: 101 us -> 32.9 us  [the longest x5 10.3 us: dot_plain(): return jnp.dot(left, right, preferred_element_type=f32)]
    psum x1 -> x0, waiting for transfers between devices: 63.5 us -> none  [per_device(): lax.psum(shard_totals[1].astype(jnp.bfloat16), 'ctx').astype(jnp.float32)]
    ppermute x4 -> x24, waiting for transfers between devices: 3.56 us -> 59 us  [the longest x22 31.1 us: swap(): return lax.ppermute(block, axis, [(i, i ^ bit) for i in devices])]
    convert_element_type x45 -> x15, other arithmetic: 42.7 us -> 8.93 us  [the longest x1 1.79 us: per_device(): rotate(first[..., :qw].reshape(micro, length, qh, HD), cosine, sine)]
    unnamed x27 -> x6, waiting for transfers between devices: 32.6 us -> 0.1 us
  transfers between devices with their start and end apart: 28 -> 30, of which waited for: 16 -> 14; matrix products, arithmetic and copies ran while one was open for 16% -> 38% of each run, Pallas kernels for 0% -> 0%
where the time goes in v1:
time: 507 us; the launch traced here: 498 us
  waiting for transfers between devices  121 us (24%)
  blocking collectives  103 us (20%)
  local copies, waits for them, and re-layouts  91.1 us (18%)
  other arithmetic  65.8 us (13%)
  matrix products  56.9 us (11%)
  starting transfers between devices  43.6 us (9%)
  between operations  17.2 us (3%)
    unnamed x2, blocking collectives  50.8 us
    all_gather x1, waiting for transfers between devices, per_device(): w_first = lax.all_gather(first_shard, 'fsdp', axis=0, tiled=True)  48.8 us
    psum x1, blocking collectives, per_device(): heads = lax.psum(heads, ('fsdp', 'ctx'))  40 us
    ppermute x22, starting transfers between devices, swap(): return lax.ppermute(block, axis, [(i, i ^ bit) for i in devices])  34 us
    ppermute x22, waiting for transfers between devices, swap(): return lax.ppermute(block, axis, [(i, i ^ bit) for i in devices])  31.1 us
    ppermute x2, waiting for transfers between devices, to_owner_columns(): return lax.ppermute(rows, ('fsdp', 'ctx'), route)  27.9 us
    another operation x10, other arithmetic  18.6 us
    unnamed x249, local copies, waits for them, and re-layouts  17.7 us
  transfers between devices with their start and end apart: 30, of which 14 were waited for; matrix products, arithmetic and copies ran while one was open for 38% of the time, Pallas kernels for 0%

profile of v1, /device:TPU:3, one launch (start us, length us, event | category | flops | bytes accessed | tf_op | source)
XLA Modules:
  0.0 498.2 jit_solution(12488190425630909869)
XLA Ops:
  10.0 4.9 collective-permute-start.2
  14.9 17.0 %collective-permute-done.2 = bf16[128,1024]{1,0:T(8,128)(2,1)S(1)} collective-permute-done((bf16[128,1024]{1,0:T(8,128)(2,1)S(1)}, bf16[128,1024]{1,0:T(8,128)(2,1)S(1)}, u32[]{:S(2)}, u32[]{:S(2)}) %collective-permute-start.2) | collective-permute-done | bytes 262176 | tf_op jit(solution)/shard_map/ppermute | solution.py:89
  40.9 24.9 %all-reduce.9 = bf16[11008]{0:T(1024)(128)(2,1)S(1)} all-reduce(bf16[11008]{0:T(1024)(128)(2,1)S(1)} %dynamic-update-slice), channel_id=2, replica_groups=mesh['fsdp'=8,'ctx'=4] {'fsdp'}, use_global_device_ids=true, to_apply=%add.9 | all-reduce | flops 11008 | bytes 44032
  73.4 10.5 %collective-permute-start.1 = (bf16[2,2,64,1024]{3,2,1,0:T(8,128)(2,1)S(1)}, bf16[2,2,64,1024]{3,2,1,0:T(8,128)(2,1)S(1)}, u32[]{:S(2)}, u32[]{:S(2)}) collective-permute-start(bf16[2,2,64,1024]{3,2,1,0:T(8,128)(2,1)S(1)} %maximum_select_fusion.9), channel_id=1, source_target_pairs={{0,1},{1,0},{2,3},{3,2},{4,5},{5,4},{6,7},{7,6},{8,9},{9,8},{10,11... | collective-permute-start | bytes 1572872 | tf_op jit(solution)/shard_map/ppermute | solution.py:41
  91.8 48.8 %all-gather.6.cloned.1.call-done = bf16[1024,1408]{1,0:T(8,128)(2,1)} async-done(((bf16[128,1408]{1,0:T(8,128)(2,1)}), bf16[1024,1408]{1,0:T(8,128)(2,1)}) %all-gather.6.cloned.1.call-update) | async-done | bytes 2883600 | tf_op jit(solution)/shard_map/all_gather | solution.py:293
  140.6 3.9 fusion.154
  157.0 7.2 %reduce-window.14 = f32[2,6,2,128]{3,2,1,0:T(2,128)} reduce-window(f32[2,6,2,128]{3,2,1,0:T(2,128)} %copy.538, f32[]{:T(128)} %constant.230.clone.1), window={size=1x1x1x128 pad=0_0x0_0x0_0x127_0}, to_apply=%region_3.4 | reduce-window | flops 390144 | bytes 24580 | tf_op jit(solution)/shard_map/reduce-window
  201.3 6.4 %collective-permute-done.4 = bf16[1,2,64,1024]{3,2,1,0:T(8,128)(2,1)} collective-permute-done((bf16[1,2,64,1024]{3,2,1,0:T(8,128)(2,1)S(1)}, bf16[1,2,64,1024]{3,2,1,0:T(8,128)(2,1)}, u32[]{:S(2)}, u32[]{:S(2)}) %collective-permute-start.4) | collective-permute-done | bytes 262176 | tf_op jit(solution)/shard_map/ppermute | solution.py:41
  241.6 4.9 collective-permute-done.12
  276.6 4.4 multiply_reduce_fusion.7
  283.4 3.7 multiply_reduce_fusion.8
  289.4 3.9 fusion.6
  293.5 3.6 reduce-window.16
  306.4 3.5 fusion.147
  311.9 3.5 concatenate.262
  315.5 5.6 %fusion.11 = (bf16[512,1024]{1,0:T(8,128)(2,1)S(1)}, f32[1024]{0:T(1024)S(1)}, f32[512,1024]{1,0:T(8,128)}) fusion(f32[2,4,64,1024]{3,2,1,0:T(8,128)S(1)} %copy-done.5, f32[1024]{0:T(1024)S(1)} %copy-done.60, f32[512]{0:T(512)S(1)} %copy-done.98, bf16[512,1408]{1,0:T(8,128)(2,1)} %concatenate.262, bf16[1024,1408]{1,0:T(8,128)(2,1)} %all-gather.6.cloned.1.call-done), kind=kOutput, calls=%fused_computation.17 | convolution fusion | flops 1479539712 | bytes 9578496 | tf_op jit(solution)/shard_map/dot_general | solution.py:36
  321.1 3.4 convolution_convert_fusion
  334.9 25.8 %all-reduce.10 = f32[8,1376]{1,0:T(8,128)S(1)} all-reduce(f32[8,1376]{1,0:T(8,128)S(1)} %concatenate.265), channel_id=4, replica_groups=mesh['fsdp'=8,'ctx'=4] {'fsdp'}, use_global_device_ids=true, to_apply=%region_23.24.clone | all-reduce | flops 11008 | bytes 88064
  361.4 12.2 %psum.14 = f32[1376]{0:T(1024)S(1)} all-reduce(f32[1376]{0:T(1024)S(1)} %dynamic-slice_reduce_fusion), channel_id=1, replica_groups=mesh['fsdp'=8,'ctx'=4] {'ctx'}, use_global_device_ids=true, to_apply=%region_24.25 | all-reduce | flops 1376 | bytes 11008 | tf_op jit(solution)/shard_map/psum | solution.py:443
  379.0 40.0 %psum.15 = f32[3,24]{1,0:T(4,128)S(1)} all-reduce(f32[3,24]{1,0:T(4,128)S(1)} %dynamic_update_slice.7), channel_id=1, replica_groups=mesh['fsdp'=8,'ctx'=4] {'fsdp','ctx'}, use_global_device_ids=true, to_apply=%region_34.35 | all-reduce | flops 72 | bytes 576 | tf_op jit(solution)/shard_map/psum | solution.py:444
  426.1 4.4 collective-permute-start.19
  433.2 10.9 %collective-permute-done.19 = bf16[128,1024]{1,0:T(8,128)(2,1)S(1)} collective-permute-done((bf16[128,1024]{1,0:T(8,128)(2,1)S(1)}, bf16[128,1024]{1,0:T(8,128)(2,1)S(1)}, u32[]{:S(2)}, u32[]{:S(2)}) %collective-permute-start.19) | collective-permute-done | bytes 262176 | tf_op jit(solution)/shard_map/ppermute | solution.py:89
  456.4 12.7 %reduce-scatter.4.cloned.1.call-done = bf16[128,1408]{1,0:T(8,128)(2,1)} async-done(((bf16[1024,1408]{1,0:T(8,128)(2,1)}), bf16[128,1408]{1,0:T(8,128)(2,1)}) %reduce-scatter.4.cloned.1.call-update) | async-done | bytes 360464 | tf_op jit(solution)/shard_map/reduce_scatter | solution.py:403
  471.7 6.3 %collective-permute-done.17 = bf16[1,128,1408]{2,1,0:T(8,128)(2,1)S(1)} collective-permute-done((bf16[1,128,1408]{2,1,0:T(8,128)(2,1)}, bf16[1,128,1408]{2,1,0:T(8,128)(2,1)S(1)}, u32[]{:S(2)}, u32[]{:S(2)}) %collective-permute-start.17) | collective-permute-done | bytes 360480 | tf_op jit(solution)/shard_map/ppermute | solution.py:41
  (535 shorter events, 208.3 us)
Async XLA Ops:
  7.2 80.8 %all-gather.10.cloned.1.call-start = ((), (), s32[]{:S(2)}) async-start(), calls=%async_computation.8 | async-start | bytes 2359296 | tf_op jit(solution)/shard_map/all_gather | solution.py:294
  10.0 22.0 %collective-permute-start.2 = (bf16[128,1024]{1,0:T(8,128)(2,1)S(1)}, bf16[128,1024]{1,0:T(8,128)(2,1)S(1)}, u32[]{:S(2)}, u32[]{:S(2)}) collective-permute-start(bf16[128,1024]{1,0:T(8,128)(2,1)S(1)} %pad_maximum_fusion.5), channel_id=1, source_target_pairs={{0,0},{1,4},{2,8},{3,12},{4,16},{5,20},{6,24},{7,28},{8,1},{9,5},{... | collective-permute-start | bytes 786440 | tf_op jit(solution)/shard_map/ppermute | solution.py:89
  32.7 108.0 %all-gather.6.cloned.1.call-start = ((), (), s32[]{:S(2)}) async-start(), calls=%async_computation.3 | async-start | bytes 3244032 | tf_op jit(solution)/shard_map/all_gather | solution.py:293
  37.1 187.7 %all-gather.8.cloned.1.call-start = ((), (), s32[]{:S(2)}) async-start(), calls=%async_computation.4 | async-start | bytes 2359296 | tf_op jit(solution)/shard_map/all_gather | solution.py:295
  37.2 36.2 %collective-permute-start = (bf16[1,2,64,1024]{3,2,1,0:T(8,128)(2,1)S(1)}, bf16[1,2,64,1024]{3,2,1,0:T(8,128)(2,1)S(1)}, u32[]{:S(2)}, u32[]{:S(2)}) collective-permute-start(bf16[1,2,64,1024]{3,2,1,0:T(8,128)(2,1)S(1)} %bitcast.519), channel_id=1, source_target_pairs={{0,2},{1,3},{2,0},{3,1},{4,6},{5,7},{6,4},{7,5},{8,10},{9,11},{10,... | collective-permute-start | bytes 786440 | tf_op jit(solution)/shard_map/ppermute | solution.py:41
  39.0 385.1 %reduce-scatter.8.cloned.1.call-start = ((), (), s32[]{:S(2)}) async-start(), calls=%async_computation.7 | async-start | bytes 3538944 | tf_op jit(solution)/shard_map/reduce_scatter | solution.py:400
  73.4 12.1 %collective-permute-start.1 = (bf16[2,2,64,1024]{3,2,1,0:T(8,128)(2,1)S(1)}, bf16[2,2,64,1024]{3,2,1,0:T(8,128)(2,1)S(1)}, u32[]{:S(2)}, u32[]{:S(2)}) collective-permute-start(bf16[2,2,64,1024]{3,2,1,0:T(8,128)(2,1)S(1)} %maximum_select_fusion.9), channel_id=1, source_target_pairs={{0,1},{1,0},{2,3},{3,2},{4,5},{5,4},{6,7},{7,6},{8,9},{9,8},{10,11... | collective-permute-start | bytes 1572872 | tf_op jit(solution)/shard_map/ppermute | solution.py:41
  199.8 7.9 %collective-permute-start.4 = (bf16[1,2,64,1024]{3,2,1,0:T(8,128)(2,1)S(1)}, bf16[1,2,64,1024]{3,2,1,0:T(8,128)(2,1)}, u32[]{:S(2)}, u32[]{:S(2)}) collective-permute-start(bf16[1,2,64,1024]{3,2,1,0:T(8,128)(2,1)S(1)} %dynamic-slice_convert_fusion.3), channel_id=1, source_target_pairs={{0,2},{1,3},{2,0},{3,1},{4,6},{5,7},{6,4},{7,5},{8,10},{9,11},{10,... | collective-permute-start | bytes 786440 | tf_op jit(solution)/shard_map/ppermute | solution.py:41
  201.0 12.3 %collective-permute-start.9 = (bf16[1,2,64,1024]{3,2,1,0:T(8,128)(2,1)S(1)}, bf16[1,2,64,1024]{3,2,1,0:T(8,128)(2,1)}, u32[]{:S(2)}, u32[]{:S(2)}) collective-permute-start(bf16[1,2,64,1024]{3,2,1,0:T(8,128)(2,1)S(1)} %bitcast.564), channel_id=1, source_target_pairs={{0,2},{1,3},{2,0},{3,1},{4,6},{5,7},{6,4},{7,5},{8,10},{9,11},{10,... | collective-permute-start | bytes 786440 | tf_op jit(solution)/shard_map/ppermute | solution.py:41
  209.5 9.3 %collective-permute-start.5 = (bf16[1,2,64,1024]{3,2,1,0:T(8,128)(2,1)S(1)}, bf16[1,2,64,1024]{3,2,1,0:T(8,128)(2,1)S(1)}, u32[]{:S(2)}, u32[]{:S(2)}) collective-permute-start(bf16[1,2,64,1024]{3,2,1,0:T(8,128)(2,1)S(1)} %multiply_convert_fusion.6), channel_id=1, source_target_pairs={{0,2},{1,3},{2,0},{3,1},{4,6},{5,7},{6,4},{7,5},{8,10},{9,11},{10,... | collective-permute-start | bytes 786440 | tf_op jit(solution)/shard_map/ppermute | solution.py:41
  214.4 6.6 %collective-permute-start.10 = (bf16[2,2,64,1024]{3,2,1,0:T(8,128)(2,1)S(1)}, bf16[2,2,64,1024]{3,2,1,0:T(8,128)(2,1)S(1)}, u32[]{:S(2)}, u32[]{:S(2)}) collective-permute-start(bf16[2,2,64,1024]{3,2,1,0:T(8,128)(2,1)S(1)} %maximum_select_fusion.12), channel_id=1, source_target_pairs={{0,1},{1,0},{2,3},{3,2},{4,5},{5,4},{6,7},{7,6},{8,9},{9,8},{10,11... | collective-permute-start | bytes 1572872 | tf_op jit(solution)/shard_map/ppermute | solution.py:41
  239.1 7.5 %collective-permute-start.12 = (bf16[1,2,64,1024]{3,2,1,0:T(8,128)(2,1)S(1)}, bf16[1,2,64,1024]{3,2,1,0:T(8,128)(2,1)S(1)}, u32[]{:S(2)}, u32[]{:S(2)}) collective-permute-start(bf16[1,2,64,1024]{3,2,1,0:T(8,128)(2,1)S(1)} %dynamic-slice_convert_fusion.1), channel_id=1, source_target_pairs={{0,2},{1,3},{2,0},{3,1},{4,6},{5,7},{6,4},{7,5},{8,10},{9,11},{10,... | collective-permute-start | bytes 786440 | tf_op jit(solution)/shard_map/ppermute | solution.py:41
  251.6 173.5 %reduce-scatter.6.cloned.1.call-start = ((), (), s32[]{:S(2)}) async-start(), calls=%async_computation.6 | async-start | bytes 1179648 | tf_op jit(solution)/shard_map/reduce_scatter | solution.py:402
  306.3 162.7 %reduce-scatter.4.cloned.1.call-start = ((), (), s32[]{:S(2)}) async-start(), calls=%async_computation.5 | async-start | bytes 3244032 | tf_op jit(solution)/shard_map/reduce_scatter | solution.py:403
  332.7 112.7 %collective-permute-start.8 = (bf16[1,2,64,1024]{3,2,1,0:T(8,128)(2,1)}, bf16[1,2,64,1024]{3,2,1,0:T(8,128)(2,1)}, u32[]{:S(2)}, u32[]{:S(2)}) collective-permute-start(bf16[1,2,64,1024]{3,2,1,0:T(8,128)(2,1)} %dynamic-slice_convert_fusion.2), channel_id=1, source_target_pairs={{0,2},{1,3},{2,0},{3,1},{4,6},{5,7},{6,4},{7,5},{8,10},{9,11},{10,... | collective-permute-start | bytes 786440 | tf_op jit(solution)/shard_map/ppermute | solution.py:41
  375.5 44.7 %collective-permute-start.15 = (bf16[2,2,64,1024]{3,2,1,0:T(8,128)(2,1)S(1)}, bf16[2,2,64,1024]{3,2,1,0:T(8,128)(2,1)}, u32[]{:S(2)}, u32[]{:S(2)}) collective-permute-start(bf16[2,2,64,1024]{3,2,1,0:T(8,128)(2,1)S(1)} %fusion.79), channel_id=1, source_target_pairs={{0,1},{1,0},{2,3},{3,2},{4,5},{5,4},{6,7},{7,6},{8,9},{9,8},{10,11... | collective-permute-start | bytes 1572872 | tf_op jit(solution)/shard_map/ppermute | solution.py:41
  422.5 9.5 %collective-permute-start.16 = (bf16[1,2,64,1024]{3,2,1,0:T(8,128)(2,1)}, bf16[1,2,64,1024]{3,2,1,0:T(8,128)(2,1)}, u32[]{:S(2)}, u32[]{:S(2)}) collective-permute-start(bf16[1,2,64,1024]{3,2,1,0:T(8,128)(2,1)} %dynamic-slice_convert_fusion), channel_id=1, source_target_pairs={{0,2},{1,3},{2,0},{3,1},{4,6},{5,7},{6,4},{7,5},{8,10},{9,11},{10,... | collective-permute-start | bytes 786440 | tf_op jit(solution)/shard_map/ppermute | solution.py:41
  426.1 17.9 %collective-permute-start.19 = (bf16[128,1024]{1,0:T(8,128)(2,1)S(1)}, bf16[128,1024]{1,0:T(8,128)(2,1)S(1)}, u32[]{:S(2)}, u32[]{:S(2)}) collective-permute-start(bf16[128,1024]{1,0:T(8,128)(2,1)S(1)} %pad_maximum_fusion.7), channel_id=1, source_target_pairs={{0,0},{4,1},{8,2},{12,3},{16,4},{20,5},{24,6},{28,7},{1,8},{5,9},{... | collective-permute-start | bytes 786440 | tf_op jit(solution)/shard_map/ppermute | solution.py:89
  431.5 12.5 %collective-permute-start.22 = (bf16[1,128,1024]{2,1,0:T(8,128)(2,1)S(1)}, bf16[1,128,1024]{2,1,0:T(8,128)(2,1)S(1)}, u32[]{:S(2)}, u32[]{:S(2)}) collective-permute-start(bf16[1,128,1024]{2,1,0:T(8,128)(2,1)S(1)} %get-tuple-element.193), channel_id=1, source_target_pairs={{0,2},{1,3},{2,0},{3,1},{4,6},{5,7},{6,4},{7,5},{8,10},{9,11},{10,... | collective-permute-start | bytes 786440 | tf_op jit(solution)/shard_map/ppermute | solution.py:41
  444.1 6.6 %collective-permute-start.20 = (bf16[1,128,1024]{2,1,0:T(8,128)(2,1)S(1)}, bf16[1,128,1024]{2,1,0:T(8,128)(2,1)S(1)}, u32[]{:S(2)}, u32[]{:S(2)}) collective-permute-start(bf16[1,128,1024]{2,1,0:T(8,128)(2,1)S(1)} %bitcast.600), channel_id=1, source_target_pairs={{0,2},{1,3},{2,0},{3,1},{4,6},{5,7},{6,4},{7,5},{8,10},{9,11},{10,... | collective-permute-start | bytes 786440 | tf_op jit(solution)/shard_map/ppermute | solution.py:41
  444.1 8.9 %collective-permute-start.23 = (bf16[2,128,1024]{2,1,0:T(8,128)(2,1)S(1)}, bf16[2,128,1024]{2,1,0:T(8,128)(2,1)S(1)}, u32[]{:S(2)}, u32[]{:S(2)}) collective-permute-start(bf16[2,128,1024]{2,1,0:T(8,128)(2,1)S(1)} %maximum_select_fusion.17), channel_id=1, source_target_pairs={{0,1},{1,0},{2,3},{3,2},{4,5},{5,4},{6,7},{7,6},{8,9},{9,8},{10,11... | collective-permute-start | bytes 1572872 | tf_op jit(solution)/shard_map/ppermute | solution.py:41
  450.8 32.1 %collective-permute-start.21 = (bf16[2,128,1024]{2,1,0:T(8,128)(2,1)S(1)}, bf16[2,128,1024]{2,1,0:T(8,128)(2,1)}, u32[]{:S(2)}, u32[]{:S(2)}) collective-permute-start(bf16[2,128,1024]{2,1,0:T(8,128)(2,1)S(1)} %maximum_select_fusion.16), channel_id=1, source_target_pairs={{0,1},{1,0},{2,3},{3,2},{4,5},{5,4},{6,7},{7,6},{8,9},{9,8},{10,11... | collective-permute-start | bytes 1572872 | tf_op jit(solution)/shard_map/ppermute | solution.py:41
  469.0 9.0 %collective-permute-start.17 = (bf16[1,128,1408]{2,1,0:T(8,128)(2,1)}, bf16[1,128,1408]{2,1,0:T(8,128)(2,1)S(1)}, u32[]{:S(2)}, u32[]{:S(2)}) collective-permute-start(bf16[1,128,1408]{2,1,0:T(8,128)(2,1)} %bitcast.589), channel_id=1, source_target_pairs={{0,2},{1,3},{2,0},{3,1},{4,6},{5,7},{6,4},{7,5},{8,10},{9,11},{10,... | collective-permute-start | bytes 1081352 | tf_op jit(solution)/shard_map/ppermute | solution.py:41
  479.2 8.1 %collective-permute-start.18 = (bf16[2,128,1408]{2,1,0:T(8,128)(2,1)S(1)}, bf16[2,128,1408]{2,1,0:T(8,128)(2,1)S(1)}, u32[]{:S(2)}, u32[]{:S(2)}) collective-permute-start(bf16[2,128,1408]{2,1,0:T(8,128)(2,1)S(1)} %maximum_select_fusion.8), channel_id=1, source_target_pairs={{0,1},{1,0},{2,3},{3,2},{4,5},{5,4},{6,7},{7,6},{8,9},{9,8},{10,11... | collective-permute-start | bytes 2162696 | tf_op jit(solution)/shard_map/ppermute | solution.py:41
  (120 other events, 1232.8 us)
Sparse Core Ops, SparseCore 0:
  32.8 49.0 all-gather.9
  84.7 55.8 all-gather.5
  142.8 48.0 all-gather.7
  251.7 73.5 reduce-scatter.7
  328.6 60.8 reduce-scatter.5
  393.3 75.6 reduce-scatter.3

commit v2 on v1

v2 whole, which is shorter than its diff:
```python
import math

import jax
import jax.numpy as jnp
from jax import lax
from jax.experimental import pallas as pl
from jax.experimental.pallas import tpu as pltpu
from jax.sharding import PartitionSpec as P

HEADS = 8
KV = 2
HD = 64
MH = 24
MP = 64
NS = 128
CONV = 4
FF = 2048
QW = 512
KW = 128
DI = 1536
XC = 1792

epsilon = 1e-05
rope_base = 100000000000.0
f32 = jnp.float32
bf16 = jnp.bfloat16


def dot_plain(left, right):
    return jnp.dot(left, right, preferred_element_type=f32)


def dot_first(left, right):
    return lax.dot_general(left, right, (((0,), (0,)), ((), ())), preferred_element_type=f32)


def dot_last(left, right):
    return lax.dot_general(left, right, (((1,), (1,)), ((), ())), preferred_element_type=f32)


def swap(block, axis, bit):
    devices = range(lax.axis_size(axis))
    return lax.ppermute(block, axis, [(i, i ^ bit) for i in devices])


def pair_gather(block, axis):
    size = lax.axis_size(axis)
    place = lax.axis_index(axis)
    out = block[None]
    bit = size // 2
    while bit:
        other = swap(out, axis, bit)
        low = (place // bit) % 2 == 0
        out = jnp.where(low, jnp.stack([out, other], 1), jnp.stack([other, out], 1))
        out = out.reshape((-1,) + block.shape)
        bit //= 2
    return out


def ctx_gather(block):
    return pair_gather(block, "ctx")


def line_groups():
    half = lax.axis_size("fsdp") // 2
    return [[2 * k + x for k in range(half)] for x in range(2)]


def line_gather(shard):
    return lax.all_gather(shard, "fsdp", axis=0, tiled=False, axis_index_groups=line_groups())


def join_pairs(column):
    first = lax.axis_index("fsdp") % 2 == 0
    other = swap(column, "fsdp", 1)
    both = jnp.where(first, jnp.stack([column, other], 1), jnp.stack([other, column], 1))
    return both.reshape((-1,) + column.shape[1:])


def fsdp_scatter(parts):
    column = lax.psum_scatter(
        parts.reshape((-1, 2) + parts.shape[1:]).astype(bf16),
        "fsdp",
        scatter_dimension=0,
        tiled=False,
        axis_index_groups=line_groups(),
    )
    mine = lax.axis_index("fsdp") % 2
    keep = lax.dynamic_index_in_dim(column, mine, 0, False)
    send = lax.dynamic_index_in_dim(column, 1 - mine, 0, False)
    return keep.astype(f32) + swap(send, "fsdp", 1).astype(f32)


def ctx_scatter(parts):
    size = lax.axis_size("ctx")
    place = lax.axis_index("ctx")
    bit = 1
    while bit < size:
        mine = (place // bit) % 2
        parts = parts.reshape((-1, 2) + parts.shape[1:])
        keep = lax.dynamic_index_in_dim(parts, mine, 1, False)
        send = lax.dynamic_index_in_dim(parts, 1 - mine, 1, False)
        got = swap(send.astype(bf16), "ctx", bit)
        parts = keep.astype(f32) + got.astype(f32)
        bit *= 2
    return parts[0]


def everywhere_sum(value):
    for axis in ("ctx", "fsdp"):
        bit = 1
        while bit < lax.axis_size(axis):
            value = value + swap(value, axis, bit)
            bit *= 2
    return value


def to_owner_columns(rows, back):
    F, C = lax.axis_size("fsdp"), lax.axis_size("ctx")
    route = []
    for f in range(F):
        for c in range(C):
            pair = (f * C + c, ((f % (F // C)) * C + c) * C + f // (F // C))
            route.append(pair[::-1] if back else pair)
    return lax.ppermute(rows, ("fsdp", "ctx"), route)


def rotary_tables(positions):
    half_width = HD // 2
    exponents = jnp.arange(half_width, dtype=f32) * (2.0 / HD)
    inverse = jnp.exp(-exponents * math.log(rope_base))
    angles = positions[:, None] * inverse[None, :]
    cosine = jnp.concatenate([jnp.cos(angles), jnp.cos(angles)], axis=1)
    sine = jnp.concatenate([jnp.sin(angles), jnp.sin(angles)], axis=1)
    return (cosine, sine)


def mixer_tables(segments, conv_own, dt_bias, a_rate, skip):
    micro, length = segments.shape
    cosine, sine = rotary_tables(jnp.arange(length).astype(f32))
    columns = []
    for distance in range(CONV):
        behind = jnp.pad(segments, ((0, 0), (distance, 0)), constant_values=-1)[:, :length]
        columns.append((behind == segments).astype(f32))
    columns.append(segments.astype(f32))
    col = jnp.pad(jnp.stack(columns, axis=2), ((0, 0), (0, 0), (0, 128 - len(columns))))
    row = jnp.broadcast_to(segments.astype(f32)[:, None, :], (micro, 8, length))
    conv = jnp.pad(conv_own, ((0, 8 - conv_own.shape[0]), (0, 0)))
    heads = dt_bias.shape[0]
    head = jnp.pad(jnp.stack([dt_bias, a_rate]), ((0, 6), (0, 128 - heads)))
    skip = jnp.broadcast_to(skip[:, None], (heads, MP)).reshape(1, heads * MP)
    double = lambda table: jnp.concatenate([table, table], axis=1)
    return col, row, double(cosine), double(sine), conv, head, skip


def lane_index(shape):
    return lax.broadcasted_iota(jnp.int32, shape, 1)


def turn(tile, forward):
    up = pltpu.roll(tile, 128 - HD // 2, 1)
    down = pltpu.roll(tile, HD // 2, 1)
    low = lane_index(tile.shape) % HD < HD // 2
    return jnp.where(low, -up, down) if forward else jnp.where(low, up, -down)


def half_select(first, second):
    return jnp.where(lane_index(first.shape) < HD, first, second)


def half_only(tile, which):
    low = lane_index(tile.shape) < HD
    return jnp.where(low if which == 0 else jnp.logical_not(low), tile, jnp.zeros_like(tile))


def allowed_pairs(col, row):
    length = col.shape[0]
    order_t = lax.broadcasted_iota(jnp.int32, (length, length), 0)
    order_s = lax.broadcasted_iota(jnp.int32, (length, length), 1)
    return (order_s <= order_t) & (col[:, CONV : CONV + 1] == row[0:1, :])


def mixer_state(conv_f, dt_raw, col, conv, head):
    length = conv_f.shape[0]
    behind = [col[:, 0:1] * conv_f]
    for k in range(1, CONV):
        behind.append(col[:, k : k + 1] * pltpu.roll(conv_f, k, 0))
    pre = conv[CONV : CONV + 1, :]
    for k in range(CONV):
        pre = pre + behind[k] * conv[CONV - 1 - k : CONV - k, :]
    step_pre = dt_raw + head[0:1, :]
    step = jnp.maximum(step_pre, 0.0) + jnp.log1p(jnp.exp(-jnp.abs(step_pre)))
    decay_log = -step * head[1:2, :]
    order_t = lax.broadcasted_iota(jnp.int32, (length, length), 0)
    order_s = lax.broadcasted_iota(jnp.int32, (length, length), 1)
    lower = (order_s <= order_t).astype(f32)
    cum = jnp.dot(lower, decay_log, precision=lax.Precision.HIGHEST, preferred_element_type=f32)
    return behind, pre, step_pre, step, decay_log, cum


def decay_kernel(cum, cum_t, valid, h):
    return jnp.exp(jnp.where(valid, cum[:, h : h + 1] - cum_t[h : h + 1, :], -1e30))


def softmax_rows(queries, keys, valid, scale):
    scores = jnp.where(valid, dot_last(queries, keys) * scale, -1e30)
    peak = jnp.max(scores, axis=-1, keepdims=True)
    expo = jnp.exp(scores - peak)
    return expo / jnp.sum(expo, axis=-1, keepdims=True)


def forward_body(
    hidden_ref,
    gain_ref,
    w_ref,
    col_ref,
    row_ref,
    cos_ref,
    sin_ref,
    conv_ref,
    head_ref,
    skip_ref,
    normed_ref,
    qkv_ref,
    gate_ref,
    conv_in_ref,
    dt_ref,
    y_ref,
    mixed_ref,
):
    scale = 1.0 / math.sqrt(HD)
    dw = gate_ref.shape[1]
    heads = dw // MP
    hidden = hidden_ref[...].astype(f32)
    inv_rms = lax.rsqrt(jnp.mean(hidden * hidden, axis=-1, keepdims=True) + epsilon)
    normed = (hidden * inv_rms * gain_ref[...]).astype(bf16)
    normed_ref[...] = normed
    first = dot_plain(normed, w_ref[...])
    col, row = col_ref[0], row_ref[0]
    valid = allowed_pairs(col, row)
    cos, sin = cos_ref[...], sin_ref[...]
    q = first[:, :128]
    q = (q * cos + turn(q, True) * sin).astype(bf16)
    kv = first[:, 128:256]
    kv = half_select(kv * cos + turn(kv, True) * sin, kv)
    qkv_ref[:, :128] = q
    qkv_ref[:, 128:] = kv.astype(bf16)
    kv_turned = pltpu.roll(kv, HD, 1)
    keys = half_select(kv, kv_turned).astype(bf16)
    values = half_select(kv_turned, kv).astype(bf16)
    outs = []
    for h in range(2):
        probability = softmax_rows(half_only(q, h), keys, valid, scale)
        outs.append(dot_plain(probability.astype(bf16), values))
    mixed_ref[:, :128] = half_select(outs[0], outs[1]).astype(bf16)

    gate_z = first[:, 256 : 256 + dw]
    gate_ref[...] = gate_z
    conv_in = first[:, 256 + dw : 256 + 2 * dw + 2 * NS].astype(bf16)
    conv_in_ref[...] = conv_in
    dt_raw = first[:, 256 + 2 * dw + 2 * NS :]
    dt_ref[...] = dt_raw
    _, pre, _, step, _, cum = mixer_state(conv_in.astype(f32), dt_raw, col, conv_ref[...], head_ref[...])
    act = pre * jax.nn.sigmoid(pre)
    cum_t = jnp.transpose(cum)
    b_map = act[:, dw : dw + NS].astype(bf16)
    c_map = act[:, dw + NS :].astype(bf16)
    cross = dot_last(c_map, b_map)
    for j in range(heads // 2):
        x = act[:, 128 * j : 128 * (j + 1)]
        driven = (x * half_select_col(step, 2 * j, x.shape)).astype(bf16)
        pair = []
        for h in (2 * j, 2 * j + 1):
            weighted = decay_kernel(cum, cum_t, valid, h) * cross
            pair.append(dot_plain(weighted.astype(bf16), driven))
        y = half_select(pair[0], pair[1]) + skip_ref[:, 128 * j : 128 * (j + 1)] * x
        y_ref[:, 128 * j : 128 * (j + 1)] = y
        z = gate_z[:, 128 * j : 128 * (j + 1)]
        mixed_ref[:, 128 * (j + 1) : 128 * (j + 2)] = (y * z * jax.nn.sigmoid(z)).astype(bf16)


def half_select_col(columns, h, shape):
    return jnp.where(lane_index(shape) < MP, columns[:, h : h + 1], columns[:, h + 1 : h + 2])


def backward_body(
    d_mid_ref,
    hidden_ref,
    w_ref,
    w_mix_ref,
    col_ref,
    row_ref,
    cos_ref,
    sin_ref,
    conv_ref,
    head_ref,
    skip_ref,
    normed_ref,
    qkv_ref,
    gate_ref,
    conv_in_ref,
    dt_ref,
    y_ref,
    mixed_ref,
    d_normed_ref,
    g_first_ref,
    g_mix_ref,
    g_gain_ref,
    g_conv_ref,
    g_head_ref,
    g_skip_ref,
    acc_first,
    acc_mix,
    d_first,
):
    scale = 1.0 / math.sqrt(HD)
    dw = gate_ref.shape[1]
    heads = dw // MP
    at_conv = 256 + dw
    at_dt = at_conv + dw + 2 * NS
    first_step = pl.program_id(0) == 0

    @pl.when(first_step)
    def _():
        acc_first[...] = jnp.zeros_like(acc_first)
        acc_mix[...] = jnp.zeros_like(acc_mix)
        g_gain_ref[...] = jnp.zeros_like(g_gain_ref)
        g_conv_ref[...] = jnp.zeros_like(g_conv_ref)
        g_head_ref[...] = jnp.zeros_like(g_head_ref)
        g_skip_ref[...] = jnp.zeros_like(g_skip_ref)

    col, row = col_ref[0], row_ref[0]
    valid = allowed_pairs(col, row)
    length = col.shape[0]
    d_mid = d_mid_ref[...]
    acc_mix[...] += dot_first(mixed_ref[...], d_mid)
    d_mixed = dot_last(d_mid, w_mix_ref[...]).astype(bf16)

    cos, sin = cos_ref[...], sin_ref[...]
    q = qkv_ref[:, :128]
    kv = qkv_ref[:, 128:].astype(f32)
    kv_turned = pltpu.roll(kv, HD, 1)
    keys = half_select(kv, kv_turned).astype(bf16)
    values = half_select(kv_turned, kv).astype(bf16)
    d_att = d_mixed[:, :128]
    d_q, d_k, d_v = [], 0.0, 0.0
    for h in range(2):
        q_h = half_only(q, h)
        d_att_h = half_only(d_att, h)
        probability = softmax_rows(q_h, keys, valid, scale)
        d_prob = dot_last(d_att_h, values)
        delta = jnp.sum(probability * d_prob, axis=-1, keepdims=True)
        d_scores = (probability * (d_prob - delta)).astype(bf16)
        d_q.append(dot_plain(d_scores, keys))
        d_k = d_k + dot_first(d_scores, q_h)
        d_v = d_v + dot_first(probability.astype(bf16), d_att_h)
    d_q = half_select(d_q[0], d_q[1]) * scale
    d_k = (d_k + pltpu.roll(d_k, HD, 1)) * scale
    d_v = d_v + pltpu.roll(d_v, HD, 1)
    d_first[:, :128] = (d_q * cos + turn(d_q * sin, False)).astype(bf16)
    d_first[:, 128:256] = half_select(d_k * cos + turn(d_k * sin, False), d_v).astype(bf16)

    conv = conv_ref[...]
    behind, pre, step_pre, step, decay_log, cum = mixer_state(
        conv_in_ref[...].astype(f32), dt_ref[...], col, conv, head_ref[...]
    )
    sig = jax.nn.sigmoid(pre)
    act = pre * sig
    slope = sig * (1.0 + pre * (1.0 - sig))
    cum_t = jnp.transpose(cum)
    b_map = act[:, dw : dw + NS].astype(bf16)
    c_map = act[:, dw + NS :].astype(bf16)
    cross = dot_last(c_map, b_map)
    d_cross = jnp.zeros((length, length), f32)
    lanes = lane_index((length, 128))
    row_sums = jnp.zeros((length, 128), f32)
    x_sums = jnp.zeros((length, 128), f32)
    col_sums = []
    d_x_parts = []
    for j in range(heads // 2):
        part = slice(128 * j, 128 * (j + 1))
        z = gate_ref[:, part]
        z_sig = jax.nn.sigmoid(z)
        d_gated = d_mixed[:, 128 * (j + 1) : 128 * (j + 2)].astype(f32)
        d_first[:, 256 + 128 * j : 256 + 128 * (j + 1)] = (
            d_gated * y_ref[:, part] * (z_sig * (1.0 + z * (1.0 - z_sig)))
        ).astype(bf16)
        d_y = d_gated * (z * z_sig)
        d_y16 = d_y.astype(bf16)
        x = act[:, part]
        step_x = half_select_col(step, 2 * j, x.shape)
        driven = (x * step_x).astype(bf16)
        pair = []
        for h in (2 * j, 2 * j + 1):
            kernel = decay_kernel(cum, cum_t, valid, h)
            weighted = kernel * cross
            d_weighted = dot_last(half_only(d_y16, h - 2 * j), driven)
            d_cross = d_cross + d_weighted * kernel
            pairs = d_weighted * weighted
            row_sums = jnp.where(lanes == h, jnp.sum(pairs, axis=1, keepdims=True), row_sums)
            col_sums.append(jnp.sum(pairs, axis=0, keepdims=True))
            pair.append(dot_first(weighted.astype(bf16), d_y16))
        d_driven = half_select(pair[0], pair[1])
        d_x_parts.append(d_driven * step_x + skip_ref[:, part] * d_y)
        dx = d_driven * x
        for h in (2 * j, 2 * j + 1):
            x_sums = jnp.where(
                lanes == h, jnp.sum(half_only(dx, h - 2 * j), axis=1, keepdims=True), x_sums
            )
        g_skip_ref[:, part] += jnp.sum(d_y * x, axis=0, keepdims=True)
    col_sums = jnp.concatenate(col_sums + [jnp.zeros((128 - heads, length), f32)], axis=0)
    d_cum = row_sums - jnp.transpose(col_sums)
    order_t = lax.broadcasted_iota(jnp.int32, (length, length), 0)
    order_s = lax.broadcasted_iota(jnp.int32, (length, length), 1)
    upper = (order_s >= order_t).astype(f32)
    d_decay = jnp.dot(upper, d_cum, precision=lax.Precision.HIGHEST, preferred_element_type=f32)
    d_dt = (x_sums - d_decay * head_ref[1:2, :]) * jax.nn.sigmoid(step_pre)
    d_first[:, at_dt:] = d_dt.astype(bf16)
    g_head_ref[0:1, :] += jnp.sum(d_dt, axis=0, keepdims=True)
    g_head_ref[1:2, :] += jnp.sum(d_decay * decay_log, axis=0, keepdims=True)
    d_cross16 = d_cross.astype(bf16)
    d_act = d_x_parts + [dot_first(d_cross16, c_map), dot_plain(d_cross16, b_map)]
    for i, piece in enumerate(d_act):
        part = slice(128 * i, 128 * (i + 1))
        d_pre = piece * slope[:, part]
        g_conv_ref[CONV : CONV + 1, part] += jnp.sum(d_pre, axis=0, keepdims=True)
        d_conv = 0.0
        for k in range(CONV):
            tap = CONV - 1 - k
            g_conv_ref[tap : tap + 1, part] += jnp.sum(d_pre * behind[k][:, part], axis=0, keepdims=True)
            moved = col[:, k : k + 1] * d_pre
            if k:
                moved = pltpu.roll(moved, length - k, 0)
            d_conv = d_conv + moved * conv[tap : tap + 1, part]
        d_first[:, at_conv + 128 * i : at_conv + 128 * (i + 1)] = d_conv.astype(bf16)

    d_all = d_first[...]
    d_normed = dot_last(d_all, w_ref[...])
    d_normed_ref[...] = d_normed
    hidden = hidden_ref[...].astype(f32)
    inv_rms = lax.rsqrt(jnp.mean(hidden * hidden, axis=-1, keepdims=True) + epsilon)
    g_gain_ref[...] += jnp.sum(d_normed * (hidden * inv_rms), axis=0, keepdims=True)
    acc_first[...] += dot_first(normed_ref[...], d_all)

    @pl.when(pl.program_id(0) == pl.num_programs(0) - 1)
    def _():
        g_first_ref[...] = acc_first[...].astype(bf16)
        g_mix_ref[...] = acc_mix[...].astype(bf16)


def ffn_body(x_ref, cot_ref, gu_ref, down_ref, d_second_ref, out_ref, g_gu_ref, g_down_ref, acc_gu, acc_down):
    fw = down_ref.shape[0]

    @pl.when(pl.program_id(0) == 0)
    def _():
        acc_gu[...] = jnp.zeros_like(acc_gu)
        acc_down[...] = jnp.zeros_like(acc_down)

    x, cot = x_ref[...], cot_ref[...]
    gate_up = dot_plain(x, gu_ref[...])
    gate, up = gate_up[:, :fw], gate_up[:, fw:]
    sig = jax.nn.sigmoid(gate)
    gate_silu = gate * sig
    d_units = dot_last(cot, down_ref[...]).astype(bf16).astype(f32)
    d_gate = (d_units * up * (sig * (1.0 + gate * (1.0 - sig)))).astype(bf16)
    d_up = (d_units * gate_silu).astype(bf16)
    d_second_ref[...] = dot_last(d_gate, gu_ref[:, :fw]) + dot_last(d_up, gu_ref[:, fw:])
    units = (gate_silu * up).astype(bf16)
    out_ref[...] = dot_plain(units, down_ref[...])
    acc_gu[:, :fw] += dot_first(x, d_gate)
    acc_gu[:, fw:] += dot_first(x, d_up)
    acc_down[...] += dot_first(units, cot)

    @pl.when(pl.program_id(0) == pl.num_programs(0) - 1)
    def _():
        g_gu_ref[...] = acc_gu[...].astype(bf16)
        g_down_ref[...] = acc_down[...].astype(bf16)


def per_pack(block_rows, width):
    return pl.BlockSpec((block_rows, width), lambda m: (m, 0))


def per_pack3(rows, width):
    return pl.BlockSpec((1, rows, width), lambda m: (m, 0, 0))


def whole(shape):
    return pl.BlockSpec(shape, lambda m: (0,) * len(shape))


def struct(shape, kind):
    return jax.ShapeDtypeStruct(shape, kind)


params = pltpu.CompilerParams(
    dimension_semantics=("arbitrary",), vmem_limit_bytes=56 * 1024 * 1024
)


def mixer_forward(hidden, gain, w_first, tables, micro):
    rows, D = hidden.shape
    length = rows // micro
    col, row, cos, sin, conv, head, skip = tables
    dw, width = skip.shape[1], w_first.shape[1]
    cw = conv.shape[1]
    shapes = [(D, bf16), (256, bf16), (dw, f32), (cw, bf16), (128, f32), (dw, f32), (128 + dw, bf16)]
    return pl.pallas_call(
        forward_body,
        grid=(micro,),
        in_specs=[
            per_pack(length, D),
            whole(gain.shape),
            whole(w_first.shape),
            per_pack3(length, 128),
            per_pack3(8, length),
            whole(cos.shape),
            whole(sin.shape),
            whole(conv.shape),
            whole(head.shape),
            whole(skip.shape),
        ],
        out_specs=[per_pack(length, n) for n, _ in shapes],
        out_shape=[struct((rows, n), kind) for n, kind in shapes],
        compiler_params=params,
        name="mixer_forward",
    )(hidden, gain, w_first, col, row, cos, sin, conv, head, skip)


def mixer_backward(d_middle, hidden, w_first, w_mix, tables, saved, micro):
    rows, D = hidden.shape
    length = rows // micro
    col, row, cos, sin, conv, head, skip = tables
    width = w_first.shape[1]
    flat = [whole(a.shape) for a in (cos, sin, conv, head, skip)]
    sums = [w_first.shape, w_mix.shape, (1, D), conv.shape, head.shape, skip.shape]
    kinds = [bf16, bf16, f32, f32, f32, f32]
    return pl.pallas_call(
        backward_body,
        grid=(micro,),
        in_specs=[
            per_pack(length, D),
            per_pack(length, D),
            whole(w_first.shape),
            whole(w_mix.shape),
            per_pack3(length, 128),
            per_pack3(8, length),
        ]
        + flat
        + [per_pack(length, a.shape[1]) for a in saved],
        out_specs=[per_pack(length, D)] + [whole(s) for s in sums],
        out_shape=[struct((rows, D), f32)] + [struct(s, k) for s, k in zip(sums, kinds)],
        scratch_shapes=[
            pltpu.VMEM(w_first.shape, f32),
            pltpu.VMEM(w_mix.shape, f32),
            pltpu.VMEM((length, width), bf16),
        ],
        compiler_params=params,
        name="mixer_backward",
    )(d_middle, hidden, w_first, w_mix, col, row, cos, sin, conv, head, skip, *saved)


def ffn_both(x, cot, w_gu, w_down, micro):
    rows, D = x.shape
    length = rows // micro
    return pl.pallas_call(
        ffn_body,
        grid=(micro,),
        in_specs=[per_pack(length, D), per_pack(length, D), whole(w_gu.shape), whole(w_down.shape)],
        out_specs=[per_pack(length, D), per_pack(length, D), whole(w_gu.shape), whole(w_down.shape)],
        out_shape=[
            struct((rows, D), f32),
            struct((rows, D), f32),
            struct(w_gu.shape, bf16),
            struct(w_down.shape, bf16),
        ],
        scratch_shapes=[pltpu.VMEM(w_gu.shape, f32), pltpu.VMEM(w_down.shape, f32)],
        compiler_params=params,
        name="feed_forward",
    )(x, cot, w_gu, w_down)


def per_device(
    hidden_in,
    segment_ids,
    out_grad,
    norm_gain,
    w_qkv,
    w_o,
    w_zx,
    w_bc,
    w_dt,
    conv_w,
    conv_b,
    dt_bias,
    a_log,
    d_skip,
    w_out,
    second_gain,
    w_gate_up,
    w_down,
):
    micro, _, tokens, D = hidden_in.shape
    F, C = lax.axis_size("fsdp"), lax.axis_size("ctx")
    c = lax.axis_index("ctx")
    f = lax.axis_index("fsdp")
    length = tokens * C
    rows = micro * length
    mh = MH // C
    qw, dw, fw = QW // C, DI // C, FF // C
    kv = c * KV // C
    dt_pad = 128 - mh

    def cols(weight, start, size):
        return lax.dynamic_slice_in_dim(weight, start, size, 1)

    block = w_qkv.shape[0]
    first_shard = jnp.concatenate(
        [
            cols(w_qkv, c * qw, qw),
            cols(w_qkv, QW + kv * HD, HD),
            cols(w_qkv, QW + KW + kv * HD, HD),
            cols(w_zx, c * dw, dw),
            cols(w_zx, DI + c * dw, dw),
            w_bc,
            cols(w_dt, c * mh, mh),
            jnp.zeros((block, dt_pad), bf16),
        ],
        axis=1,
    )
    gu_shard = jnp.concatenate([cols(w_gate_up, c * fw, fw), cols(w_gate_up, FF + c * fw, fw)], 1)
    ro, rz, rd = w_o.shape[0] // C, w_out.shape[0] // C, w_down.shape[0] // C
    row_shard = jnp.concatenate(
        [
            lax.dynamic_slice_in_dim(w_o, c * ro, ro, 0),
            lax.dynamic_slice_in_dim(w_out, c * rz, rz, 0),
            lax.dynamic_slice_in_dim(w_down, c * rd, rd, 0),
        ],
        axis=0,
    )
    row_shard = to_owner_columns(row_shard, False)
    xb = conv_b.shape[0]
    small_shard = jnp.concatenate(
        [conv_w.reshape(-1), conv_b, norm_gain, second_gain], axis=0
    )
    small_all = pair_gather(small_shard, "fsdp")
    first_column = line_gather(first_shard)
    first_column, row_shard = lax.optimization_barrier((first_column, row_shard))
    row_column = line_gather(row_shard)
    row_column, gu_shard = lax.optimization_barrier((row_column, gu_shard))
    gu_column = line_gather(gu_shard)
    w_first = join_pairs(first_column).reshape(D, -1)
    row_all = join_pairs(row_column)
    w_gu = join_pairs(gu_column).reshape(D, -1)

    conv_all = small_all[:, : (CONV + 1) * xb].reshape(F, CONV + 1, xb)
    conv_all = conv_all.transpose(1, 0, 2).reshape(CONV + 1, XC).astype(f32)
    conv_own = jnp.concatenate([cols(conv_all, c * dw, dw), conv_all[:, DI:]], axis=1)
    gains = small_all[:, (CONV + 1) * xb :].astype(f32)
    gain = gains[:, :block].reshape(1, D)
    gain_two = gains[:, block:].reshape(1, D)
    w_mix = jnp.concatenate(
        [row_all[:, :ro].reshape(F * ro, D), row_all[:, ro : ro + rz].reshape(F * rz, D)], axis=0
    )
    w_down_own = row_all[:, ro + rz :].reshape(F * rd, D)
    dtb = lax.dynamic_slice_in_dim(dt_bias, c * mh, mh, 0)
    a_rate = jnp.exp(lax.dynamic_slice_in_dim(a_log, c * mh, mh, 0))
    skip = lax.dynamic_slice_in_dim(d_skip, c * mh, mh, 0)

    def gather_tokens(own):
        return ctx_gather(own).transpose(1, 0, 2, 3).reshape(rows, D)

    def scatter_tokens(partial):
        return ctx_scatter(partial.reshape(micro, C, tokens, D).transpose(1, 0, 2, 3))

    hidden_own = hidden_in[:, 0].astype(f32)
    hidden = gather_tokens(hidden_in[:, 0])
    cot = gather_tokens(out_grad[:, 0])
    tables = mixer_tables(segment_ids[:, 0], conv_own, dtb, a_rate, skip)

    normed, *saved = mixer_forward(hidden, gain, w_first, tables, micro)
    mixed = dot_plain(saved[-1], w_mix)
    middle = hidden_own + scatter_tokens(mixed)
    second_rms = lax.rsqrt(jnp.mean(middle * middle, axis=-1, keepdims=True) + epsilon)
    second_normed = gather_tokens((middle * second_rms * gain_two).astype(bf16))

    d_second, ffn_out, g_gu, g_down = ffn_both(second_normed, cot, w_gu, w_down_own, micro)
    d_second = scatter_tokens(d_second)
    block_out = (middle + scatter_tokens(ffn_out)).astype(bf16)
    g_gain_two = jnp.sum(d_second * middle * second_rms, axis=(0, 1))
    scaled_two = d_second * gain_two
    d_middle_own = (
        out_grad[:, 0].astype(f32)
        + second_rms * scaled_two
        - middle * second_rms**3 * jnp.mean(middle * scaled_two, axis=-1, keepdims=True)
    ).astype(bf16)
    d_middle = gather_tokens(d_middle_own)
    d_normed_part, g_first, g_mix, g_gain, g_conv, g_head, g_skip = mixer_backward(
        d_middle, hidden, w_first, w_mix, tables, (normed, *saved), micro
    )
    g_gain = g_gain[0]
    g_conv = g_conv[: CONV + 1]
    g_dtb, g_alog = g_head[0, :mh], g_head[1, :mh]
    g_skip = g_skip.reshape(mh, MP).sum(1)
    d_normed = scatter_tokens(d_normed_part)
    inv_own = lax.rsqrt(jnp.mean(hidden_own * hidden_own, axis=-1, keepdims=True) + epsilon)
    scaled = d_normed * gain
    grad_in = (
        d_middle_own.astype(f32)
        + inv_own * scaled
        - hidden_own * inv_own**3 * jnp.mean(hidden_own * scaled, axis=-1, keepdims=True)
    ).astype(bf16)

    ffn = jnp.concatenate([g_gu.reshape(F, block, -1), g_down.reshape(F, rd, D)], axis=1)
    ffn = fsdp_scatter(ffn).astype(bf16)
    width = w_first.shape[1]
    g_o, g_out = g_mix[: F * ro].reshape(F, ro, D), g_mix[F * ro :].reshape(F, rz, D)
    spare = ((0, 0), (0, 0), (0, width - D))
    last = jnp.concatenate(
        [g_first.reshape(F, block, width), jnp.pad(g_o, spare), jnp.pad(g_out, spare)], axis=1
    )
    last = fsdp_scatter(last).astype(bf16)
    first_sum = last[:block]
    mix = last[block:, :D]
    turned = to_owner_columns(jnp.concatenate([mix, ffn[block:]], axis=0), True)
    turned = ctx_gather(turned).astype(f32)
    grad_o = turned[:, :ro].reshape(C * ro, D)
    grad_out = turned[:, ro : ro + rz].reshape(C * rz, D)
    grad_down = turned[:, ro + rz :].reshape(C * rd, D)

    def side(parts):
        return jnp.concatenate([parts[i] for i in range(C)], axis=1)

    gu_all = ctx_gather(ffn[:block]).astype(f32)
    grad_gate_up = jnp.concatenate([side(gu_all[:, :, :fw]), side(gu_all[:, :, fw:])], axis=1)
    first_all = ctx_gather(first_sum).astype(f32)
    at = qw
    kv_pairs = first_all[:, :, at : at + 2 * HD].reshape(KV, C // KV, block, 2 * HD).sum(1)
    grad_qkv = jnp.concatenate(
        [side(first_all[:, :, :qw])]
        + [kv_pairs[j, :, :HD] for j in range(KV)]
        + [kv_pairs[j, :, HD:] for j in range(KV)],
        axis=1,
    )
    at += 2 * HD
    grad_zx = jnp.concatenate(
        [side(first_all[:, :, at : at + dw]), side(first_all[:, :, at + dw : at + 2 * dw])], axis=1
    )
    at += 2 * dw
    grad_bc = first_all[:, :, at : at + 2 * NS].sum(0)
    at += 2 * NS
    grad_dt = side(first_all[:, :, at : at + mh])

    conv_x = lax.dynamic_update_slice(
        jnp.zeros((CONV + 1, DI), f32), g_conv[:, :dw], (0, c * dw)
    )
    conv_full = jnp.concatenate([conv_x, g_conv[:, dw:]], axis=1)
    conv_full = conv_full.reshape(CONV + 1, F, xb).transpose(1, 0, 2).reshape(F, -1)
    small = jnp.concatenate([conv_full, g_gain.reshape(F, block), g_gain_two.reshape(F, block)], 1)
    heads = jnp.stack([g_dtb, g_alog, g_skip])
    heads = lax.dynamic_update_slice(jnp.zeros((3, MH), f32), heads, (0, c * mh))
    total = everywhere_sum(jnp.concatenate([small.reshape(-1), heads.reshape(-1)]))
    small = lax.dynamic_index_in_dim(total[: small.size].reshape(small.shape), f, 0, False)
    heads = total[-3 * MH :].reshape(3, MH)
    conv_sum = small[: (CONV + 1) * xb].reshape(CONV + 1, xb)
    at = (CONV + 1) * xb
    return (
        block_out[:, None],
        grad_in[:, None],
        small[at : at + block],
        grad_qkv,
        grad_o,
        grad_zx,
        grad_bc,
        grad_dt,
        conv_sum[:CONV],
        conv_sum[CONV],
        heads[0],
        heads[1],
        heads[2],
        grad_out,
        small[at + block :],
        grad_gate_up,
        grad_down,
    )


def solution(mesh):
    tokens = P(None, "fsdp", "ctx", None)
    rows = P("fsdp", None)
    return jax.shard_map(
        per_device,
        mesh=mesh,
        in_specs=(
            tokens,
            P(None, "fsdp", None),
            tokens,
            P("fsdp"),
            rows,
            rows,
            rows,
            rows,
            rows,
            P(None, "fsdp"),
            P("fsdp"),
            P(),
            P(),
            P(),
            rows,
            P("fsdp"),
            rows,
            rows,
        ),
        out_specs=(
            tokens,
            tokens,
            P("fsdp"),
            rows,
            rows,
            rows,
            rows,
            rows,
            P(None, "fsdp"),
            P("fsdp"),
            P(),
            P(),
            P(),
            rows,
            P("fsdp"),
            rows,
            rows,
        ),
        check_vma=False,
    )
```

time: 507 us -> 391 us (0.77); the launches traced: 498 us -> 389 us
  blocking collectives: 103 us -> 0 us
  matrix products: 56.9 us -> 0.71 us
  waiting for transfers between devices: 121 us -> 165 us
  Pallas kernels: 0 us -> 39.1 us
  other arithmetic: 65.8 us -> 35.4 us
  local copies, waits for them, and re-layouts: 91.1 us -> 64.6 us
  starting transfers between devices: 43.6 us -> 69.7 us
    psum x2 -> x0, blocking collectives: 52.2 us -> none  [the longest x1 40 us: per_device(): heads = lax.psum(heads, ('fsdp', 'ctx'))]
    unnamed x2 -> x0, blocking collectives: 50.8 us -> none
    dot_general x21 -> x0, matrix products: 44.2 us -> none  [the longest x5 14.3 us: dot_last(): lax.dot_general(left, right, (((1,), (1,)), ((), ())), preferred_element_...]
    pallas_call x0 -> x3, Pallas kernels: none -> 39.1 us  [the longest x1 19.8 us: mixer_backward(): pl.pallas_call(backward_body, grid=(micro,), in_specs=[per_pack(length, D...]
    ppermute x22 -> x35, waiting for transfers between devices: 31.1 us -> 64.3 us  [swap(): return lax.ppermute(block, axis, [(i, i ^ bit) for i in devices])]
    reduce_scatter x3 -> x2, waiting for transfers between devices: 12.7 us -> 42 us  [fsdp_scatter(): lax.psum_scatter(parts.reshape((-1, 2) + parts.shape[1:]).astype(bf16), '...]
    ppermute x22 -> x35, starting transfers between devices: 34 us -> 61.2 us  [swap(): return lax.ppermute(block, axis, [(i, i ^ bit) for i in devices])]
    another operation x10 -> x1, other arithmetic: 18.6 us -> 0.6 us  [mixer_tables(): head = jnp.pad(jnp.stack([dt_bias, a_rate]), ((0, 6), (0, 128 - heads)))]
  transfers between devices with their start and end apart: 30 -> 42, of which waited for: 14 -> 23; matrix products, arithmetic and copies ran while one was open for 38% -> 18% of each run, Pallas kernels for 0% -> 7%
where the time goes in v2:
time: 391 us; the launch traced here: 389 us
  waiting for transfers between devices  165 us (42%)
  starting transfers between devices  69.7 us (18%)
  local copies, waits for them, and re-layouts  64.6 us (17%)
  Pallas kernels  39.1 us (10%)
  other arithmetic  35.4 us (9%)
  between operations  14.9 us (4%)
    ppermute x35, waiting for transfers between devices, swap(): return lax.ppermute(block, axis, [(i, i ^ bit) for i in devices])  64.3 us
    ppermute x35, starting transfers between devices, swap(): return lax.ppermute(block, axis, [(i, i ^ bit) for i in devices])  61.2 us
    all_gather x3, waiting for transfers between devices, line_gather(): lax.all_gather(shard, 'fsdp', axis=0, tiled=False, axis_index_groups=line...  47 us
    reduce_scatter x2, waiting for transfers between devices, fsdp_scatter(): lax.psum_scatter(parts.reshape((-1, 2) + parts.shape[1:]).astype(bf16), '...  42 us
    pallas_call x1, Pallas kernels, mixer_backward(): pl.pallas_call(backward_body, grid=(micro,), in_specs=[per_pack(length, D...  19.8 us
    unnamed x88, local copies, waits for them, and re-layouts  15.7 us
    ppermute x2, waiting for transfers between devices, to_owner_columns(): return lax.ppermute(rows, ('fsdp', 'ctx'), route)  11.2 us
    pallas_call x1, Pallas kernels, ffn_both(): pl.pallas_call(ffn_body, grid=(micro,), in_specs=[per_pack(length, D), pe...  10.8 us
  transfers between devices with their start and end apart: 42, of which 23 were waited for; matrix products, arithmetic and copies ran while one was open for 18% of the time, Pallas kernels for 7%

profile of v2, /device:TPU:3, one launch (start us, length us, event | category | flops | bytes accessed | tf_op | source)
XLA Modules:
  0.0 388.9 jit_solution(17289208397480598085)
XLA Ops:
  14.5 4.8 %collective-permute-start.5 = (bf16[128,1024]{1,0:T(8,128)(2,1)S(1)}, bf16[128,1024]{1,0:T(8,128)(2,1)S(1)}, u32[]{:S(2)}, u32[]{:S(2)}) collective-permute-start(bf16[128,1024]{1,0:T(8,128)(2,1)S(1)} %pad_maximum_fusion.3), channel_id=1, source_target_pairs={{0,0},{1,4},{2,8},{3,12},{4,16},{5,20},{6,24},{7,28},{8,1},{9,5},{... | collective-permute-start | bytes 786440 | tf_op jit(solution)/shard_map/ppermute | solution.py:125
  27.3 13.3 %collective-permute-start.3 = (bf16[2,1376]{1,0:T(2,128)(2,1)S(1)}, bf16[2,1376]{1,0:T(2,128)(2,1)S(1)}, u32[]{:S(2)}, u32[]{:S(2)}) collective-permute-start(bf16[2,1376]{1,0:T(2,128)(2,1)S(1)} %broadcast_select_fusion.1), channel_id=1, source_target_pairs={{0,8},{4,12},{8,0},{12,4},{16,24},{20,28},{24,16},{28,20},{1,9},{5... | collective-permute-start | bytes 16520 | tf_op jit(solution)/shard_map/ppermute | solution.py:43
  40.7 8.8 %all-gather.7.cloned.1.call-done = bf16[512,1408]{1,0:T(8,128)(2,1)} async-done(((bf16[128,1408]{1,0:T(8,128)(2,1)}), bf16[512,1408]{1,0:T(8,128)(2,1)}) %all-gather.7.cloned.1.call-update) | async-done | bytes 1441808 | tf_op jit(solution)/shard_map/all_gather | solution.py:70
  49.7 11.2 %collective-permute-start.4 = (bf16[4,1376]{1,0:T(4,128)(2,1)S(1)}, bf16[4,1376]{1,0:T(4,128)(2,1)S(1)}, u32[]{:S(2)}, u32[]{:S(2)}) collective-permute-start(bf16[4,1376]{1,0:T(4,128)(2,1)S(1)} %select_n.494), channel_id=1, source_target_pairs={{0,4},{4,0},{8,12},{12,8},{16,20},{20,16},{24,28},{28,24},{1,5},{5... | collective-permute-start | bytes 33032 | tf_op jit(solution)/shard_map/ppermute | solution.py:43
  66.6 25.5 %all-gather.9.cloned.1.call-done = bf16[512,1024]{1,0:T(8,128)(2,1)} async-done(((bf16[128,1024]{1,0:T(8,128)(2,1)}), bf16[512,1024]{1,0:T(8,128)(2,1)}) %all-gather.9.cloned.1.call-update) | async-done | bytes 1048592 | tf_op jit(solution)/shard_map/all_gather | solution.py:70
  98.7 8.5 %mixer_forward.1 = (bf16[512,1024]{1,0:T(8,128)(2,1)}, bf16[512,256]{1,0:T(8,128)(2,1)}, f32[512,384]{1,0:T(8,128)}, bf16[512,640]{1,0:T(8,128)(2,1)}, f32[512,1...) custom-call(bf16[512,1024]{1,0:T(8,128)(2,1)} %bitcast.396, f32[1,1024]{1,0:T(1,128)} %bitcast.482, ...), custom_call_target="tpu_custom_call" | custom-call | tf_op jit(solution)/shard_map/mixer_forward/pallas_call | solution.py:508
  107.4 11.0 %collective-permute-done.7 = bf16[4,128,1024]{2,1,0:T(8,128)(2,1)S(1)} collective-permute-done((bf16[4,128,1024]{2,1,0:T(8,128)(2,1)}, bf16[4,128,1024]{2,1,0:T(8,128)(2,1)S(1)}, u32[]{:S(2)}, u32[]{:S(2)}) %collective-permute-start.7) | collective-permute-done | bytes 1048608 | tf_op jit(solution)/shard_map/ppermute | solution.py:43
  127.2 12.7 %all-gather.11.cloned.1.call-done = bf16[512,1024]{1,0:T(8,128)(2,1)} async-done(((bf16[128,1024]{1,0:T(8,128)(2,1)}), bf16[512,1024]{1,0:T(8,128)(2,1)}) %all-gather.11.cloned.1.call-update) | async-done | bytes 1048592 | tf_op jit(solution)/shard_map/all_gather | solution.py:70
  144.2 4.0 %collective-permute-done.10 = bf16[1,2,64,1024]{3,2,1,0:T(8,128)(2,1)S(1)} collective-permute-done((bf16[1,2,64,1024]{3,2,1,0:T(8,128)(2,1)S(1)}, bf16[1,2,64,1024]{3,2,1,0:T(8,128)(2,1)S(1)}, u32[]{:S(2)}, u32[]{:S(2)}) %collective-permute-start.10) | collective-permute-done | bytes 262176 | tf_op jit(solution)/shard_map/ppermute | solution.py:43
  155.1 8.8 %collective-permute-done.14 = bf16[4,128,1024]{2,1,0:T(8,128)(2,1)S(1)} collective-permute-done((bf16[4,128,1024]{2,1,0:T(8,128)(2,1)}, bf16[4,128,1024]{2,1,0:T(8,128)(2,1)S(1)}, u32[]{:S(2)}, u32[]{:S(2)}) %collective-permute-start.14) | collective-permute-done | bytes 1048608 | tf_op jit(solution)/shard_map/ppermute | solution.py:43
  165.6 10.8 %feed_forward.1 = (f32[512,1024]{1,0:T(8,128)}, f32[512,1024]{1,0:T(8,128)}, bf16[1024,1024]{1,0:T(8,128)(2,1)}, bf16[512,1024]{1,0:T(8,128)(2,1)}) custom-call(bf16[512,1024]{1,0:T(8,128)(2,1)} %bitcast.423, bf16[512,1024]{1,0:T(8,128)(2,1)} %bitcast.420, bf16[1024,1024]{1,0:T(8,128)(2,1)} %bitcast.412, bf16[512,1024]{1,0:T(8,128)(2,1)} %bitcast.421), custom_call_target="tpu_custom_call" | custom-call | tf_op jit(solution)/shard_map/feed_forward/pallas_call | solution.py:566
  176.4 3.9 %pad_maximum_fusion.1 = bf16[4,2,192,1024]{3,2,1,0:T(8,128)(2,1)} fusion(bf16[4,2,64,1024]{3,2,1,0:T(8,128)(2,1)} %bitcast.457, bf16[4,2,128,1024]{3,2,1,0:T(8,128)(2,1)} %bitcast.443), kind=kLoop, calls=%fused_computation.1 | loop fusion | flops 6291456 | bytes 6291456 | tf_op jit(solution)/shard_map/concatenate | solution.py:714
  186.8 6.4 %collective-permute-done.18 = bf16[1,2,64,1024]{3,2,1,0:T(8,128)(2,1)S(1)} collective-permute-done((bf16[1,2,64,1024]{3,2,1,0:T(8,128)(2,1)S(1)}, bf16[1,2,64,1024]{3,2,1,0:T(8,128)(2,1)S(1)}, u32[]{:S(2)}, u32[]{:S(2)}) %collective-permute-start.18) | collective-permute-done | bytes 262176 | tf_op jit(solution)/shard_map/ppermute | solution.py:43
  195.0 5.6 %collective-permute-done.19 = bf16[1,2,64,1024]{3,2,1,0:T(8,128)(2,1)S(1)} collective-permute-done((bf16[1,2,64,1024]{3,2,1,0:T(8,128)(2,1)S(1)}, bf16[1,2,64,1024]{3,2,1,0:T(8,128)(2,1)S(1)}, u32[]{:S(2)}, u32[]{:S(2)}) %collective-permute-start.19) | collective-permute-done | bytes 262176 | tf_op jit(solution)/shard_map/ppermute | solution.py:43
  205.5 19.8 %mixer_backward.1 = (f32[512,1024]{1,0:T(8,128)}, bf16[1024,1408]{1,0:T(8,128)(2,1)}, bf16[512,1024]{1,0:T(8,128)(2,1)}, f32[1,1024]{1,0:T(1,128)}, f32[8,640]{1...) custom-call(bf16[512,1024]{1,0:T(8,128)(2,1)} %bitcast.422, bf16[512,1024]{1,0:T(8,128)(2,1)} %bitcast.397, ...), custom_call_target="tpu_custom_call" | custom-call | tf_op jit(solution)/shard_map/mixer_backward/pallas_call | solution.py:538
  265.6 4.3 %collective-permute-done.35 = bf16[1,128,1024]{2,1,0:T(8,128)(2,1)} collective-permute-done((bf16[1,128,1024]{2,1,0:T(8,128)(2,1)}, bf16[1,128,1024]{2,1,0:T(8,128)(2,1)}, u32[]{:S(2)}, u32[]{:S(2)}) %collective-permute-start.35) | collective-permute-done | bytes 262176 | tf_op jit(solution)/shard_map/ppermute | solution.py:43
  271.2 3.9 collective-permute-start.36
  275.1 2.3 fusion.38
  281.9 42.0 %reduce-scatter.3.cloned.1.call-done = bf16[1,2,192,1408]{3,2,1,0:T(8,128)(2,1)} async-done(((bf16[4,2,192,1408]{3,2,1,0:T(8,128)(2,1)}), bf16[1,2,192,1408]{3,2,1,0:T(8,128)(2,1)}) %reduce-scatter.3.cloned.1.call-update) | async-done | bytes 1081360 | tf_op jit(solution)/shard_map/reduce_scatter | solution.py:81
  327.4 11.2 %collective-permute-done.28 = bf16[192,1408]{1,0:T(8,128)(2,1)S(1)} collective-permute-done((bf16[192,1408]{1,0:T(8,128)(2,1)S(1)}, bf16[192,1408]{1,0:T(8,128)(2,1)S(1)}, u32[]{:S(2)}, u32[]{:S(2)}) %collective-permute-start.28) | collective-permute-done | bytes 540704 | tf_op jit(solution)/shard_map/ppermute | solution.py:43
  339.7 3.1 collective-permute-start.32
  345.8 11.1 %collective-permute-done.32 = bf16[128,1024]{1,0:T(8,128)(2,1)S(1)} collective-permute-done((bf16[128,1024]{1,0:T(8,128)(2,1)S(1)}, bf16[128,1024]{1,0:T(8,128)(2,1)S(1)}, u32[]{:S(2)}, u32[]{:S(2)}) %collective-permute-start.32) | collective-permute-done | bytes 262176 | tf_op jit(solution)/shard_map/ppermute | solution.py:125
  360.2 3.1 collective-permute-done.33
  363.5 2.4 collective-permute-start.34
  (334 shorter events, 135.6 us)
Async XLA Ops:
  7.3 42.3 %all-gather.7.cloned.1.call-start = ((), (), s32[]{:S(2)}) async-start(), calls=%async_computation.4 | async-start | bytes 1802240 | tf_op jit(solution)/shard_map/all_gather | solution.py:70
  12.7 79.4 %all-gather.9.cloned.1.call-start = ((), (), s32[]{:S(2)}) async-start(), calls=%async_computation.5 | async-start | bytes 1310720 | tf_op jit(solution)/shard_map/all_gather | solution.py:70
  14.5 26.2 %collective-permute-start.5 = (bf16[128,1024]{1,0:T(8,128)(2,1)S(1)}, bf16[128,1024]{1,0:T(8,128)(2,1)S(1)}, u32[]{:S(2)}, u32[]{:S(2)}) collective-permute-start(bf16[128,1024]{1,0:T(8,128)(2,1)S(1)} %pad_maximum_fusion.3), channel_id=1, source_target_pairs={{0,0},{1,4},{2,8},{3,12},{4,16},{5,20},{6,24},{7,28},{8,1},{9,5},{... | collective-permute-start | bytes 786440 | tf_op jit(solution)/shard_map/ppermute | solution.py:125
  20.8 43.1 %collective-permute-start = (bf16[1,2,64,1024]{3,2,1,0:T(8,128)(2,1)S(1)}, bf16[1,2,64,1024]{3,2,1,0:T(8,128)(2,1)S(1)}, u32[]{:S(2)}, u32[]{:S(2)}) collective-permute-start(bf16[1,2,64,1024]{3,2,1,0:T(8,128)(2,1)S(1)} %bitcast.391), channel_id=1, source_target_pairs={{0,2},{1,3},{2,0},{3,1},{4,6},{5,7},{6,4},{7,5},{8,10},{9,11},{10,... | collective-permute-start | bytes 786440 | tf_op jit(solution)/shard_map/ppermute | solution.py:43
  27.3 22.3 %collective-permute-start.3 = (bf16[2,1376]{1,0:T(2,128)(2,1)S(1)}, bf16[2,1376]{1,0:T(2,128)(2,1)S(1)}, u32[]{:S(2)}, u32[]{:S(2)}) collective-permute-start(bf16[2,1376]{1,0:T(2,128)(2,1)S(1)} %broadcast_select_fusion.1), channel_id=1, source_target_pairs={{0,8},{4,12},{8,0},{12,4},{16,24},{20,28},{24,16},{28,20},{1,9},{5... | collective-permute-start | bytes 16520 | tf_op jit(solution)/shard_map/ppermute | solution.py:43
  49.6 90.3 %all-gather.11.cloned.1.call-start = ((), (), s32[]{:S(2)}) async-start(), calls=%async_computation.6 | async-start | bytes 1310720 | tf_op jit(solution)/shard_map/all_gather | solution.py:70
  49.7 13.5 %collective-permute-start.4 = (bf16[4,1376]{1,0:T(4,128)(2,1)S(1)}, bf16[4,1376]{1,0:T(4,128)(2,1)S(1)}, u32[]{:S(2)}, u32[]{:S(2)}) collective-permute-start(bf16[4,1376]{1,0:T(4,128)(2,1)S(1)} %select_n.494), channel_id=1, source_target_pairs={{0,4},{4,0},{8,12},{12,8},{16,20},{20,16},{24,28},{28,24},{1,5},{5... | collective-permute-start | bytes 33032 | tf_op jit(solution)/shard_map/ppermute | solution.py:43
  63.3 32.9 %collective-permute-start.6 = (bf16[4,128,1408]{2,1,0:T(8,128)(2,1)}, bf16[4,128,1408]{2,1,0:T(8,128)(2,1)S(1)}, u32[]{:S(2)}, u32[]{:S(2)}) collective-permute-start(bf16[4,128,1408]{2,1,0:T(8,128)(2,1)} %bitcast.445), channel_id=1, source_target_pairs={{0,4},{4,0},{8,12},{12,8},{16,20},{20,16},{24,28},{28,24},{1,5},{5... | collective-permute-start | bytes 4325384 | tf_op jit(solution)/shard_map/ppermute | solution.py:43
  64.8 28.9 %collective-permute-start.1 = (bf16[2,2,64,1024]{3,2,1,0:T(8,128)(2,1)}, bf16[2,2,64,1024]{3,2,1,0:T(8,128)(2,1)}, u32[]{:S(2)}, u32[]{:S(2)}) collective-permute-start(bf16[2,2,64,1024]{3,2,1,0:T(8,128)(2,1)} %maximum_select_fusion.12), channel_id=1, source_target_pairs={{0,1},{1,0},{2,3},{3,2},{4,5},{5,4},{6,7},{7,6},{8,9},{9,8},{10,11... | collective-permute-start | bytes 1572872 | tf_op jit(solution)/shard_map/ppermute | solution.py:43
  92.1 26.4 %collective-permute-start.7 = (bf16[4,128,1024]{2,1,0:T(8,128)(2,1)}, bf16[4,128,1024]{2,1,0:T(8,128)(2,1)S(1)}, u32[]{:S(2)}, u32[]{:S(2)}) collective-permute-start(bf16[4,128,1024]{2,1,0:T(8,128)(2,1)} %bitcast.449), channel_id=1, source_target_pairs={{0,4},{4,0},{8,12},{12,8},{16,20},{20,16},{24,28},{28,24},{1,5},{5... | collective-permute-start | bytes 3145736 | tf_op jit(solution)/shard_map/ppermute | solution.py:43
  107.2 142.9 %reduce-scatter.5.cloned.1.call-start = ((), (), s32[]{:S(2)}) async-start(), calls=%async_computation.3 | async-start | bytes 3932160 | tf_op jit(solution)/shard_map/reduce_scatter | solution.py:81
  125.6 14.5 %collective-permute-start.9 = (bf16[1,2,64,1024]{3,2,1,0:T(8,128)(2,1)S(1)}, bf16[1,2,64,1024]{3,2,1,0:T(8,128)(2,1)}, u32[]{:S(2)}, u32[]{:S(2)}) collective-permute-start(bf16[1,2,64,1024]{3,2,1,0:T(8,128)(2,1)S(1)} %dynamic-slice_convert_fusion.3), channel_id=1, source_target_pairs={{0,2},{1,3},{2,0},{3,1},{4,6},{5,7},{6,4},{7,5},{8,10},{9,11},{10,... | collective-permute-start | bytes 786440 | tf_op jit(solution)/shard_map/ppermute | solution.py:43
  125.7 16.9 %collective-permute-start.12 = (bf16[1,2,64,1024]{3,2,1,0:T(8,128)(2,1)S(1)}, bf16[1,2,64,1024]{3,2,1,0:T(8,128)(2,1)S(1)}, u32[]{:S(2)}, u32[]{:S(2)}) collective-permute-start(bf16[1,2,64,1024]{3,2,1,0:T(8,128)(2,1)S(1)} %bitcast.428), channel_id=1, source_target_pairs={{0,2},{1,3},{2,0},{3,1},{4,6},{5,7},{6,4},{7,5},{8,10},{9,11},{10,... | collective-permute-start | bytes 786440 | tf_op jit(solution)/shard_map/ppermute | solution.py:43
  139.9 24.1 %collective-permute-start.14 = (bf16[4,128,1024]{2,1,0:T(8,128)(2,1)}, bf16[4,128,1024]{2,1,0:T(8,128)(2,1)S(1)}, u32[]{:S(2)}, u32[]{:S(2)}) collective-permute-start(bf16[4,128,1024]{2,1,0:T(8,128)(2,1)} %bitcast.451), channel_id=1, source_target_pairs={{0,4},{4,0},{8,12},{12,8},{16,20},{20,16},{24,28},{28,24},{1,5},{5... | collective-permute-start | bytes 3145736 | tf_op jit(solution)/shard_map/ppermute | solution.py:43
  180.3 143.6 %reduce-scatter.3.cloned.1.call-start = ((), (), s32[]{:S(2)}) async-start(), calls=%async_computation.2 | async-start | bytes 5406720 | tf_op jit(solution)/shard_map/reduce_scatter | solution.py:81
  231.4 11.4 %collective-permute-start.15 = (bf16[2,2,64,1024]{3,2,1,0:T(8,128)(2,1)S(1)}, bf16[2,2,64,1024]{3,2,1,0:T(8,128)(2,1)S(1)}, u32[]{:S(2)}, u32[]{:S(2)}) collective-permute-start(bf16[2,2,64,1024]{3,2,1,0:T(8,128)(2,1)S(1)} %fusion.13), channel_id=1, source_target_pairs={{0,1},{1,0},{2,3},{3,2},{4,5},{5,4},{6,7},{7,6},{8,9},{9,8},{10,11... | collective-permute-start | bytes 1572872 | tf_op jit(solution)/shard_map/ppermute | solution.py:43
  241.7 12.9 %collective-permute-start.21 = (bf16[2,2,64,1024]{3,2,1,0:T(8,128)(2,1)}, bf16[2,2,64,1024]{3,2,1,0:T(8,128)(2,1)}, u32[]{:S(2)}, u32[]{:S(2)}) collective-permute-start(bf16[2,2,64,1024]{3,2,1,0:T(8,128)(2,1)} %fusion.15), channel_id=1, source_target_pairs={{0,1},{1,0},{2,3},{3,2},{4,5},{5,4},{6,7},{7,6},{8,9},{9,8},{10,11... | collective-permute-start | bytes 1572872 | tf_op jit(solution)/shard_map/ppermute | solution.py:43
  247.4 27.7 %collective-permute-start.16 = (bf16[1,2,64,1024]{3,2,1,0:T(8,128)(2,1)}, bf16[1,2,64,1024]{3,2,1,0:T(8,128)(2,1)}, u32[]{:S(2)}, u32[]{:S(2)}) collective-permute-start(bf16[1,2,64,1024]{3,2,1,0:T(8,128)(2,1)} %dynamic-slice_convert_fusion.2), channel_id=1, source_target_pairs={{0,2},{1,3},{2,0},{3,1},{4,6},{5,7},{6,4},{7,5},{8,10},{9,11},{10,... | collective-permute-start | bytes 786440 | tf_op jit(solution)/shard_map/ppermute | solution.py:43
  261.8 8.0 %collective-permute-start.35 = (bf16[1,128,1024]{2,1,0:T(8,128)(2,1)}, bf16[1,128,1024]{2,1,0:T(8,128)(2,1)}, u32[]{:S(2)}, u32[]{:S(2)}) collective-permute-start(bf16[1,128,1024]{2,1,0:T(8,128)(2,1)} %get-tuple-element.168), channel_id=1, source_target_pairs={{0,2},{1,3},{2,0},{3,1},{4,6},{5,7},{6,4},{7,5},{8,10},{9,11},{10,... | collective-permute-start | bytes 786440 | tf_op jit(solution)/shard_map/ppermute | solution.py:43
  271.2 8.8 %collective-permute-start.36 = (bf16[2,128,1024]{2,1,0:T(8,128)(2,1)S(1)}, bf16[2,128,1024]{2,1,0:T(8,128)(2,1)S(1)}, u32[]{:S(2)}, u32[]{:S(2)}) collective-permute-start(bf16[2,128,1024]{2,1,0:T(8,128)(2,1)S(1)} %maximum_select_fusion.20), channel_id=1, source_target_pairs={{0,1},{1,0},{2,3},{3,2},{4,5},{5,4},{6,7},{7,6},{8,9},{9,8},{10,11... | collective-permute-start | bytes 1572872 | tf_op jit(solution)/shard_map/ppermute | solution.py:43
  325.1 13.5 %collective-permute-start.28 = (bf16[192,1408]{1,0:T(8,128)(2,1)S(1)}, bf16[192,1408]{1,0:T(8,128)(2,1)S(1)}, u32[]{:S(2)}, u32[]{:S(2)}) collective-permute-start(bf16[192,1408]{1,0:T(8,128)(2,1)S(1)} %dynamic-slice_bitcast_fusion), channel_id=1, source_target_pairs={{0,4},{4,0},{8,12},{12,8},{16,20},{20,16},{24,28},{28,24},{1,5},{5... | collective-permute-start | bytes 1622024 | tf_op jit(solution)/shard_map/ppermute | solution.py:43
  339.7 17.2 %collective-permute-start.32 = (bf16[128,1024]{1,0:T(8,128)(2,1)S(1)}, bf16[128,1024]{1,0:T(8,128)(2,1)S(1)}, u32[]{:S(2)}, u32[]{:S(2)}) collective-permute-start(bf16[128,1024]{1,0:T(8,128)(2,1)S(1)} %pad_maximum_fusion.5), channel_id=1, source_target_pairs={{0,0},{4,1},{8,2},{12,3},{16,4},{20,5},{24,6},{28,7},{1,8},{5,9},{... | collective-permute-start | bytes 786440 | tf_op jit(solution)/shard_map/ppermute | solution.py:125
  342.9 15.7 %collective-permute-start.29 = (bf16[1,128,1408]{2,1,0:T(8,128)(2,1)S(1)}, bf16[1,128,1408]{2,1,0:T(8,128)(2,1)S(1)}, u32[]{:S(2)}, u32[]{:S(2)}) collective-permute-start(bf16[1,128,1408]{2,1,0:T(8,128)(2,1)S(1)} %get-tuple-element.166), channel_id=1, source_target_pairs={{0,2},{1,3},{2,0},{3,1},{4,6},{5,7},{6,4},{7,5},{8,10},{9,11},{10,... | collective-permute-start | bytes 1081352 | tf_op jit(solution)/shard_map/ppermute | solution.py:43
  358.7 11.8 %collective-permute-start.30 = (bf16[2,128,1408]{2,1,0:T(8,128)(2,1)S(1)}, bf16[2,128,1408]{2,1,0:T(8,128)(2,1)S(1)}, u32[]{:S(2)}, u32[]{:S(2)}) collective-permute-start(bf16[2,128,1408]{2,1,0:T(8,128)(2,1)S(1)} %maximum_select_fusion.11), channel_id=1, source_target_pairs={{0,1},{1,0},{2,3},{3,2},{4,5},{5,4},{6,7},{7,6},{8,9},{9,8},{10,11... | collective-permute-start | bytes 2162696 | tf_op jit(solution)/shard_map/ppermute | solution.py:43
  (53 other events, 412.8 us)
Sparse Core Ops, SparseCore 0:
  12.8 36.6 all-gather.6
  51.7 40.3 all-gather.8
  107.3 32.4 all-gather.10
  180.4 60.8 reduce-scatter.4
  243.5 80.3 reduce-scatter.2

commit v3 on v2

--- a/solution.py
+++ b/solution.py
@@ -70,6 +70,12 @@
     return lax.all_gather(shard, "fsdp", axis=0, tiled=False, axis_index_groups=line_groups())
 
 
+def both_of_pair(shard):
+    first = lax.axis_index("fsdp") % 2 == 0
+    other = swap(shard, "fsdp", 1)
+    return jnp.where(first, jnp.stack([shard, other]), jnp.stack([other, shard]))
+
+
 def join_pairs(column):
     first = lax.axis_index("fsdp") % 2 == 0
     other = swap(column, "fsdp", 1)
@@ -77,18 +83,40 @@
     return both.reshape((-1,) + column.shape[1:])
 
 
-def fsdp_scatter(parts):
-    column = lax.psum_scatter(
-        parts.reshape((-1, 2) + parts.shape[1:]).astype(bf16),
-        "fsdp",
-        scatter_dimension=0,
-        tiled=False,
-        axis_index_groups=line_groups(),
-    )
+def line_scatter(parts):
+    return lax.psum_scatter(
+        parts, "fsdp", scatter_dimension=0, tiled=False, axis_index_groups=line_groups()
+    )
+
+
+def hop(block, step):
+    size = lax.axis_size("fsdp")
+    route = [(i, i + 2 * step) for i in range(size) if 0 <= i + 2 * step < size]
+    return lax.ppermute(block, "fsdp", route)
+
+
+def line_scatter_hops(parts):
+    size = parts.shape[0]
+    if size > 4:
+        return line_scatter(parts)
+    place = lax.axis_index("fsdp") // 2
+    piece = lambda k: lax.dynamic_index_in_dim(parts, k % size, 0, False).astype(f32)
+    up = down = 0.0
+    for step in range(1, size):
+        up = hop((piece(size - step + place) + up).astype(bf16), 1).astype(f32)
+        down = hop((piece(step + place) + down).astype(bf16), -1).astype(f32)
+    return (piece(place) + up + down).astype(bf16)
+
+
+def pair_sum(parts, axis):
     mine = lax.axis_index("fsdp") % 2
-    keep = lax.dynamic_index_in_dim(column, mine, 0, False)
-    send = lax.dynamic_index_in_dim(column, 1 - mine, 0, False)
-    return keep.astype(f32) + swap(send, "fsdp", 1).astype(f32)
+    keep = lax.dynamic_index_in_dim(parts, mine, axis, False)
+    send = lax.dynamic_index_in_dim(parts, 1 - mine, axis, False)
+    return (keep.astype(f32) + swap(send, "fsdp", 1).astype(f32)).astype(bf16)
+
+
+def split_pairs(parts):
+    return parts.reshape((-1, 2) + parts.shape[1:])
 
 
 def ctx_scatter(parts):
@@ -304,13 +332,11 @@
     mixed_ref,
     d_normed_ref,
     g_first_ref,
-    g_mix_ref,
     g_gain_ref,
     g_conv_ref,
     g_head_ref,
     g_skip_ref,
     acc_first,
-    acc_mix,
     d_first,
 ):
     scale = 1.0 / math.sqrt(HD)
@@ -323,7 +349,6 @@
     @pl.when(first_step)
     def _():
         acc_first[...] = jnp.zeros_like(acc_first)
-        acc_mix[...] = jnp.zeros_like(acc_mix)
         g_gain_ref[...] = jnp.zeros_like(g_gain_ref)
         g_conv_ref[...] = jnp.zeros_like(g_conv_ref)
         g_head_ref[...] = jnp.zeros_like(g_head_ref)
@@ -333,7 +358,6 @@
     valid = allowed_pairs(col, row)
     length = col.shape[0]
     d_mid = d_mid_ref[...]
-    acc_mix[...] += dot_first(mixed_ref[...], d_mid)
     d_mixed = dot_last(d_mid, w_mix_ref[...]).astype(bf16)
 
     cos, sin = cos_ref[...], sin_ref[...]
@@ -445,11 +469,11 @@
     @pl.when(pl.program_id(0) == pl.num_programs(0) - 1)
     def _():
         g_first_ref[...] = acc_first[...].astype(bf16)
-        g_mix_ref[...] = acc_mix[...].astype(bf16)
-
-
-def ffn_body(x_ref, cot_ref, gu_ref, down_ref, d_second_ref, out_ref, g_gu_ref, g_down_ref, acc_gu, acc_down):
+
+
+def ffn_body(x_ref, cot_ref, gu_ref, down_ref, d_second_ref, out_ref, *rest):
     fw = down_ref.shape[0]
+    acc_gu, acc_down = rest[-2:]
 
     @pl.when(pl.program_id(0) == 0)
     def _():
@@ -473,8 +497,15 @@
 
     @pl.when(pl.program_id(0) == pl.num_programs(0) - 1)
     def _():
-        g_gu_ref[...] = acc_gu[...].astype(bf16)
-        g_down_ref[...] = acc_down[...].astype(bf16)
+        if len(rest) == 4:
+            rest[0][...] = acc_gu[...].astype(bf16)
+            rest[1][...] = acc_down[...].astype(bf16)
+        else:
+            parts = rest[0].shape[0]
+            block, rd = acc_gu.shape[0] // parts, acc_down.shape[0] // parts
+            for i in range(parts):
+                rest[0][i, :block] = acc_gu[i * block : (i + 1) * block].astype(bf16)
+                rest[0][i, block:] = acc_down[i * rd : (i + 1) * rd].astype(bf16)
 
 
 def per_pack(block_rows, width):
@@ -533,8 +564,8 @@
     col, row, cos, sin, conv, head, skip = tables
     width = w_first.shape[1]
     flat = [whole(a.shape) for a in (cos, sin, conv, head, skip)]
-    sums = [w_first.shape, w_mix.shape, (1, D), conv.shape, head.shape, skip.shape]
-    kinds = [bf16, bf16, f32, f32, f32, f32]
+    sums = [w_first.shape, (1, D), conv.shape, head.shape, skip.shape]
+    kinds = [bf16, f32, f32, f32, f32]
     return pl.pallas_call(
         backward_body,
         grid=(micro,),
@@ -552,7 +583,6 @@
         out_shape=[struct((rows, D), f32)] + [struct(s, k) for s, k in zip(sums, kinds)],
         scratch_shapes=[
             pltpu.VMEM(w_first.shape, f32),
-            pltpu.VMEM(w_mix.shape, f32),
             pltpu.VMEM((length, width), bf16),
         ],
         compiler_params=params,
@@ -560,24 +590,68 @@
     )(d_middle, hidden, w_first, w_mix, col, row, cos, sin, conv, head, skip, *saved)
 
 
-def ffn_both(x, cot, w_gu, w_down, micro):
+def ffn_both(x, cot, w_gu, w_down, micro, parts):
     rows, D = x.shape
     length = rows // micro
-    return pl.pallas_call(
+    block, rd = D // parts, w_down.shape[0] // parts
+    joined = block % 16 == 0 and rd % 16 == 0
+    shapes = [(parts, block + rd, D)] if joined else [w_gu.shape, w_down.shape]
+    out = pl.pallas_call(
         ffn_body,
         grid=(micro,),
         in_specs=[per_pack(length, D), per_pack(length, D), whole(w_gu.shape), whole(w_down.shape)],
-        out_specs=[per_pack(length, D), per_pack(length, D), whole(w_gu.shape), whole(w_down.shape)],
-        out_shape=[
-            struct((rows, D), f32),
-            struct((rows, D), f32),
-            struct(w_gu.shape, bf16),
-            struct(w_down.shape, bf16),
-        ],
+        out_specs=[per_pack(length, D), per_pack(length, D)] + [whole(s) for s in shapes],
+        out_shape=[struct((rows, D), f32), struct((rows, D), f32)]
+        + [struct(s, bf16) for s in shapes],
         scratch_shapes=[pltpu.VMEM(w_gu.shape, f32), pltpu.VMEM(w_down.shape, f32)],
         compiler_params=params,
         name="feed_forward",
     )(x, cot, w_gu, w_down)
+    if joined:
+        return out
+    d_second, ffn_out, g_gu, g_down = out
+    g_ffn = jnp.concatenate([g_gu.reshape(parts, block, -1), g_down.reshape(parts, rd, D)], axis=1)
+    return d_second, ffn_out, g_ffn
+
+
+def assemble_body(first_ref, qkv_ref, zx_ref, bc_ref, dt_ref):
+    size, block, _ = first_ref.shape
+    dw = zx_ref.shape[1] // 2 // size
+    mh = dt_ref.shape[1] // size
+    at_bc = 256 + 2 * dw
+    group = size // KV
+    heads = []
+    for v in range(KV):
+        tile = 0.0
+        for i in range(v * group, (v + 1) * group):
+            tile = tile + first_ref[i, :, 128:256].astype(f32)
+        heads.append(tile)
+    qkv_ref[:, QW : QW + KW] = half_select(heads[0], pltpu.roll(heads[1], HD, 1))
+    qkv_ref[:, QW + KW :] = half_select(pltpu.roll(heads[0], HD, 1), heads[1])
+    bc = 0.0
+    steps = jnp.zeros((block, 128), f32)
+    lanes = lane_index((block, 128))
+    for i in range(size):
+        qkv_ref[:, 128 * i : 128 * (i + 1)] = first_ref[i, :, :128].astype(f32)
+        zx_ref[:, dw * i : dw * (i + 1)] = first_ref[i, :, 256 : 256 + dw].astype(f32)
+        zx_ref[:, DI + dw * i : DI + dw * (i + 1)] = first_ref[i, :, 256 + dw : at_bc].astype(f32)
+        bc = bc + first_ref[i, :, at_bc : at_bc + 2 * NS].astype(f32)
+        tile = first_ref[i, :, at_bc + 2 * NS :].astype(f32)
+        if i:
+            tile = pltpu.roll(tile, mh * i, 1)
+        steps = jnp.where((lanes >= mh * i) & (lanes < mh * (i + 1)), tile, steps)
+    bc_ref[...] = bc
+    dt_ref[...] = steps[:, : mh * size]
+
+
+def assemble_first(first_all, widths):
+    block = first_all.shape[1]
+    return pl.pallas_call(
+        assemble_body,
+        out_shape=[struct((block, n), f32) for n in widths],
+        compiler_params=pltpu.CompilerParams(vmem_limit_bytes=56 * 1024 * 1024),
+        name="assemble_first",
+    )(first_all)
 
 
 def per_device(
@@ -644,14 +718,14 @@
         [conv_w.reshape(-1), conv_b, norm_gain, second_gain], axis=0
     )
     small_all = pair_gather(small_shard, "fsdp")
+    bar = lax.optimization_barrier
     first_column = line_gather(first_shard)
-    first_column, row_shard = lax.optimization_barrier((first_column, row_shard))
+    first_column, row_shard = bar((first_column, row_shard))
     row_column = line_gather(row_shard)
-    row_column, gu_shard = lax.optimization_barrier((row_column, gu_shard))
-    gu_column = line_gather(gu_shard)
+    row_column, gu_pair = bar((row_column, both_of_pair(gu_shard)))
+    w_gu = line_gather(gu_pair).reshape(D, -1)
     w_first = join_pairs(first_column).reshape(D, -1)
     row_all = join_pairs(row_column)
-    w_gu = join_pairs(gu_column).reshape(D, -1)
 
     conv_all = small_all[:, : (CONV + 1) * xb].reshape(F, CONV + 1, xb)
     conv_all = conv_all.transpose(1, 0, 2).reshape(CONV + 1, XC).astype(f32)
@@ -684,7 +758,7 @@
     second_rms = lax.rsqrt(jnp.mean(middle * middle, axis=-1, keepdims=True) + epsilon)
     second_normed = gather_tokens((middle * second_rms * gain_two).astype(bf16))
 
-    d_second, ffn_out, g_gu, g_down = ffn_both(second_normed, cot, w_gu, w_down_own, micro)
+    d_second, ffn_out, g_ffn = ffn_both(second_normed, cot, w_gu, w_down_own, micro, F)
     d_second = scatter_tokens(d_second)
     block_out = (middle + scatter_tokens(ffn_out)).astype(bf16)
     g_gain_two = jnp.sum(d_second * middle * second_rms, axis=(0, 1))
@@ -695,14 +769,36 @@
         - middle * second_rms**3 * jnp.mean(middle * scaled_two, axis=-1, keepdims=True)
     ).astype(bf16)
     d_middle = gather_tokens(d_middle_own)
-    d_normed_part, g_first, g_mix, g_gain, g_conv, g_head, g_skip = mixer_backward(
+    g_mix = dot_first(saved[-1], d_middle).astype(bf16)
+    d_middle, g_mix = bar((d_middle, g_mix))
+    g_o, g_out = g_mix[: F * ro].reshape(F, ro, D), g_mix[F * ro :].reshape(F, rz, D)
+    mix_half = pair_sum(split_pairs(jnp.concatenate([g_o, g_out], axis=1)), 1)
+    d_normed_part, g_first, g_gain, g_conv, g_head, g_skip = mixer_backward(
         d_middle, hidden, w_first, w_mix, tables, (normed, *saved), micro
     )
+    ffn = line_scatter(split_pairs(g_ffn))
+    first_half = pair_sum(split_pairs(g_first.reshape(F, block, -1)), 1)
+    d_normed = scatter_tokens(d_normed_part)
     g_gain = g_gain[0]
     g_conv = g_conv[: CONV + 1]
     g_dtb, g_alog = g_head[0, :mh], g_head[1, :mh]
     g_skip = g_skip.reshape(mh, MP).sum(1)
-    d_normed = scatter_tokens(d_normed_part)
+    conv_x = lax.dynamic_update_slice(
+        jnp.zeros((CONV + 1, DI), f32), g_conv[:, :dw], (0, c * dw)
+    )
+    conv_full = jnp.concatenate([conv_x, g_conv[:, dw:]], axis=1)
+    conv_full = conv_full.reshape(CONV + 1, F, xb).transpose(1, 0, 2).reshape(F, -1)
+    small = jnp.concatenate([conv_full, g_gain.reshape(F, block), g_gain_two.reshape(F, block)], 1)
+    heads = jnp.stack([g_dtb, g_alog, g_skip])
+    heads = lax.dynamic_update_slice(jnp.zeros((3, MH), f32), heads, (0, c * mh))
+    total = jnp.concatenate([small.reshape(-1), heads.reshape(-1)])
+    mix = line_scatter_hops(mix_half)
+    ffn, first_half, mix, d_normed, total = bar((ffn, first_half, mix, d_normed, total))
+    first_sum = line_scatter(first_half)
+    ffn = pair_sum(ffn, 0)
+    total = everywhere_sum(total)
+    small = lax.dynamic_index_in_dim(total[: small.size].reshape(small.shape), f, 0, False)
+    heads = total[-3 * MH :].reshape(3, MH)
     inv_own = lax.rsqrt(jnp.mean(hidden_own * hidden_own, axis=-1, keepdims=True) + epsilon)
     scaled = d_normed * gain
     grad_in = (
@@ -711,17 +807,6 @@
         - hidden_own * inv_own**3 * jnp.mean(hidden_own * scaled, axis=-1, keepdims=True)
     ).astype(bf16)
 
-    ffn = jnp.concatenate([g_gu.reshape(F, block, -1), g_down.reshape(F, rd, D)], axis=1)
-    ffn = fsdp_scatter(ffn).astype(bf16)
-    width = w_first.shape[1]
-    g_o, g_out = g_mix[: F * ro].reshape(F, ro, D), g_mix[F * ro :].reshape(F, rz, D)
-    spare = ((0, 0), (0, 0), (0, width - D))
-    last = jnp.concatenate(
-        [g_first.reshape(F, block, width), jnp.pad(g_o, spare), jnp.pad(g_out, spare)], axis=1
-    )
-    last = fsdp_scatter(last).astype(bf16)
-    first_sum = last[:block]
-    mix = last[block:, :D]
     turned = to_owner_columns(jnp.concatenate([mix, ffn[block:]], axis=0), True)
     turned = ctx_gather(turned).astype(f32)
     grad_o = turned[:, :ro].reshape(C * ro, D)
@@ -733,35 +818,10 @@
 
     gu_all = ctx_gather(ffn[:block]).astype(f32)
     grad_gate_up = jnp.concatenate([side(gu_all[:, :, :fw]), side(gu_all[:, :, fw:])], axis=1)
-    first_all = ctx_gather(first_sum).astype(f32)
-    at = qw
-    kv_pairs = first_all[:, :, at : at + 2 * HD].reshape(KV, C // KV, block, 2 * HD).sum(1)
-    grad_qkv = jnp.concatenate(
-        [side(first_all[:, :, :qw])]
-        + [kv_pairs[j, :, :HD] for j in range(KV)]
-        + [kv_pairs[j, :, HD:] for j in range(KV)],
-        axis=1,
-    )
-    at += 2 * HD
-    grad_zx = jnp.concatenate(
-        [side(first_all[:, :, at : at + dw]), side(first_all[:, :, at + dw : at + 2 * dw])], axis=1
-    )
-    at += 2 * dw
-    grad_bc = first_all[:, :, at : at + 2 * NS].sum(0)
-    at += 2 * NS
-    grad_dt = side(first_all[:, :, at : at + mh])
-
-    conv_x = lax.dynamic_update_slice(
-        jnp.zeros((CONV + 1, DI), f32), g_conv[:, :dw], (0, c * dw)
-    )
-    conv_full = jnp.concatenate([conv_x, g_conv[:, dw:]], axis=1)
-    conv_full = conv_full.reshape(CONV + 1, F, xb).transpose(1, 0, 2).reshape(F, -1)
-    small = jnp.concatenate([conv_full, g_gain.reshape(F, block), g_gain_two.reshape(F, block)], 1)
-    heads = jnp.stack([g_dtb, g_alog, g_skip])
-    heads = lax.dynamic_update_slice(jnp.zeros((3, MH), f32), heads, (0, c * mh))
-    total = everywhere_sum(jnp.concatenate([small.reshape(-1), heads.reshape(-1)]))
-    small = lax.dynamic_index_in_dim(total[: small.size].reshape(small.shape), f, 0, False)
-    heads = total[-3 * MH :].reshape(3, MH)
+    grad_qkv, grad_zx, grad_bc, grad_dt = assemble_first(
+        ctx_gather(first_sum), [w_qkv.shape[1], w_zx.shape[1], w_bc.shape[1], w_dt.shape[1]]
+    )
+
     conv_sum = small[: (CONV + 1) * xb].reshape(CONV + 1, xb)
     at = (CONV + 1) * xb
     return (

time: 391 us -> 372 us (0.951)
  waiting for transfers between devices: 165 us -> 147 us
  local copies, waits for them, and re-layouts: 64.6 us -> 51.8 us
  starting transfers between devices: 69.7 us -> 78.5 us
    reduce_scatter x2, waiting for transfers between devices: 42 us -> 0.01 us  [line_scatter(): lax.psum_scatter(parts, 'fsdp', scatter_dimension=0, tiled=False, axis_in...]
    ppermute x2, waiting for transfers between devices: 11.2 us -> 44.9 us  [to_owner_columns(): return lax.ppermute(rows, ('fsdp', 'ctx'), route)]
    all_gather x3, waiting for transfers between devices: 47 us -> 28.6 us  [line_gather(): lax.all_gather(shard, 'fsdp', axis=0, tiled=False, axis_index_groups=line...]
    ppermute x0 -> x6, starting transfers between devices: none -> 13.8 us  [hop(): return lax.ppermute(block, 'fsdp', route)]
    ppermute x0 -> x6, waiting for transfers between devices: none -> 12.2 us  [hop(): return lax.ppermute(block, 'fsdp', route)]
    concatenate x4 -> x1, other arithmetic: 7.48 us -> 0.63 us  [per_device(): total = jnp.concatenate([small.reshape(-1), heads.reshape(-1)])]
    unnamed x88 -> x83, local copies, waits for them, and re-layouts: 15.7 us -> 10.2 us
    convert_element_type x3 -> x8, other arithmetic: 1.34 us -> 5.51 us  [the longest x3 5.32 us: pair_sum(): return (keep.astype(f32) + swap(send, 'fsdp', 1).astype(f32)).astype(bf16)]
  transfers between devices with their start and end apart: 42 -> 49, of which waited for: 23 -> 23; matrix products, arithmetic and copies ran while one was open for 18% -> 22% of each run, Pallas kernels for 7% -> 7%
where the time goes in v3:
time: 372 us; the launch traced here: 370 us
  waiting for transfers between devices  147 us (40%)
  starting transfers between devices  78.5 us (21%)
  local copies, waits for them, and re-layouts  51.8 us (14%)
  Pallas kernels  40.6 us (11%)
  other arithmetic  36.1 us (10%)
  between operations  14.9 us (4%)
    ppermute x36, waiting for transfers between devices, swap(): return lax.ppermute(block, axis, [(i, i ^ bit) for i in devices])  60.8 us
    ppermute x36, starting transfers between devices, swap(): return lax.ppermute(block, axis, [(i, i ^ bit) for i in devices])  58 us
    ppermute x2, waiting for transfers between devices, to_owner_columns(): return lax.ppermute(rows, ('fsdp', 'ctx'), route)  44.9 us
    all_gather x3, waiting for transfers between devices, line_gather(): lax.all_gather(shard, 'fsdp', axis=0, tiled=False, axis_index_groups=line...  28.6 us
    pallas_call x1, Pallas kernels, mixer_backward(): pl.pallas_call(backward_body, grid=(micro,), in_specs=[per_pack(length, D...  18.4 us
    ppermute x6, starting transfers between devices, hop(): return lax.ppermute(block, 'fsdp', route)  13.8 us
    ppermute x6, waiting for transfers between devices, hop(): return lax.ppermute(block, 'fsdp', route)  12.2 us
    pallas_call x1, Pallas kernels, ffn_both(): pl.pallas_call(ffn_body, grid=(micro,), in_specs=[per_pack(length, D), pe...  10.9 us
  transfers between devices with their start and end apart: 49, of which 23 were waited for; matrix products, arithmetic and copies ran while one was open for 22% of the time, Pallas kernels for 7%

profile of v3, /device:TPU:3, one launch (start us, length us, event | category | flops | bytes accessed | tf_op | source)
XLA Modules:
  0.0 370.0 jit_solution(8326194091925571833)
XLA Ops:
  20.8 3.2 collective-permute-start.5
  28.7 19.4 %collective-permute-done.5 = bf16[128,1024]{1,0:T(8,128)(2,1)S(1)} collective-permute-done((bf16[128,1024]{1,0:T(8,128)(2,1)S(1)}, bf16[128,1024]{1,0:T(8,128)(2,1)S(1)}, u32[]{:S(2)}, u32[]{:S(2)}) %collective-permute-start.5) | collective-permute-done | bytes 262176 | tf_op jit(solution)/shard_map/ppermute | solution.py:153
  48.0 5.8 %all-gather.7.cloned.1.call-done = bf16[512,1408]{1,0:T(8,128)(2,1)} async-done(((bf16[128,1408]{1,0:T(8,128)(2,1)}), bf16[512,1408]{1,0:T(8,128)(2,1)}) %all-gather.7.cloned.1.call-update) | async-done | bytes 1441808 | tf_op jit(solution)/shard_map/all_gather | solution.py:70
  54.0 13.4 %collective-permute-start.4 = (bf16[4,1376]{1,0:T(4,128)(2,1)S(1)}, bf16[4,1376]{1,0:T(4,128)(2,1)S(1)}, u32[]{:S(2)}, u32[]{:S(2)}) collective-permute-start(bf16[4,1376]{1,0:T(4,128)(2,1)S(1)} %select_n.540), channel_id=1, source_target_pairs={{0,4},{4,0},{8,12},{12,8},{16,20},{20,16},{24,28},{28,24},{1,5},{5... | collective-permute-start | bytes 33032 | tf_op jit(solution)/shard_map/ppermute | solution.py:43
  75.7 20.0 %all-gather.9.cloned.1.call-done = bf16[512,1024]{1,0:T(8,128)(2,1)} async-done(((bf16[128,1024]{1,0:T(8,128)(2,1)}), bf16[512,1024]{1,0:T(8,128)(2,1)}) %all-gather.9.cloned.1.call-update) | async-done | bytes 1048592 | tf_op jit(solution)/shard_map/all_gather | solution.py:70
  99.3 3.9 %collective-permute-done.6 = bf16[4,128,1408]{2,1,0:T(8,128)(2,1)S(1)} collective-permute-done((bf16[4,128,1408]{2,1,0:T(8,128)(2,1)}, bf16[4,128,1408]{2,1,0:T(8,128)(2,1)S(1)}, u32[]{:S(2)}, u32[]{:S(2)}) %collective-permute-start.6) | collective-permute-done | bytes 1441824 | tf_op jit(solution)/shard_map/ppermute | solution.py:43
  105.7 8.5 %mixer_forward.1 = (bf16[512,1024]{1,0:T(8,128)(2,1)}, bf16[512,256]{1,0:T(8,128)(2,1)}, f32[512,384]{1,0:T(8,128)}, bf16[512,640]{1,0:T(8,128)(2,1)}, f32[512,1...) custom-call(bf16[512,1024]{1,0:T(8,128)(2,1)} %bitcast.342, f32[1,1024]{1,0:T(1,128)} %bitcast.425, ...), custom_call_target="tpu_custom_call" | custom-call | tf_op jit(solution)/shard_map/mixer_forward/pallas_call | solution.py:539
  114.4 11.2 %collective-permute-done.8 = bf16[4,128,1024]{2,1,0:T(8,128)(2,1)S(1)} collective-permute-done((bf16[4,128,1024]{2,1,0:T(8,128)(2,1)}, bf16[4,128,1024]{2,1,0:T(8,128)(2,1)S(1)}, u32[]{:S(2)}, u32[]{:S(2)}) %collective-permute-start.8) | collective-permute-done | bytes 1048608 | tf_op jit(solution)/shard_map/ppermute | solution.py:43
  135.5 6.2 %collective-permute-done.10 = bf16[1,2,64,1024]{3,2,1,0:T(8,128)(2,1)S(1)} collective-permute-done((bf16[1,2,64,1024]{3,2,1,0:T(8,128)(2,1)S(1)}, bf16[1,2,64,1024]{3,2,1,0:T(8,128)(2,1)S(1)}, u32[]{:S(2)}, u32[]{:S(2)}) %collective-permute-start.10) | collective-permute-done | bytes 262176 | tf_op jit(solution)/shard_map/ppermute | solution.py:43
  142.3 4.9 %collective-permute-done.13 = bf16[1,2,64,1024]{3,2,1,0:T(8,128)(2,1)S(1)} collective-permute-done((bf16[1,2,64,1024]{3,2,1,0:T(8,128)(2,1)S(1)}, bf16[1,2,64,1024]{3,2,1,0:T(8,128)(2,1)S(1)}, u32[]{:S(2)}, u32[]{:S(2)}) %collective-permute-start.13) | collective-permute-done | bytes 262176 | tf_op jit(solution)/shard_map/ppermute | solution.py:43
  149.3 3.6 collective-permute-done.11
  161.7 10.9 %feed_forward.1 = (f32[512,1024]{1,0:T(8,128)}, f32[512,1024]{1,0:T(8,128)}, bf16[8,192,1024]{2,1,0:T(8,128)(2,1)}) custom-call(bf16[512,1024]{1,0:T(8,128)(2,1)} %bitcast.368, bf16[512,1024]{1,0:T(8,128)(2,1)} %bitcast.366, bf16[1024,1024]{1,0:T(8,128)(2,1)} %bitcast.391, bf16[512,1024]{1,0:T(8,128)(2,1)} %bitcast.367), custom_call_target="tpu_custom_call" | custom-call | tf_op jit(solution)/shard_map/feed_forward/pallas_call | solution.py:599
  178.1 6.4 %collective-permute-done.18 = bf16[1,2,64,1024]{3,2,1,0:T(8,128)(2,1)S(1)} collective-permute-done((bf16[1,2,64,1024]{3,2,1,0:T(8,128)(2,1)S(1)}, bf16[1,2,64,1024]{3,2,1,0:T(8,128)(2,1)S(1)}, u32[]{:S(2)}, u32[]{:S(2)}) %collective-permute-start.18) | collective-permute-done | bytes 262176 | tf_op jit(solution)/shard_map/ppermute | solution.py:43
  208.1 18.4 %mixer_backward.1 = (f32[512,1024]{1,0:T(8,128)}, bf16[1024,1408]{1,0:T(8,128)(2,1)}, f32[1,1024]{1,0:T(1,128)}, f32[8,640]{1,0:T(8,128)}, f32[8,128]{1,0:T(8,128)}, /*index=5*/f32[1,384]{1,0:T(1,128)}) custom-call(bf16[512,1024]{1,0:T(8,128)(2,1)} %bitcast.365, bf16[512,1024]{1,0:T(8,128)(2,1)} %bitcast.343, bf16[1024,1408]{1,0:T(8,128)(2,1)} %bitcast.336, ...), custom_call_target="tpu_custom_call" | custom-call | tf_op jit(solution)/shard_map/mixer_backward/pallas_call | solution.py:569
  239.9 4.2 %collective-permute-start.24 = (bf16[64,1024]{1,0:T(8,128)(2,1)S(1)}, bf16[64,1024]{1,0:T(8,128)(2,1)S(1)}, u32[]{:S(2)}, u32[]{:S(2)}) collective-permute-start(bf16[64,1024]{1,0:T(8,128)(2,1)S(1)} %fusion.28), channel_id=1, source_target_pairs={{0,8},{4,12},{8,16},{12,20},{16,24},{20,28},{1,9},{5,13},{9,17},{1... | collective-permute-start | bytes 393224 | tf_op jit(solution)/shard_map/ppermute | solution.py:95
  250.3 3.1 collective-permute-done.26
  255.4 4.1 %collective-permute-start.25 = (bf16[64,1024]{1,0:T(8,128)(2,1)S(1)}, bf16[64,1024]{1,0:T(8,128)(2,1)S(1)}, u32[]{:S(2)}, u32[]{:S(2)}) collective-permute-start(bf16[64,1024]{1,0:T(8,128)(2,1)S(1)} %get-tuple-element.167), channel_id=1, source_target_pairs={{0,8},{4,12},{8,16},{12,20},{16,24},{20,28},{1,9},{5,13},{9,17},{1... | collective-permute-start | bytes 393224 | tf_op jit(solution)/shard_map/ppermute | solution.py:95
  261.3 4.0 %collective-permute-done.28 = bf16[64,1024]{1,0:T(8,128)(2,1)S(1)} collective-permute-done((bf16[64,1024]{1,0:T(8,128)(2,1)S(1)}, bf16[64,1024]{1,0:T(8,128)(2,1)S(1)}, u32[]{:S(2)}, u32[]{:S(2)}) %collective-permute-start.28) | collective-permute-done | bytes 131104 | tf_op jit(solution)/shard_map/ppermute | solution.py:95
  268.3 3.6 collective-permute-start.31
  278.0 6.6 %collective-permute-done.33 = f32[11080]{0:T(1024)S(1)} collective-permute-done((f32[11080]{0:T(1024)S(1)}, f32[11080]{0:T(1024)S(1)}, u32[]{:S(2)}, u32[]{:S(2)}) %collective-permute-start.33) | collective-permute-done | bytes 44352 | tf_op jit(solution)/shard_map/ppermute | solution.py:43
  298.8 25.5 %collective-permute-done.39 = bf16[128,1024]{1,0:T(8,128)(2,1)} collective-permute-done((bf16[128,1024]{1,0:T(8,128)(2,1)S(1)}, bf16[128,1024]{1,0:T(8,128)(2,1)}, u32[]{:S(2)}, u32[]{:S(2)}) %collective-permute-start.39) | collective-permute-done | bytes 262176 | tf_op jit(solution)/shard_map/ppermute | solution.py:153
  324.4 3.4 collective-permute-start.43
  332.4 3.7 %collective-permute-start.41 = (bf16[2,128,1024]{2,1,0:T(8,128)(2,1)}, bf16[2,128,1024]{2,1,0:T(8,128)(2,1)S(1)}, u32[]{:S(2)}, u32[]{:S(2)}) collective-permute-start(bf16[2,128,1024]{2,1,0:T(8,128)(2,1)} %maximum_select_fusion.18), channel_id=1, source_target_pairs={{0,1},{1,0},{2,3},{3,2},{4,5},{5,4},{6,7},{7,6},{8,9},{9,8},{10,11... | collective-permute-start | bytes 1572872 | tf_op jit(solution)/shard_map/ppermute | solution.py:43
  342.8 8.8 %collective-permute-done.36 = bf16[1,128,1408]{2,1,0:T(8,128)(2,1)S(1)} collective-permute-done((bf16[1,128,1408]{2,1,0:T(8,128)(2,1)}, bf16[1,128,1408]{2,1,0:T(8,128)(2,1)S(1)}, u32[]{:S(2)}, u32[]{:S(2)}) %collective-permute-start.36) | collective-permute-done | bytes 360480 | tf_op jit(solution)/shard_map/ppermute | solution.py:43
  (337 shorter events, 152.2 us)
Async XLA Ops:
  7.2 46.6 %all-gather.7.cloned.1.call-start = ((), (), s32[]{:S(2)}) async-start(), calls=%async_computation.4 | async-start | bytes 1802240 | tf_op jit(solution)/shard_map/all_gather | solution.py:70
  7.3 64.2 %collective-permute-start = (bf16[1,2,64,1024]{3,2,1,0:T(8,128)(2,1)}, bf16[1,2,64,1024]{3,2,1,0:T(8,128)(2,1)S(1)}, u32[]{:S(2)}, u32[]{:S(2)}) collective-permute-start(bf16[1,2,64,1024]{3,2,1,0:T(8,128)(2,1)} %bitcast.337), channel_id=1, source_target_pairs={{0,2},{1,3},{2,0},{3,1},{4,6},{5,7},{6,4},{7,5},{8,10},{9,11},{10,... | collective-permute-start | bytes 786440 | tf_op jit(solution)/shard_map/ppermute | solution.py:43
  11.4 17.1 %collective-permute-start.2 = (bf16[1,1376]{1,0:T(2,128)(2,1)S(1)}, bf16[1,1376]{1,0:T(2,128)(2,1)S(1)}, u32[]{:S(2)}, u32[]{:S(2)}) collective-permute-start(bf16[1,1376]{1,0:T(2,128)(2,1)S(1)} %broadcast_in_dim.20), channel_id=1, source_target_pairs={{0,16},{4,20},{8,24},{12,28},{16,0},{20,4},{24,8},{28,12},{1,17},{... | collective-permute-start | bytes 8264 | tf_op jit(solution)/shard_map/ppermute | solution.py:43
  19.0 76.7 %all-gather.9.cloned.1.call-start = ((), (), s32[]{:S(2)}) async-start(), calls=%async_computation.5 | async-start | bytes 1310720 | tf_op jit(solution)/shard_map/all_gather | solution.py:70
  20.8 27.2 %collective-permute-start.5 = (bf16[128,1024]{1,0:T(8,128)(2,1)S(1)}, bf16[128,1024]{1,0:T(8,128)(2,1)S(1)}, u32[]{:S(2)}, u32[]{:S(2)}) collective-permute-start(bf16[128,1024]{1,0:T(8,128)(2,1)S(1)} %pad_maximum_fusion.1), channel_id=1, source_target_pairs={{0,0},{1,4},{2,8},{3,12},{4,16},{5,20},{6,24},{7,28},{8,1},{9,5},{... | collective-permute-start | bytes 786440 | tf_op jit(solution)/shard_map/ppermute | solution.py:153
  25.1 48.7 %collective-permute-start.7 = (bf16[128,1024]{1,0:T(8,128)(2,1)S(1)}, bf16[128,1024]{1,0:T(8,128)(2,1)}, u32[]{:S(2)}, u32[]{:S(2)}) collective-permute-start(bf16[128,1024]{1,0:T(8,128)(2,1)S(1)} %get-tuple-element.178), channel_id=1, source_target_pairs={{0,4},{4,0},{8,12},{12,8},{16,20},{20,16},{24,28},{28,24},{1,5},{5... | collective-permute-start | bytes 786440 | tf_op jit(solution)/shard_map/ppermute | solution.py:43
  28.5 25.4 %collective-permute-start.3 = (bf16[2,1376]{1,0:T(2,128)(2,1)S(1)}, bf16[2,1376]{1,0:T(2,128)(2,1)S(1)}, u32[]{:S(2)}, u32[]{:S(2)}) collective-permute-start(bf16[2,1376]{1,0:T(2,128)(2,1)S(1)} %broadcast_select_fusion.1), channel_id=1, source_target_pairs={{0,8},{4,12},{8,0},{12,4},{16,24},{20,28},{24,16},{28,20},{1,9},{5... | collective-permute-start | bytes 16520 | tf_op jit(solution)/shard_map/ppermute | solution.py:43
  53.9 107.8 %all-gather.11.cloned.1.call-start = ((), (), s32[]{:S(2)}) async-start(), calls=%async_computation.6 | async-start | bytes 2621440 | tf_op jit(solution)/shard_map/all_gather | solution.py:70
  54.0 16.3 %collective-permute-start.4 = (bf16[4,1376]{1,0:T(4,128)(2,1)S(1)}, bf16[4,1376]{1,0:T(4,128)(2,1)S(1)}, u32[]{:S(2)}, u32[]{:S(2)}) collective-permute-start(bf16[4,1376]{1,0:T(4,128)(2,1)S(1)} %select_n.540), channel_id=1, source_target_pairs={{0,4},{4,0},{8,12},{12,8},{16,20},{20,16},{24,28},{28,24},{1,5},{5... | collective-permute-start | bytes 33032 | tf_op jit(solution)/shard_map/ppermute | solution.py:43
  70.5 32.7 %collective-permute-start.6 = (bf16[4,128,1408]{2,1,0:T(8,128)(2,1)}, bf16[4,128,1408]{2,1,0:T(8,128)(2,1)S(1)}, u32[]{:S(2)}, u32[]{:S(2)}) collective-permute-start(bf16[4,128,1408]{2,1,0:T(8,128)(2,1)} %bitcast.392), channel_id=1, source_target_pairs={{0,4},{4,0},{8,12},{12,8},{16,20},{20,16},{24,28},{28,24},{1,5},{5... | collective-permute-start | bytes 4325384 | tf_op jit(solution)/shard_map/ppermute | solution.py:43
  72.3 25.7 %collective-permute-start.1 = (bf16[2,2,64,1024]{3,2,1,0:T(8,128)(2,1)}, bf16[2,2,64,1024]{3,2,1,0:T(8,128)(2,1)S(1)}, u32[]{:S(2)}, u32[]{:S(2)}) collective-permute-start(bf16[2,2,64,1024]{3,2,1,0:T(8,128)(2,1)} %maximum_select_fusion.11), channel_id=1, source_target_pairs={{0,1},{1,0},{2,3},{3,2},{4,5},{5,4},{6,7},{7,6},{8,9},{9,8},{10,11... | collective-permute-start | bytes 1572872 | tf_op jit(solution)/shard_map/ppermute | solution.py:43
  95.7 29.9 %collective-permute-start.8 = (bf16[4,128,1024]{2,1,0:T(8,128)(2,1)}, bf16[4,128,1024]{2,1,0:T(8,128)(2,1)S(1)}, u32[]{:S(2)}, u32[]{:S(2)}) collective-permute-start(bf16[4,128,1024]{2,1,0:T(8,128)(2,1)} %bitcast.397), channel_id=1, source_target_pairs={{0,4},{4,0},{8,12},{12,8},{16,20},{20,16},{24,28},{28,24},{1,5},{5... | collective-permute-start | bytes 3145736 | tf_op jit(solution)/shard_map/ppermute | solution.py:43
  114.1 154.1 %reduce-scatter.3.cloned.1.call-start = ((), (), s32[]{:S(2)}) async-start(), calls=%async_computation.2 | async-start | bytes 3932160 | tf_op jit(solution)/shard_map/reduce_scatter | solution.py:87
  134.0 13.2 %collective-permute-start.13 = (bf16[1,2,64,1024]{3,2,1,0:T(8,128)(2,1)S(1)}, bf16[1,2,64,1024]{3,2,1,0:T(8,128)(2,1)S(1)}, u32[]{:S(2)}, u32[]{:S(2)}) collective-permute-start(bf16[1,2,64,1024]{3,2,1,0:T(8,128)(2,1)S(1)} %bitcast.373), channel_id=1, source_target_pairs={{0,2},{1,3},{2,0},{3,1},{4,6},{5,7},{6,4},{7,5},{8,10},{9,11},{10,... | collective-permute-start | bytes 786440 | tf_op jit(solution)/shard_map/ppermute | solution.py:43
  177.9 163.5 %reduce-scatter.5.cloned.1.call-start = ((), (), s32[]{:S(2)}) async-start(), calls=%async_computation.3 | async-start | bytes 1802240 | tf_op jit(solution)/shard_map/reduce_scatter | solution.py:87
  204.5 29.6 %collective-permute-start.22 = (bf16[4,64,1024]{2,1,0:T(8,128)(2,1)}, bf16[4,64,1024]{2,1,0:T(8,128)(2,1)}, u32[]{:S(2)}, u32[]{:S(2)}) collective-permute-start(bf16[4,64,1024]{2,1,0:T(8,128)(2,1)} %fusion.20), channel_id=1, source_target_pairs={{0,4},{4,0},{8,12},{12,8},{16,20},{20,16},{24,28},{28,24},{1,5},{5... | collective-permute-start | bytes 1572872 | tf_op jit(solution)/shard_map/ppermute | solution.py:43
  229.3 36.2 %collective-permute-start.21 = (bf16[4,128,1408]{2,1,0:T(8,128)(2,1)}, bf16[4,128,1408]{2,1,0:T(8,128)(2,1)}, u32[]{:S(2)}, u32[]{:S(2)}) collective-permute-start(bf16[4,128,1408]{2,1,0:T(8,128)(2,1)} %dynamic-slice_bitcast_fusion), channel_id=1, source_target_pairs={{0,4},{4,0},{8,12},{12,8},{16,20},{20,16},{24,28},{28,24},{1,5},{5... | collective-permute-start | bytes 4325384 | tf_op jit(solution)/shard_map/ppermute | solution.py:43
  230.4 17.3 %collective-permute-start.29 = (bf16[2,2,64,1024]{3,2,1,0:T(8,128)(2,1)}, bf16[2,2,64,1024]{3,2,1,0:T(8,128)(2,1)}, u32[]{:S(2)}, u32[]{:S(2)}) collective-permute-start(bf16[2,2,64,1024]{3,2,1,0:T(8,128)(2,1)} %fusion.18), channel_id=1, source_target_pairs={{0,1},{1,0},{2,3},{3,2},{4,5},{5,4},{6,7},{7,6},{8,9},{9,8},{10,11... | collective-permute-start | bytes 1572872 | tf_op jit(solution)/shard_map/ppermute | solution.py:43
  249.3 11.9 %collective-permute-start.30 = (bf16[1,2,64,1024]{3,2,1,0:T(8,128)(2,1)S(1)}, bf16[1,2,64,1024]{3,2,1,0:T(8,128)(2,1)S(1)}, u32[]{:S(2)}, u32[]{:S(2)}) collective-permute-start(bf16[1,2,64,1024]{3,2,1,0:T(8,128)(2,1)S(1)} %dynamic-slice_convert_fusion), channel_id=1, source_target_pairs={{0,2},{1,3},{2,0},{3,1},{4,6},{5,7},{6,4},{7,5},{8,10},{9,11},{10,... | collective-permute-start | bytes 786440 | tf_op jit(solution)/shard_map/ppermute | solution.py:43
  272.9 17.8 %collective-permute-start.38 = (bf16[192,1024]{1,0:T(8,128)(2,1)S(1)}, bf16[192,1024]{1,0:T(8,128)(2,1)}, u32[]{:S(2)}, u32[]{:S(2)}) collective-permute-start(bf16[192,1024]{1,0:T(8,128)(2,1)S(1)} %dynamic-slice_bitcast_fusion.1), channel_id=1, source_target_pairs={{0,4},{4,0},{8,12},{12,8},{16,20},{20,16},{24,28},{28,24},{1,5},{5... | collective-permute-start | bytes 1179656 | tf_op jit(solution)/shard_map/ppermute | solution.py:43
  292.0 32.3 %collective-permute-start.39 = (bf16[128,1024]{1,0:T(8,128)(2,1)S(1)}, bf16[128,1024]{1,0:T(8,128)(2,1)}, u32[]{:S(2)}, u32[]{:S(2)}) collective-permute-start(bf16[128,1024]{1,0:T(8,128)(2,1)S(1)} %pad_maximum_fusion.3), channel_id=1, source_target_pairs={{0,0},{4,1},{8,2},{12,3},{16,4},{20,5},{24,6},{28,7},{1,8},{5,9},{... | collective-permute-start | bytes 786440 | tf_op jit(solution)/shard_map/ppermute | solution.py:153
  295.6 28.7 %collective-permute-start.42 = (bf16[1,128,1024]{2,1,0:T(8,128)(2,1)S(1)}, bf16[1,128,1024]{2,1,0:T(8,128)(2,1)S(1)}, u32[]{:S(2)}, u32[]{:S(2)}) collective-permute-start(bf16[1,128,1024]{2,1,0:T(8,128)(2,1)S(1)} %get-tuple-element.176), channel_id=1, source_target_pairs={{0,2},{1,3},{2,0},{3,1},{4,6},{5,7},{6,4},{7,5},{8,10},{9,11},{10,... | collective-permute-start | bytes 786440 | tf_op jit(solution)/shard_map/ppermute | solution.py:43
  324.4 12.8 %collective-permute-start.43 = (bf16[2,128,1024]{2,1,0:T(8,128)(2,1)S(1)}, bf16[2,128,1024]{2,1,0:T(8,128)(2,1)S(1)}, u32[]{:S(2)}, u32[]{:S(2)}) collective-permute-start(bf16[2,128,1024]{2,1,0:T(8,128)(2,1)S(1)} %maximum_select_fusion.20), channel_id=1, source_target_pairs={{0,1},{1,0},{2,3},{3,2},{4,5},{5,4},{6,7},{7,6},{8,9},{9,8},{10,11... | collective-permute-start | bytes 1572872 | tf_op jit(solution)/shard_map/ppermute | solution.py:43
  332.4 22.0 %collective-permute-start.41 = (bf16[2,128,1024]{2,1,0:T(8,128)(2,1)}, bf16[2,128,1024]{2,1,0:T(8,128)(2,1)S(1)}, u32[]{:S(2)}, u32[]{:S(2)}) collective-permute-start(bf16[2,128,1024]{2,1,0:T(8,128)(2,1)} %maximum_select_fusion.18), channel_id=1, source_target_pairs={{0,1},{1,0},{2,3},{3,2},{4,5},{5,4},{6,7},{7,6},{8,9},{9,8},{10,11... | collective-permute-start | bytes 1572872 | tf_op jit(solution)/shard_map/ppermute | solution.py:43
  (62 other events, 568.3 us)
Sparse Core Ops, SparseCore 0:
  19.1 34.6 all-gather.6
  56.0 39.7 all-gather.8
  114.3 47.3 all-gather.10
  178.0 57.6 reduce-scatter.2
  287.2 42.7 reduce-scatter.4

commit v4 on v3

--- a/solution.py
+++ b/solution.py
@@ -756,11 +756,12 @@
     mixed = dot_plain(saved[-1], w_mix)
     middle = hidden_own + scatter_tokens(mixed)
     second_rms = lax.rsqrt(jnp.mean(middle * middle, axis=-1, keepdims=True) + epsilon)
-    second_normed = gather_tokens((middle * second_rms * gain_two).astype(bf16))
+    second_own = (middle * second_rms * gain_two).astype(bf16)
+    second_own, w_gu = bar((second_own, w_gu))
+    second_normed = gather_tokens(second_own)
 
     d_second, ffn_out, g_ffn = ffn_both(second_normed, cot, w_gu, w_down_own, micro, F)
     d_second = scatter_tokens(d_second)
-    block_out = (middle + scatter_tokens(ffn_out)).astype(bf16)
     g_gain_two = jnp.sum(d_second * middle * second_rms, axis=(0, 1))
     scaled_two = d_second * gain_two
     d_middle_own = (
@@ -793,7 +794,10 @@
     heads = lax.dynamic_update_slice(jnp.zeros((3, MH), f32), heads, (0, c * mh))
     total = jnp.concatenate([small.reshape(-1), heads.reshape(-1)])
     mix = line_scatter_hops(mix_half)
-    ffn, first_half, mix, d_normed, total = bar((ffn, first_half, mix, d_normed, total))
+    ffn, first_half, mix, d_normed, total, ffn_out = bar(
+        (ffn, first_half, mix, d_normed, total, ffn_out)
+    )
+    block_out = (middle + scatter_tokens(ffn_out)).astype(bf16)
     first_sum = line_scatter(first_half)
     ffn = pair_sum(ffn, 0)
     total = everywhere_sum(total)

time: 372 us -> 364 us (0.978)
  waiting for transfers between devices: 147 us -> 139 us
  starting transfers between devices: 78.5 us -> 71.3 us
  other arithmetic: 36.1 us -> 41.5 us
    ppermute x36, starting transfers between devices: 58 us -> 50.2 us  [swap(): return lax.ppermute(block, axis, [(i, i ^ bit) for i in devices])]
    ppermute x2, waiting for transfers between devices: 44.9 us -> 39.5 us  [to_owner_columns(): return lax.ppermute(rows, ('fsdp', 'ctx'), route)]
    ppermute x36, waiting for transfers between devices: 60.8 us -> 57.1 us  [swap(): return lax.ppermute(block, axis, [(i, i ^ bit) for i in devices])]
    unnamed x83 -> x85, local copies, waits for them, and re-layouts: 10.2 us -> 10.6 us
  transfers between devices with their start and end apart: 49 -> 49, of which waited for: 23 -> 25; matrix products, arithmetic and copies ran while one was open for 22% -> 23% of each run, Pallas kernels for 7% -> 7%
where the time goes in v4:
time: 364 us; the launch traced here: 363 us
  waiting for transfers between devices  139 us (38%)
  starting transfers between devices  71.3 us (20%)
  local copies, waits for them, and re-layouts  53.7 us (15%)
  other arithmetic  41.5 us (11%)
  Pallas kernels  40.8 us (11%)
  between operations  14.9 us (4%)
    ppermute x36, waiting for transfers between devices, swap(): return lax.ppermute(block, axis, [(i, i ^ bit) for i in devices])  57.1 us
    ppermute x36, starting transfers between devices, swap(): return lax.ppermute(block, axis, [(i, i ^ bit) for i in devices])  50.2 us
    ppermute x2, waiting for transfers between devices, to_owner_columns(): return lax.ppermute(rows, ('fsdp', 'ctx'), route)  39.5 us
    all_gather x3, waiting for transfers between devices, line_gather(): lax.all_gather(shard, 'fsdp', axis=0, tiled=False, axis_index_groups=line...  30.3 us
    pallas_call x1, Pallas kernels, mixer_backward(): pl.pallas_call(backward_body, grid=(micro,), in_specs=[per_pack(length, D...  18.4 us
    ppermute x6, starting transfers between devices, hop(): return lax.ppermute(block, 'fsdp', route)  15 us
    select_n x24, other arithmetic, pair_gather(): out = jnp.where(low, jnp.stack([out, other], 1), jnp.stack([other, out], 1))  12.6 us
    ppermute x6, waiting for transfers between devices, hop(): return lax.ppermute(block, 'fsdp', route)  11.9 us
  transfers between devices with their start and end apart: 49, of which 25 were waited for; matrix products, arithmetic and copies ran while one was open for 23% of the time, Pallas kernels for 7%

profile of v4, /device:TPU:3, one launch (start us, length us, event | category | flops | bytes accessed | tf_op | source)
XLA Modules:
  0.0 362.6 jit_solution(17562090823022493720)
XLA Ops:
  20.8 3.2 collective-permute-start.5
  28.7 19.3 %collective-permute-done.5 = bf16[128,1024]{1,0:T(8,128)(2,1)S(1)} collective-permute-done((bf16[128,1024]{1,0:T(8,128)(2,1)S(1)}, bf16[128,1024]{1,0:T(8,128)(2,1)S(1)}, u32[]{:S(2)}, u32[]{:S(2)}) %collective-permute-start.5) | collective-permute-done | bytes 262176 | tf_op jit(solution)/shard_map/ppermute | solution.py:153
  48.0 5.8 %all-gather.7.cloned.1.call-done = bf16[512,1408]{1,0:T(8,128)(2,1)} async-done(((bf16[128,1408]{1,0:T(8,128)(2,1)}), bf16[512,1408]{1,0:T(8,128)(2,1)}) %all-gather.7.cloned.1.call-update) | async-done | bytes 1441808 | tf_op jit(solution)/shard_map/all_gather | solution.py:70
  54.0 13.4 %collective-permute-start.4 = (bf16[4,1376]{1,0:T(4,128)(2,1)S(1)}, bf16[4,1376]{1,0:T(4,128)(2,1)S(1)}, u32[]{:S(2)}, u32[]{:S(2)}) collective-permute-start(bf16[4,1376]{1,0:T(4,128)(2,1)S(1)} %select_n.540), channel_id=1, source_target_pairs={{0,4},{4,0},{8,12},{12,8},{16,20},{20,16},{24,28},{28,24},{1,5},{5... | collective-permute-start | bytes 33032 | tf_op jit(solution)/shard_map/ppermute | solution.py:43
  74.1 21.7 %all-gather.9.cloned.1.call-done = bf16[512,1024]{1,0:T(8,128)(2,1)} async-done(((bf16[128,1024]{1,0:T(8,128)(2,1)}), bf16[512,1024]{1,0:T(8,128)(2,1)}) %all-gather.9.cloned.1.call-update) | async-done | bytes 1048592 | tf_op jit(solution)/shard_map/all_gather | solution.py:70
  105.0 8.7 %mixer_forward.1 = (bf16[512,1024]{1,0:T(8,128)(2,1)}, bf16[512,256]{1,0:T(8,128)(2,1)}, f32[512,384]{1,0:T(8,128)}, bf16[512,640]{1,0:T(8,128)(2,1)}, f32[512,1...) custom-call(bf16[512,1024]{1,0:T(8,128)(2,1)} %bitcast.321, f32[1,1024]{1,0:T(1,128)} %bitcast.408, ...), custom_call_target="tpu_custom_call" | custom-call | tf_op jit(solution)/shard_map/mixer_forward/pallas_call | solution.py:539
  113.8 11.3 %collective-permute-done.8 = bf16[4,128,1024]{2,1,0:T(8,128)(2,1)S(1)} collective-permute-done((bf16[4,128,1024]{2,1,0:T(8,128)(2,1)}, bf16[4,128,1024]{2,1,0:T(8,128)(2,1)S(1)}, u32[]{:S(2)}, u32[]{:S(2)}) %collective-permute-start.8) | collective-permute-done | bytes 1048608 | tf_op jit(solution)/shard_map/ppermute | solution.py:43
  133.9 6.2 %collective-permute-done.10 = bf16[1,2,64,1024]{3,2,1,0:T(8,128)(2,1)S(1)} collective-permute-done((bf16[1,2,64,1024]{3,2,1,0:T(8,128)(2,1)S(1)}, bf16[1,2,64,1024]{3,2,1,0:T(8,128)(2,1)S(1)}, u32[]{:S(2)}, u32[]{:S(2)}) %collective-permute-start.10) | collective-permute-done | bytes 262176 | tf_op jit(solution)/shard_map/ppermute | solution.py:43
  140.4 2.8 all-gather.11.cloned.1.call-done
  147.3 4.0 %collective-permute-done.11 = bf16[1,2,64,1024]{3,2,1,0:T(8,128)(2,1)S(1)} collective-permute-done((bf16[1,2,64,1024]{3,2,1,0:T(8,128)(2,1)S(1)}, bf16[1,2,64,1024]{3,2,1,0:T(8,128)(2,1)S(1)}, u32[]{:S(2)}, u32[]{:S(2)}) %collective-permute-start.11) | collective-permute-done | bytes 262176 | tf_op jit(solution)/shard_map/ppermute | solution.py:43
  157.4 10.9 %feed_forward.1 = (f32[512,1024]{1,0:T(8,128)}, f32[512,1024]{1,0:T(8,128)}, bf16[8,192,1024]{2,1,0:T(8,128)(2,1)}) custom-call(bf16[512,1024]{1,0:T(8,128)(2,1)} %bitcast.347, bf16[512,1024]{1,0:T(8,128)(2,1)} %bitcast.345, bf16[1024,1024]{1,0:T(8,128)(2,1)} %bitcast.372, bf16[512,1024]{1,0:T(8,128)(2,1)} %bitcast.346), custom_call_target="tpu_custom_call" | custom-call | tf_op jit(solution)/shard_map/feed_forward/pallas_call | solution.py:599
  173.5 6.8 %collective-permute-done.16 = bf16[1,2,64,1024]{3,2,1,0:T(8,128)(2,1)} collective-permute-done((bf16[1,2,64,1024]{3,2,1,0:T(8,128)(2,1)}, bf16[1,2,64,1024]{3,2,1,0:T(8,128)(2,1)}, u32[]{:S(2)}, u32[]{:S(2)}) %collective-permute-start.16) | collective-permute-done | bytes 262176 | tf_op jit(solution)/shard_map/ppermute | solution.py:43
  183.6 6.0 %collective-permute-done.17 = bf16[1,2,64,1024]{3,2,1,0:T(8,128)(2,1)S(1)} collective-permute-done((bf16[1,2,64,1024]{3,2,1,0:T(8,128)(2,1)S(1)}, bf16[1,2,64,1024]{3,2,1,0:T(8,128)(2,1)S(1)}, u32[]{:S(2)}, u32[]{:S(2)}) %collective-permute-start.17) | collective-permute-done | bytes 262176 | tf_op jit(solution)/shard_map/ppermute | solution.py:43
  200.5 18.4 %mixer_backward.1 = (f32[512,1024]{1,0:T(8,128)}, bf16[1024,1408]{1,0:T(8,128)(2,1)}, f32[1,1024]{1,0:T(1,128)}, f32[8,640]{1,0:T(8,128)}, f32[8,128]{1,0:T(8,128)}, /*index=5*/f32[1,384]{1,0:T(1,128)}) custom-call(bf16[512,1024]{1,0:T(8,128)(2,1)} %bitcast.344, bf16[512,1024]{1,0:T(8,128)(2,1)} %bitcast.322, bf16[1024,1408]{1,0:T(8,128)(2,1)} %bitcast.315, ...), custom_call_target="tpu_custom_call" | custom-call | tf_op jit(solution)/shard_map/mixer_backward/pallas_call | solution.py:569
  232.1 3.0 collective-permute-done.21
  235.1 4.2 %collective-permute-start.22 = (bf16[64,1024]{1,0:T(8,128)(2,1)S(1)}, bf16[64,1024]{1,0:T(8,128)(2,1)S(1)}, u32[]{:S(2)}, u32[]{:S(2)}) collective-permute-start(bf16[64,1024]{1,0:T(8,128)(2,1)S(1)} %fusion.28), channel_id=1, source_target_pairs={{0,8},{4,12},{8,16},{12,20},{16,24},{20,28},{1,9},{5,13},{9,17},{1... | collective-permute-start | bytes 393224 | tf_op jit(solution)/shard_map/ppermute | solution.py:95
  245.6 3.8 %collective-permute-done.24 = bf16[64,1024]{1,0:T(8,128)(2,1)S(1)} collective-permute-done((bf16[64,1024]{1,0:T(8,128)(2,1)S(1)}, bf16[64,1024]{1,0:T(8,128)(2,1)S(1)}, u32[]{:S(2)}, u32[]{:S(2)}) %collective-permute-start.24) | collective-permute-done | bytes 131104 | tf_op jit(solution)/shard_map/ppermute | solution.py:95
  250.8 4.0 %collective-permute-start.23 = (bf16[64,1024]{1,0:T(8,128)(2,1)S(1)}, bf16[64,1024]{1,0:T(8,128)(2,1)S(1)}, u32[]{:S(2)}, u32[]{:S(2)}) collective-permute-start(bf16[64,1024]{1,0:T(8,128)(2,1)S(1)} %get-tuple-element.174), channel_id=1, source_target_pairs={{0,8},{4,12},{8,16},{12,20},{16,24},{20,28},{1,9},{5,13},{9,17},{1... | collective-permute-start | bytes 393224 | tf_op jit(solution)/shard_map/ppermute | solution.py:95
  258.1 3.3 collective-permute-done.26
  261.4 2.8 fusion
  266.3 3.8 %collective-permute-start.29 = (bf16[2,2,64,1024]{3,2,1,0:T(8,128)(2,1)}, bf16[2,2,64,1024]{3,2,1,0:T(8,128)(2,1)}, u32[]{:S(2)}, u32[]{:S(2)}) collective-permute-start(bf16[2,2,64,1024]{3,2,1,0:T(8,128)(2,1)} %fusion.18), channel_id=1, source_target_pairs={{0,1},{1,0},{2,3},{3,2},{4,5},{5,4},{6,7},{7,6},{8,9},{9,8},{10,11... | collective-permute-start | bytes 1572872 | tf_op jit(solution)/shard_map/ppermute | solution.py:43
  300.0 20.2 %collective-permute-done.39 = bf16[128,1024]{1,0:T(8,128)(2,1)S(1)} collective-permute-done((bf16[128,1024]{1,0:T(8,128)(2,1)}, bf16[128,1024]{1,0:T(8,128)(2,1)S(1)}, u32[]{:S(2)}, u32[]{:S(2)}) %collective-permute-start.39) | collective-permute-done | bytes 262176 | tf_op jit(solution)/shard_map/ppermute | solution.py:153
  335.4 8.8 %collective-permute-done.36 = bf16[1,128,1408]{2,1,0:T(8,128)(2,1)S(1)} collective-permute-done((bf16[1,128,1408]{2,1,0:T(8,128)(2,1)}, bf16[1,128,1408]{2,1,0:T(8,128)(2,1)S(1)}, u32[]{:S(2)}, u32[]{:S(2)}) %collective-permute-start.36) | collective-permute-done | bytes 360480 | tf_op jit(solution)/shard_map/ppermute | solution.py:43
  351.7 2.9 assemble_first.1
  (338 shorter events, 152.5 us)
Async XLA Ops:
  7.2 46.6 %all-gather.7.cloned.1.call-start = ((), (), s32[]{:S(2)}) async-start(), calls=%async_computation.4 | async-start | bytes 1802240 | tf_op jit(solution)/shard_map/all_gather | solution.py:70
  7.3 63.2 %collective-permute-start = (bf16[1,2,64,1024]{3,2,1,0:T(8,128)(2,1)}, bf16[1,2,64,1024]{3,2,1,0:T(8,128)(2,1)S(1)}, u32[]{:S(2)}, u32[]{:S(2)}) collective-permute-start(bf16[1,2,64,1024]{3,2,1,0:T(8,128)(2,1)} %bitcast.318), channel_id=1, source_target_pairs={{0,2},{1,3},{2,0},{3,1},{4,6},{5,7},{6,4},{7,5},{8,10},{9,11},{10,... | collective-permute-start | bytes 786440 | tf_op jit(solution)/shard_map/ppermute | solution.py:43
  11.4 17.1 %collective-permute-start.2 = (bf16[1,1376]{1,0:T(2,128)(2,1)S(1)}, bf16[1,1376]{1,0:T(2,128)(2,1)S(1)}, u32[]{:S(2)}, u32[]{:S(2)}) collective-permute-start(bf16[1,1376]{1,0:T(2,128)(2,1)S(1)} %broadcast_in_dim.22), channel_id=1, source_target_pairs={{0,16},{4,20},{8,24},{12,28},{16,0},{20,4},{24,8},{28,12},{1,17},{... | collective-permute-start | bytes 8264 | tf_op jit(solution)/shard_map/ppermute | solution.py:43
  19.0 76.7 %all-gather.9.cloned.1.call-start = ((), (), s32[]{:S(2)}) async-start(), calls=%async_computation.5 | async-start | bytes 1310720 | tf_op jit(solution)/shard_map/all_gather | solution.py:70
  20.8 27.2 %collective-permute-start.5 = (bf16[128,1024]{1,0:T(8,128)(2,1)S(1)}, bf16[128,1024]{1,0:T(8,128)(2,1)S(1)}, u32[]{:S(2)}, u32[]{:S(2)}) collective-permute-start(bf16[128,1024]{1,0:T(8,128)(2,1)S(1)} %pad_maximum_fusion.1), channel_id=1, source_target_pairs={{0,0},{1,4},{2,8},{3,12},{4,16},{5,20},{6,24},{7,28},{8,1},{9,5},{... | collective-permute-start | bytes 786440 | tf_op jit(solution)/shard_map/ppermute | solution.py:153
  25.1 48.1 %collective-permute-start.7 = (bf16[128,1024]{1,0:T(8,128)(2,1)S(1)}, bf16[128,1024]{1,0:T(8,128)(2,1)S(1)}, u32[]{:S(2)}, u32[]{:S(2)}) collective-permute-start(bf16[128,1024]{1,0:T(8,128)(2,1)S(1)} %get-tuple-element.185), channel_id=1, source_target_pairs={{0,4},{4,0},{8,12},{12,8},{16,20},{20,16},{24,28},{28,24},{1,5},{5... | collective-permute-start | bytes 786440 | tf_op jit(solution)/shard_map/ppermute | solution.py:43
  28.6 25.4 %collective-permute-start.3 = (bf16[2,1376]{1,0:T(2,128)(2,1)S(1)}, bf16[2,1376]{1,0:T(2,128)(2,1)S(1)}, u32[]{:S(2)}, u32[]{:S(2)}) collective-permute-start(bf16[2,1376]{1,0:T(2,128)(2,1)S(1)} %broadcast_select_fusion.1), channel_id=1, source_target_pairs={{0,8},{4,12},{8,0},{12,4},{16,24},{20,28},{24,16},{28,20},{1,9},{5... | collective-permute-start | bytes 16520 | tf_op jit(solution)/shard_map/ppermute | solution.py:43
  53.9 89.4 %all-gather.11.cloned.1.call-start = ((), (), s32[]{:S(2)}) async-start(), calls=%async_computation.6 | async-start | bytes 2621440 | tf_op jit(solution)/shard_map/all_gather | solution.py:70
  54.0 15.7 %collective-permute-start.4 = (bf16[4,1376]{1,0:T(4,128)(2,1)S(1)}, bf16[4,1376]{1,0:T(4,128)(2,1)S(1)}, u32[]{:S(2)}, u32[]{:S(2)}) collective-permute-start(bf16[4,1376]{1,0:T(4,128)(2,1)S(1)} %select_n.540), channel_id=1, source_target_pairs={{0,4},{4,0},{8,12},{12,8},{16,20},{20,16},{24,28},{28,24},{1,5},{5... | collective-permute-start | bytes 33032 | tf_op jit(solution)/shard_map/ppermute | solution.py:43
  69.8 32.7 %collective-permute-start.6 = (bf16[4,128,1408]{2,1,0:T(8,128)(2,1)}, bf16[4,128,1408]{2,1,0:T(8,128)(2,1)S(1)}, u32[]{:S(2)}, u32[]{:S(2)}) collective-permute-start(bf16[4,128,1408]{2,1,0:T(8,128)(2,1)} %bitcast.373), channel_id=1, source_target_pairs={{0,4},{4,0},{8,12},{12,8},{16,20},{20,16},{24,28},{28,24},{1,5},{5... | collective-permute-start | bytes 4325384 | tf_op jit(solution)/shard_map/ppermute | solution.py:43
  71.3 26.2 %collective-permute-start.1 = (bf16[2,2,64,1024]{3,2,1,0:T(8,128)(2,1)}, bf16[2,2,64,1024]{3,2,1,0:T(8,128)(2,1)}, u32[]{:S(2)}, u32[]{:S(2)}) collective-permute-start(bf16[2,2,64,1024]{3,2,1,0:T(8,128)(2,1)} %maximum_select_fusion.11), channel_id=1, source_target_pairs={{0,1},{1,0},{2,3},{3,2},{4,5},{5,4},{6,7},{7,6},{8,9},{9,8},{10,11... | collective-permute-start | bytes 1572872 | tf_op jit(solution)/shard_map/ppermute | solution.py:43
  95.7 29.4 %collective-permute-start.8 = (bf16[4,128,1024]{2,1,0:T(8,128)(2,1)}, bf16[4,128,1024]{2,1,0:T(8,128)(2,1)S(1)}, u32[]{:S(2)}, u32[]{:S(2)}) collective-permute-start(bf16[4,128,1024]{2,1,0:T(8,128)(2,1)} %bitcast.378), channel_id=1, source_target_pairs={{0,4},{4,0},{8,12},{12,8},{16,20},{20,16},{24,28},{28,24},{1,5},{5... | collective-permute-start | bytes 3145736 | tf_op jit(solution)/shard_map/ppermute | solution.py:43
  97.2 167.0 %reduce-scatter.3.cloned.1.call-start = ((), (), s32[]{:S(2)}) async-start(), calls=%async_computation.2 | async-start | bytes 3932160 | tf_op jit(solution)/shard_map/reduce_scatter | solution.py:87
  132.5 13.1 %collective-permute-start.13 = (bf16[1,2,64,1024]{3,2,1,0:T(8,128)(2,1)S(1)}, bf16[1,2,64,1024]{3,2,1,0:T(8,128)(2,1)S(1)}, u32[]{:S(2)}, u32[]{:S(2)}) collective-permute-start(bf16[1,2,64,1024]{3,2,1,0:T(8,128)(2,1)S(1)} %bitcast.352), channel_id=1, source_target_pairs={{0,2},{1,3},{2,0},{3,1},{4,6},{5,7},{6,4},{7,5},{8,10},{9,11},{10,... | collective-permute-start | bytes 786440 | tf_op jit(solution)/shard_map/ppermute | solution.py:43
  173.3 160.7 %reduce-scatter.5.cloned.1.call-start = ((), (), s32[]{:S(2)}) async-start(), calls=%async_computation.3 | async-start | bytes 1802240 | tf_op jit(solution)/shard_map/reduce_scatter | solution.py:87
  199.2 28.7 %collective-permute-start.20 = (bf16[4,64,1024]{2,1,0:T(8,128)(2,1)}, bf16[4,64,1024]{2,1,0:T(8,128)(2,1)}, u32[]{:S(2)}, u32[]{:S(2)}) collective-permute-start(bf16[4,64,1024]{2,1,0:T(8,128)(2,1)} %fusion.20), channel_id=1, source_target_pairs={{0,4},{4,0},{8,12},{12,8},{16,20},{20,16},{24,28},{28,24},{1,5},{5... | collective-permute-start | bytes 1572872 | tf_op jit(solution)/shard_map/ppermute | solution.py:43
  221.7 39.7 %collective-permute-start.19 = (bf16[4,128,1408]{2,1,0:T(8,128)(2,1)}, bf16[4,128,1408]{2,1,0:T(8,128)(2,1)}, u32[]{:S(2)}, u32[]{:S(2)}) collective-permute-start(bf16[4,128,1408]{2,1,0:T(8,128)(2,1)} %dynamic-slice_bitcast_fusion), channel_id=1, source_target_pairs={{0,4},{4,0},{8,12},{12,8},{16,20},{20,16},{24,28},{28,24},{1,5},{5... | collective-permute-start | bytes 4325384 | tf_op jit(solution)/shard_map/ppermute | solution.py:43
  223.8 20.0 %collective-permute-start.27 = (bf16[2,2,64,1024]{3,2,1,0:T(8,128)(2,1)}, bf16[2,2,64,1024]{3,2,1,0:T(8,128)(2,1)}, u32[]{:S(2)}, u32[]{:S(2)}) collective-permute-start(bf16[2,2,64,1024]{3,2,1,0:T(8,128)(2,1)} %fusion.17), channel_id=1, source_target_pairs={{0,1},{1,0},{2,3},{3,2},{4,5},{5,4},{6,7},{7,6},{8,9},{9,8},{10,11... | collective-permute-start | bytes 1572872 | tf_op jit(solution)/shard_map/ppermute | solution.py:43
  245.4 11.8 %collective-permute-start.28 = (bf16[1,2,64,1024]{3,2,1,0:T(8,128)(2,1)S(1)}, bf16[1,2,64,1024]{3,2,1,0:T(8,128)(2,1)S(1)}, u32[]{:S(2)}, u32[]{:S(2)}) collective-permute-start(bf16[1,2,64,1024]{3,2,1,0:T(8,128)(2,1)S(1)} %dynamic-slice_convert_fusion.1), channel_id=1, source_target_pairs={{0,2},{1,3},{2,0},{3,1},{4,6},{5,7},{6,4},{7,5},{8,10},{9,11},{10,... | collective-permute-start | bytes 786440 | tf_op jit(solution)/shard_map/ppermute | solution.py:43
  266.3 29.7 %collective-permute-start.29 = (bf16[2,2,64,1024]{3,2,1,0:T(8,128)(2,1)}, bf16[2,2,64,1024]{3,2,1,0:T(8,128)(2,1)}, u32[]{:S(2)}, u32[]{:S(2)}) collective-permute-start(bf16[2,2,64,1024]{3,2,1,0:T(8,128)(2,1)} %fusion.18), channel_id=1, source_target_pairs={{0,1},{1,0},{2,3},{3,2},{4,5},{5,4},{6,7},{7,6},{8,9},{9,8},{10,11... | collective-permute-start | bytes 1572872 | tf_op jit(solution)/shard_map/ppermute | solution.py:43
  291.0 29.2 %collective-permute-start.39 = (bf16[128,1024]{1,0:T(8,128)(2,1)}, bf16[128,1024]{1,0:T(8,128)(2,1)S(1)}, u32[]{:S(2)}, u32[]{:S(2)}) collective-permute-start(bf16[128,1024]{1,0:T(8,128)(2,1)} %pad_maximum_fusion.3), channel_id=1, source_target_pairs={{0,0},{4,1},{8,2},{12,3},{16,4},{20,5},{24,6},{28,7},{1,8},{5,9},{... | collective-permute-start | bytes 786440 | tf_op jit(solution)/shard_map/ppermute | solution.py:153
  293.2 27.0 %collective-permute-start.42 = (bf16[1,128,1024]{2,1,0:T(8,128)(2,1)S(1)}, bf16[1,128,1024]{2,1,0:T(8,128)(2,1)}, u32[]{:S(2)}, u32[]{:S(2)}) collective-permute-start(bf16[1,128,1024]{2,1,0:T(8,128)(2,1)S(1)} %get-tuple-element.183), channel_id=1, source_target_pairs={{0,2},{1,3},{2,0},{3,1},{4,6},{5,7},{6,4},{7,5},{8,10},{9,11},{10,... | collective-permute-start | bytes 786440 | tf_op jit(solution)/shard_map/ppermute | solution.py:43
  298.0 26.7 %collective-permute-start.30 = (bf16[1,2,64,1024]{3,2,1,0:T(8,128)(2,1)}, bf16[1,2,64,1024]{3,2,1,0:T(8,128)(2,1)}, u32[]{:S(2)}, u32[]{:S(2)}) collective-permute-start(bf16[1,2,64,1024]{3,2,1,0:T(8,128)(2,1)} %dynamic-slice_convert_fusion), channel_id=1, source_target_pairs={{0,2},{1,3},{2,0},{3,1},{4,6},{5,7},{6,4},{7,5},{8,10},{9,11},{10,... | collective-permute-start | bytes 786440 | tf_op jit(solution)/shard_map/ppermute | solution.py:43
  327.4 19.6 %collective-permute-start.41 = (bf16[2,128,1024]{2,1,0:T(8,128)(2,1)}, bf16[2,128,1024]{2,1,0:T(8,128)(2,1)S(1)}, u32[]{:S(2)}, u32[]{:S(2)}) collective-permute-start(bf16[2,128,1024]{2,1,0:T(8,128)(2,1)} %maximum_select_fusion.18), channel_id=1, source_target_pairs={{0,1},{1,0},{2,3},{3,2},{4,5},{5,4},{6,7},{7,6},{8,9},{9,8},{10,11... | collective-permute-start | bytes 1572872 | tf_op jit(solution)/shard_map/ppermute | solution.py:43
  (62 other events, 528.6 us)
Sparse Core Ops, SparseCore 0:
  19.1 34.6 all-gather.6
  56.0 39.7 all-gather.8
  97.4 45.8 all-gather.10
  173.4 58.2 reduce-scatter.2
  275.0 43.6 reduce-scatter.4
